TPU v7x, 128 devices: a whole 4x4x4 slice. The times are simulated.
128 devices in a mesh: dp: 32 (over z, y, x_hi), mp: 4 (over x_lo, core).
Axes of the slice: x: 4 (x_hi: 2, x_lo: 2; x = x_hi * 2 + x_lo), y: 4, z: 4, core: 2. Of those that a mesh axis runs over, the one named last changes fastest.
Arguments:
- gen_input: bfloat16 [12288, 3072], P(('dp', 'mp')), may hold values from -6 to 6
- noise_score: bfloat16 [12288, 3072], P(('dp', 'mp')), may hold values from -24 to 24
- gen_steps: int32 [12], replicated, may hold values from 0 to 999
- score_steps: int32 [12], replicated, may hold values from 20 to 979
- base_up: bfloat16 [3072, 6144], P('dp', 'mp'), may hold values from -0.109375 to 0.109375
- base_down: bfloat16 [6144, 3072], P('mp', 'dp'), may hold values from -0.078125 to 0.078125
- gen_adapt_in: bfloat16 [3072, 64], replicated, may hold values from -0.109375 to 0.109375
- gen_adapt_out: bfloat16 [64, 6144], P(None, 'mp'), may hold values from -0.75 to 0.75
- fake_adapt_in: bfloat16 [3072, 64], replicated, may hold values from -0.109375 to 0.109375
- fake_adapt_out: bfloat16 [64, 6144], P(None, 'mp'), may hold values from -0.75 to 0.75
- modulation_scale: float32 [3072], replicated, may hold values from -1.8 to 1.8
- modulation_shift: float32 [3072], replicated, may hold values from -1.8 to 1.8
- output_gate: float32 [3072], replicated, may hold values from 0.5 to 1.5
Outputs:
- score_diff: bfloat16 [12288, 3072], P(('dp', 'mp'))
- gen_grad_in: float32 [3072, 64], P(('dp', 'mp'))
- gen_grad_out: float32 [64, 6144], P('dp', 'mp')
- fake_grad_in: float32 [3072, 64], P(('dp', 'mp'))
- fake_grad_out: float32 [64, 6144], P('dp', 'mp')
All inputs are finite; a program needn't handle non-finite values.
Results may differ from a plain program's by a relative error of at most 0.035.
Values may be sent and summed in bfloat16 or wider, within the bound.
No kernel may reach another device: no remote copies, remote signals or barrier semaphores. Data moves between devices by JAX's collectives and lax.ppermute only.
A program may use at most 128 MiB of HBM per device.

v0:
```python
import functools
import math

import jax
import jax.numpy as jnp
from jax import lax
from jax.experimental import pallas as pl
from jax.experimental.pallas import tpu as pltpu
from jax.sharding import Mesh
from jax.sharding import PartitionSpec as P

IMG_TOK = 1024
AXES = ("z", "y", "xh", "xl", "core")
CHIPS = ("z", "y", "xh", "xl")

gelu_coef = 0.044715
root_two_pi = math.sqrt(2.0 / math.pi)


def gelu_value(pre):
    inner_arg = root_two_pi * (pre + gelu_coef * pre * pre * pre)
    return 0.5 * pre * (1.0 + jnp.tanh(inner_arg))


def gelu_slope(pre):
    tanh_val = jnp.tanh(root_two_pi * (pre + gelu_coef * pre * pre * pre))
    return 0.5 * (1.0 + tanh_val) + 0.5 * pre * (1.0 - tanh_val * tanh_val) * root_two_pi * (
        1.0 + 3.0 * gelu_coef * pre * pre
    )


def embedding(steps, feature_count):
    half_width = feature_count // 2
    frequency = jnp.exp(-math.log(10000.0) * jnp.arange(half_width, dtype=jnp.float32) / half_width)
    phase_angle = steps.astype(jnp.float32)[:, None] * frequency[None, :]
    return jnp.concatenate([jnp.sin(phase_angle), jnp.cos(phase_angle)], axis=1)


def modulate(rows, scale_rows, shift_rows):
    widened = rows.astype(jnp.float32)
    normed = widened * lax.rsqrt(jnp.mean(widened * widened, axis=1, keepdims=True) + 1e-06)
    return (normed * scale_rows + shift_rows).astype(jnp.bfloat16)


def matmul(left, right):
    return jnp.dot(left, right, preferred_element_type=jnp.float32)


def contract(left, right, left_dim, right_dim):
    return lax.dot_general(
        left, right, (((left_dim,), (right_dim,)), ((), ())), preferred_element_type=jnp.float32
    )


def swap_cores(value):
    return lax.ppermute(value, "core", [(0, 1), (1, 0)])


RING_AXES = (("y", "z", "x"), ("z", "x", "y"), ("x", "y", "z"))
RING = 4


def chip_ring(axis):
    pairs = []
    for device in range(128):
        place = {"z": device // 32, "y": device // 8 % 4, "x": device // 2 % 4, "core": device % 2}
        step = 1 if place["core"] == 0 else -1
        place[axis] = (place[axis] + step) % RING
        target = place["z"] * 32 + place["y"] * 8 + place["x"] * 2 + place["core"]
        pairs.append((device, target))
    return pairs


def ring(pieces, phase):
    slots = [[piece] for piece in pieces]
    for _ in range(RING - 1):
        for i, held in enumerate(slots):
            held.append(lax.ppermute(held[-1], AXES, chip_ring(RING_AXES[i][phase])))
    return slots


def ring_slots(pieces, early, middle):
    for phase in range(2):
        pieces = [jnp.concatenate(held, axis=0) for held in ring(pieces, phase)]
    pieces, early = lax.optimization_barrier((pieces, early))
    count = pieces[0].shape[0] // 2
    slots = [[[piece[h * count : (h + 1) * count]] for piece in pieces] for h in range(2)]
    for step in range(1, RING):
        if step == RING - 1:
            held = [slots[0][i][-1] for i in range(3)]
            held, middle = lax.optimization_barrier((held, middle))
            for i in range(3):
                slots[0][i][-1] = held[i]
        for h in range(2):
            for i in range(3):
                slots[h][i].append(lax.ppermute(slots[h][i][-1], AXES, chip_ring(RING_AXES[i][2])))
    return slots, early, middle


SHARD = 96
PIECE = 64
REST = SHARD - PIECE
TILE = 512
MIB = 2**20
ANYWHERE = pl.BlockSpec(memory_space=pl.ANY)
IN_VMEM = pl.BlockSpec(memory_space=pltpu.VMEM)
IN_SMEM = pl.BlockSpec(memory_space=pltpu.SMEM)
NT = (((1,), (1,)), ((), ()))
TN = (((0,), (0,)), ((), ()))


def dot(left, right, dims=(((1,), (0,)), ((), ()))):
    return lax.dot_general(left, right, dims, preferred_element_type=jnp.float32)


def gelu_and_slope(pre):
    square = pre * pre
    tanh_val = jnp.tanh(root_two_pi * (pre + gelu_coef * square * pre))
    half = 0.5 * (1.0 + tanh_val)
    slope = half + 0.5 * pre * (1.0 - tanh_val * tanh_val) * root_two_pi * (
        1.0 + 3.0 * gelu_coef * square
    )
    return pre * half, slope


IN_HBM = pl.BlockSpec(memory_space=pltpu.HBM)


def piece_place(place_ref, i, step, k):
    me = {"z": place_ref[0], "y": place_ref[1], "x": place_ref[2]}
    direction = place_ref[3]
    first, second, third = RING_AXES[i]

    def source(axis, distance):
        return lax.rem(me[axis] - distance * direction + RING, RING)

    at = {
        first: source(first, lax.rem(k, RING)),
        second: source(second, lax.div(k, RING)),
        third: source(third, step),
    }
    group = (at["z"] * 4 + at["y"]) * 2 + lax.div(at["x"], 2)
    return lax.rem(at["x"], 2), pl.multiple_of(group * SHARD, 32)


def each(count, one, unroll=4):
    def step(k, carry):
        one(k)
        return carry

    lax.fori_loop(0, count, step, 0, unroll=unroll)


def wait_all(ref, sem):
    pltpu.make_async_copy(ref, ref, sem).wait()


def start_piece(i, source, quarter, row, up, down, sem):
    hidden = source.shape[1]
    cols = pl.ds(pl.multiple_of(quarter * hidden, 128), hidden)
    if i < 2:
        target = (up, down)[i].at[pl.ds(row, PIECE), cols]
        pltpu.make_async_copy(source, target, sem).start()
    else:
        for n, matrix in enumerate((up, down)):
            rows = pl.ds(pl.multiple_of(row + PIECE, 32), REST)
            pltpu.make_async_copy(source.at[pl.ds(n * REST, REST)], matrix.at[rows, cols], sem).start()


def load_body(place_ref, *refs):
    slots, (up_out, down_out, up, down, sems) = refs[:18], refs[18:]
    for n, slot in enumerate(slots):
        step, half, i = n // 6, n // 3 % 2, n % 3

        def one(k, slot=slot, step=step, half=half, i=i, n=n):
            quarter, row = piece_place(place_ref, i, step, 2 * RING * half + k)
            start_piece(i, slot.at[k], quarter, row, up, down, sems.at[n])

        each(2 * RING, one)
    for n, slot in enumerate(slots):
        if n % 3 != 1:
            wait_all(slot, sems.at[n])
    up_copy = pltpu.make_async_copy(up, up_out, sems.at[18])
    up_copy.start()
    for n, slot in enumerate(slots):
        if n % 3 == 1:
            wait_all(slot, sems.at[n])
    down_copy = pltpu.make_async_copy(down, down_out, sems.at[19])
    down_copy.start()
    up_copy.wait()
    down_copy.wait()


def load_weights(coords, slots, width, hidden):
    flat = [
        slots[half][i][step].reshape(2 * RING, PIECE, hidden)
        for step in range(3)
        for half in range(2)
        for i in range(3)
    ]
    shape = jax.ShapeDtypeStruct((width, 2 * hidden), jnp.bfloat16)
    return pl.pallas_call(
        load_body,
        out_shape=(shape, shape),
        in_specs=[IN_SMEM] + [ANYWHERE] * 18,
        out_specs=(IN_HBM, IN_HBM),
        scratch_shapes=[
            pltpu.VMEM(shape.shape, shape.dtype),
            pltpu.VMEM(shape.shape, shape.dtype),
            pltpu.SemaphoreType.DMA((20,)),
        ],
        compiler_params=pltpu.CompilerParams(vmem_limit_bytes=40 * MIB),
        cost_estimate=pl.CostEstimate(
            flops=0, bytes_accessed=8 * width * hidden * 4, transcendentals=0
        ),
        name="load_weights",
    )(coords, *flat)


def column_copy(source, target, sems, n):
    cols = pl.ds(pl.multiple_of(n * TILE, TILE), TILE)
    return pltpu.make_async_copy(source.at[:, cols], target.at[:, cols], sems.at[n])


def row_copy(source, target, sems, n):
    rows = pl.ds(pl.multiple_of(n * TILE, TILE), TILE)
    return pltpu.make_async_copy(source.at[rows], target.at[rows], sems.at[n])


def tile_at(n):
    return pl.ds(pl.multiple_of(n * TILE, TILE), TILE)


def gen_body(place_ref, u, low, adapt, *refs):
    slots, (up_in, down_in, up_out, down_out, slope, mine, other) = refs[:6], refs[6:13]
    up, down, last, act, sems, up_sems, down_sems = refs[13:]
    rows = mine.shape[0]
    tiles = up.shape[1] // TILE
    per_quarter = tiles // 2
    pieces = RING * RING
    fetches = {}
    for i in (0, 2, 1):
        for half in range(2):
            n = 2 * i + half
            target = last.at[i, pl.ds(half * 2 * RING, 2 * RING)]
            fetches[n] = pltpu.make_async_copy(slots[n], target, sems.at[n])
    for n in (0, 1, 4, 5):
        fetches[n].start()
    each(tiles, lambda n: column_copy(up_in, up, up_sems, n).start(), 1)
    for n in (2, 3):
        fetches[n].start()
    whole_down = pltpu.make_async_copy(down_in, down, down_sems.at[0])
    whole_down.start()
    for n in (0, 1, 4, 5):
        fetches[n].wait()

    def hidden_tile(n):
        column_copy(up_in, up, up_sems, n).wait()
        cols = tile_at(n)
        part = pl.ds(pl.multiple_of(lax.rem(n, per_quarter) * TILE, TILE), TILE)

        def place(k):
            for i in (0, 2):
                quarter, row = piece_place(place_ref, i, 3, k)

                @pl.when(quarter == lax.div(n, per_quarter))
                def _(i=i, row=row):
                    if i == 0:
                        up[pl.ds(row, PIECE), cols] = last[0, k, :, part]
                    else:
                        up[pl.ds(pl.multiple_of(row + PIECE, 32), REST), cols] = last[2, k, :REST, part]

        each(pieces, place, 1)
        pre = dot(u[...], up[:, cols]) + dot(low[...], adapt[:, cols])
        value, slope[:, cols] = gelu_and_slope(pre)
        act[:, cols] = value.astype(act.dtype)

    each(tiles, hidden_tile, 1)
    for n in (2, 3):
        fetches[n].wait()
    whole_down.wait()
    hidden = last.shape[3]

    def place_down(k):
        for i in (1, 2):
            quarter, row = piece_place(place_ref, i, 3, k)
            cols = pl.ds(pl.multiple_of(quarter * hidden, 128), hidden)
            if i == 1:
                down[pl.ds(row, PIECE), cols] = last[1, k]
            else:
                down[pl.ds(pl.multiple_of(row + PIECE, 32), REST), cols] = last[2, k, REST:]

    each(pieces, place_down, 1)
    for i in range(3):

        def store(k, i=i):
            quarter, row = piece_place(place_ref, i, 3, k)
            start_piece(i, last.at[i, k], quarter, row, up_out, down_out, sems.at[6 + i])

        each(pieces, store)

    def width_tile(n):
        cols = tile_at(n)
        out = dot(act[...], down[cols, :], NT)
        mine[:, cols] = out[:rows]
        other[:, cols] = out[rows:].astype(other.dtype)

    each(down.shape[0] // TILE, width_tile, 1)
    for i in range(3):
        wait_all(last.at[i], sems.at[6 + i])


def gen_forward(coords, u, low, adapt, slots, up, down):
    group, width = u.shape
    hidden = up.shape[1]
    rows = group // 2
    f32, bf16 = jnp.float32, jnp.bfloat16
    shape = jax.ShapeDtypeStruct((width, hidden), bf16)
    last = [
        slots[half][i][3].reshape(2 * RING, PIECE, hidden // 2) for i in range(3) for half in range(2)
    ]
    return pl.pallas_call(
        gen_body,
        out_shape=(
            shape,
            shape,
            jax.ShapeDtypeStruct((group, hidden), f32),
            jax.ShapeDtypeStruct((rows, width), f32),
            jax.ShapeDtypeStruct((rows, width), bf16),
        ),
        in_specs=[IN_SMEM] + [IN_VMEM] * 3 + [ANYWHERE] * 6 + [IN_HBM] * 2,
        out_specs=(IN_HBM, IN_HBM) + (IN_VMEM,) * 3,
        scratch_shapes=[
            pltpu.VMEM(shape.shape, bf16),
            pltpu.VMEM(shape.shape, bf16),
            pltpu.VMEM((3, RING * RING, PIECE, hidden // 2), bf16),
            pltpu.VMEM((group, hidden), bf16),
            pltpu.SemaphoreType.DMA((9,)),
            pltpu.SemaphoreType.DMA((hidden // TILE,)),
            pltpu.SemaphoreType.DMA((1,)),
        ],
        input_output_aliases={10: 0, 11: 1},
        compiler_params=pltpu.CompilerParams(vmem_limit_bytes=56 * MIB),
        cost_estimate=pl.CostEstimate(
            flops=4 * group * width * hidden,
            bytes_accessed=50 * MIB,
            transcendentals=group * hidden,
        ),
        name="gen_forward",
    )(coords, u, low, adapt, *last, up, down)


def score_body(
    u_mine, u_other, adapt_in, adapt_out, up_in, down_in, slope, low, real, fake, others, *scratch
):
    u, act, up, down, up_sems, down_sems = scratch
    hidden_tiles, width_tiles = up.shape[1] // TILE, down.shape[0] // TILE
    each(hidden_tiles, lambda n: column_copy(up_in, up, up_sems, n).start(), 1)
    each(width_tiles, lambda n: row_copy(down_in, down, down_sems, n).start(), 1)
    rows = u_mine.shape[0]
    group = 2 * rows
    u[:rows] = u_mine[...]
    u[rows:] = u_other[...]
    low[...] = dot(u[...], adapt_in[...], NT).astype(low.dtype)

    def hidden_tile(n):
        column_copy(up_in, up, up_sems, n).wait()
        cols = tile_at(n)
        pre_real = dot(u[...], up[:, cols])
        pre_fake = pre_real + dot(low[...], adapt_out[:, cols])
        act[:group, cols] = gelu_value(pre_real).astype(act.dtype)
        value, slope[:, cols] = gelu_and_slope(pre_fake)
        act[group:, cols] = value.astype(act.dtype)

    each(hidden_tiles, hidden_tile, 1)

    def width_tile(n):
        row_copy(down_in, down, down_sems, n).wait()
        cols = tile_at(n)
        out = dot(act[...], down[cols, :], NT)
        real[:, cols] = out[:rows]
        others[:rows, cols] = out[rows:group].astype(others.dtype)
        fake[:, cols] = out[group : group + rows]
        others[rows:, cols] = out[group + rows :].astype(others.dtype)

    each(width_tiles, width_tile, 1)


def score_forward(u_mine, u_other, adapt_in, adapt_out, up, down):
    rows, width = u_mine.shape
    hidden = up.shape[1]
    group = 2 * rows
    f32, bf16 = jnp.float32, jnp.bfloat16
    return pl.pallas_call(
        score_body,
        out_shape=(
            jax.ShapeDtypeStruct((group, hidden), f32),
            jax.ShapeDtypeStruct((group, adapt_in.shape[0]), bf16),
            jax.ShapeDtypeStruct((rows, width), f32),
            jax.ShapeDtypeStruct((rows, width), f32),
            jax.ShapeDtypeStruct((group, width), bf16),
        ),
        in_specs=[IN_VMEM] * 4 + [IN_HBM] * 2,
        out_specs=(IN_VMEM,) * 5,
        scratch_shapes=[
            pltpu.VMEM((group, width), bf16),
            pltpu.VMEM((2 * group, hidden), bf16),
            pltpu.VMEM(up.shape, bf16),
            pltpu.VMEM(down.shape, bf16),
            pltpu.SemaphoreType.DMA((hidden // TILE,)),
            pltpu.SemaphoreType.DMA((width // TILE,)),
        ],
        compiler_params=pltpu.CompilerParams(vmem_limit_bytes=56 * MIB),
        cost_estimate=pl.CostEstimate(
            flops=6 * group * width * hidden,
            bytes_accessed=50 * MIB,
            transcendentals=2 * group * hidden,
        ),
        name="score_forward",
    )(u_mine, u_other, adapt_in, adapt_out, up, down)


def back_body(
    cots_mine, cots_other, slope_gen, slope_fake, low_gen, low_fake, gen_out, fake_out, down_in, grads, mix, *scratch
):
    cots, down, sems = scratch
    tiles = down.shape[1] // TILE
    each(tiles, lambda n: column_copy(down_in, down, sems, n).start(), 1)
    group = cots_mine.shape[0]
    rows = group // 2
    for i in range(2):
        cots[i * group : i * group + rows] = cots_mine[i * rows : (i + 1) * rows]
        cots[i * group + rows : (i + 1) * group] = cots_other[i * rows : (i + 1) * rows]
    mix[...] = jnp.zeros_like(mix)

    def hidden_tile(n):
        column_copy(down_in, down, sems, n).wait()
        cols = tile_at(n)
        raw = dot(cots[...], down[:, cols])
        back_gen = (raw[:group] * slope_gen[:, cols]).astype(jnp.bfloat16)
        back_fake = (raw[group:] * slope_fake[:, cols]).astype(jnp.bfloat16)
        grads[0, :, cols] = dot(low_gen[...], back_gen, TN).astype(grads.dtype)
        grads[1, :, cols] = dot(low_fake[...], back_fake, TN).astype(grads.dtype)
        mix[0] += dot(back_gen, gen_out[:, cols], NT)
        mix[1] += dot(back_fake, fake_out[:, cols], NT)

    each(tiles, hidden_tile, 1)


def backward(cots_mine, cots_other, slope_gen, slope_fake, low_gen, low_fake, gen_out, fake_out, down):
    group, width = cots_mine.shape
    hidden = down.shape[1]
    rank = low_gen.shape[1]
    f32, bf16 = jnp.float32, jnp.bfloat16
    return pl.pallas_call(
        back_body,
        out_shape=(
            jax.ShapeDtypeStruct((2, rank, hidden), bf16),
            jax.ShapeDtypeStruct((2, group, rank), f32),
        ),
        in_specs=[IN_VMEM] * 8 + [IN_HBM],
        out_specs=(IN_VMEM,) * 2,
        scratch_shapes=[
            pltpu.VMEM((2 * group, width), bf16),
            pltpu.VMEM(down.shape, bf16),
            pltpu.SemaphoreType.DMA((hidden // TILE,)),
        ],
        compiler_params=pltpu.CompilerParams(vmem_limit_bytes=40 * MIB),
        cost_estimate=pl.CostEstimate(
            flops=4 * group * width * hidden, bytes_accessed=30 * MIB, transcendentals=0
        ),
        name="backward",
    )(cots_mine, cots_other, slope_gen, slope_fake, low_gen, low_fake, gen_out, fake_out, down)


STRIP = 16


def noise_body(ends, blends, given, noise, mine, other, mods, gate, latents_ref, noised_ref, u_ref):
    f32 = jnp.float32

    def strip(n, carry):
        rows = pl.ds(pl.multiple_of(n * STRIP, STRIP), STRIP)
        in_last = n * STRIP + lax.broadcasted_iota(jnp.int32, (STRIP, 1), 0) >= ends[0]
        out = mine[rows] + other[rows].astype(f32)
        latents = (given[rows].astype(f32) + gate[...] * out).astype(latents_ref.dtype)
        latents_ref[rows] = latents
        blend = jnp.where(in_last, blends[1], blends[0])
        noised = (
            (1.0 - blend) * latents.astype(f32) + blend * noise[rows].astype(f32)
        ).astype(noised_ref.dtype)
        noised_ref[rows] = noised
        scale = jnp.where(in_last, mods[1:2], mods[0:1])
        shift = jnp.where(in_last, mods[3:4], mods[2:3])
        u_ref[rows] = modulate(noised, scale, shift)
        return carry

    lax.fori_loop(0, given.shape[0] // STRIP, strip, 0)


def add_noise(ends, blends, given, noise, mine, other, mods, gate):
    shape = jax.ShapeDtypeStruct(given.shape, given.dtype)
    return pl.pallas_call(
        noise_body,
        out_shape=(shape,) * 3,
        in_specs=[IN_SMEM] * 2 + [IN_VMEM] * 6,
        out_specs=(IN_VMEM,) * 3,
        compiler_params=pltpu.CompilerParams(vmem_limit_bytes=10 * MIB),
        cost_estimate=pl.CostEstimate(flops=0, bytes_accessed=6 * MIB, transcendentals=0),
        name="add_noise",
    )(ends, blends, given, noise, mine, other, mods, gate)


def cotangent_body(scale, real, fake, others, gate_ref, noise, latents, noised, diff_ref, cots):
    f32 = jnp.float32
    count = real.shape[0]

    def strip(n, carry):
        start = pl.multiple_of(n * STRIP, STRIP)
        rows, second = pl.ds(start, STRIP), pl.ds(count + start, STRIP)
        gate = gate_ref[...]
        out_real = real[rows] + others[rows].astype(f32)
        out_fake = fake[rows] + others[second].astype(f32)
        diff = (gate * (out_fake - out_real)).astype(diff_ref.dtype)
        diff_ref[rows] = diff
        cots[rows] = (gate * diff.astype(f32) * scale).astype(cots.dtype)
        target = noise[rows].astype(f32) - latents[rows].astype(f32)
        cots[second] = (
            gate * (noised[rows].astype(f32) + gate * out_fake - target) * scale
        ).astype(cots.dtype)
        return carry

    lax.fori_loop(0, count // STRIP, strip, 0)


def cotangents(scale, real, fake, others, gate, noise, latents, noised):
    rows, width = real.shape
    return pl.pallas_call(
        functools.partial(cotangent_body, scale),
        out_shape=(
            jax.ShapeDtypeStruct((rows, width), noise.dtype),
            jax.ShapeDtypeStruct((2 * rows, width), noise.dtype),
        ),
        in_specs=[IN_VMEM] * 7,
        out_specs=(IN_VMEM,) * 2,
        compiler_params=pltpu.CompilerParams(vmem_limit_bytes=12 * MIB),
        cost_estimate=pl.CostEstimate(flops=0, bytes_accessed=8 * MIB, transcendentals=0),
        name="cotangents",
    )(real, fake, others, gate, noise, latents, noised)


def three_terms(value):
    high = lax.reduce_precision(value, 8, 7)
    rest = value - high
    middle = lax.reduce_precision(rest, 8, 7)
    low = rest - middle
    return jnp.concatenate([high, middle, low], axis=1).astype(jnp.bfloat16)


def local(
    gen_input,
    noise_score,
    gen_steps,
    score_steps,
    base_up,
    base_down,
    gen_adapt_in,
    gen_adapt_out,
    fake_adapt_in,
    fake_adapt_out,
    modulation_scale,
    modulation_shift,
    output_gate,
):
    bf16, f32 = jnp.bfloat16, jnp.float32
    shard_rows, width = gen_input.shape
    hidden = base_up.shape[1]
    rank = gen_adapt_in.shape[1]
    image_count = gen_steps.shape[0]
    loss_scale = 1.0 / math.sqrt(image_count * IMG_TOK)
    core = lax.axis_index("core")
    xl = lax.axis_index("xl")
    first_row = lax.axis_index(AXES) * shard_rows
    first_image = first_row // IMG_TOK
    last_image = (first_row + shard_rows - 1) // IMG_TOK
    row_ids = first_row + jnp.arange(shard_rows, dtype=jnp.int32)
    in_last = (row_ids >= last_image * IMG_TOK)[:, None]

    def two_steps(steps):
        return jnp.stack([steps[first_image], steps[last_image]])

    def modulation(steps):
        embed = embedding(two_steps(steps), width)
        return 1.0 + modulation_scale[None, :] * embed, modulation_shift[None, :] * embed

    def both_rows(mine):
        return jnp.concatenate([mine, swap_cores(mine)], axis=0)

    coords = jnp.stack(
        [
            lax.axis_index("z"),
            lax.axis_index("y"),
            lax.axis_index("xh") * 2 + xl,
            1 - 2 * core,
        ]
    ).astype(jnp.int32)
    down_rows = base_down.T

    def both_quarters(mine):
        theirs = lax.ppermute(mine, "xl", [(0, 1), (1, 0)])
        quarters = [jnp.where(xl == 0, mine, theirs), jnp.where(xl == 0, theirs, mine)]
        return jnp.concatenate(quarters, axis=1)

    adapt_out = both_quarters(jnp.concatenate([gen_adapt_out, fake_adapt_out], axis=0))
    gen_scale, gen_shift = modulation(gen_steps)
    u_mine = modulate(
        gen_input,
        jnp.where(in_last, gen_scale[1:], gen_scale[:1]),
        jnp.where(in_last, gen_shift[1:], gen_shift[:1]),
    )
    u_gen = both_rows(u_mine)
    low_gen = matmul(u_gen, gen_adapt_in).astype(bf16)
    mods = jnp.concatenate(modulation(score_steps), axis=0)
    blends = (two_steps(score_steps).astype(f32) + 0.5) / 1000.0
    ends = (last_image * IMG_TOK - first_row).astype(jnp.int32).reshape(1)
    slots, adapt_out, prepared = ring_slots(
        [
            base_up[:PIECE],
            down_rows[:PIECE],
            jnp.concatenate([base_up[PIECE:], down_rows[PIECE:]], axis=0),
        ],
        adapt_out,
        (u_gen, low_gen, mods, blends, ends, coords),
    )
    u_gen, low_gen, mods, blends, ends, coords = prepared
    gen_out, fake_out = adapt_out[:rank], adapt_out[rank:]
    up_part, down_part = load_weights(coords, slots, width, hidden)

    up_all, down_all, slope_gen, out_mine, out_other = gen_forward(
        coords, u_gen, low_gen, gen_out, slots, up_part, down_part
    )
    gate = output_gate.reshape(1, width)
    latents, noised, u_score = add_noise(
        ends, blends, gen_input, noise_score, out_mine, swap_cores(out_other), mods, gate
    )
    u_score_other = swap_cores(u_score)
    slope_fake, low_fake, out_real, out_fake, outs_other = score_forward(
        u_score, u_score_other, fake_adapt_in.T, fake_out, up_all, down_all
    )
    score_diff, cots = cotangents(
        loss_scale, out_real, out_fake, swap_cores(outs_other), gate, noise_score, latents, noised
    )
    out_grads, mix = backward(
        cots, swap_cores(cots), slope_gen, slope_fake, low_gen, low_fake, gen_out, fake_out, down_all
    )
    mix = jnp.concatenate([mix[0], mix[1]], axis=1)
    mix_other = swap_cores(mix)
    mix = mix + jnp.concatenate([mix_other[shard_rows:], mix_other[:shard_rows]], axis=0)

    def in_grad(u, mix_part):
        product = contract(u, three_terms(mix_part), 0, 0)
        total = product[:, :rank] + product[:, rank : 2 * rank] + product[:, 2 * rank :]
        chips = total.reshape(-1, 2, width // 128, rank)
        return jnp.where(core == 0, chips[:, 0], chips[:, 1])

    u_score_group = jnp.concatenate([u_score, u_score_other], axis=0)
    in_grads = jnp.concatenate(
        [in_grad(u_gen, mix[:, :rank]), in_grad(u_score_group, mix[:, rank:])], axis=2
    )
    chips, in_rows = in_grads.shape[0], in_grads.shape[1]
    groups = chips // 2
    out_grads = out_grads.reshape(2, groups, rank // groups, 2, hidden).transpose(1, 3, 0, 2, 4)
    out_rows = 2 * (rank // groups) * hidden // 128
    packed = jnp.concatenate(
        [in_grads.astype(bf16), out_grads.reshape(chips, out_rows, 128)], axis=1
    )
    received = lax.all_to_all(packed, CHIPS, 0, 0, tiled=True)
    summed = jnp.sum(received.astype(f32), axis=0)
    gen_grad_in, fake_grad_in = summed[:in_rows, :rank], summed[:in_rows, rank:]
    grads_out = summed[in_rows:].reshape(2, rank // groups, hidden)
    return (score_diff, gen_grad_in, grads_out[0], fake_grad_in, grads_out[1])


def solution(mesh):
    fine = Mesh(mesh.devices.reshape(4, 4, 2, 2, 2), AXES)
    dp, mp = ("z", "y", "xh"), ("xl", "core")
    return jax.shard_map(
        local,
        mesh=fine,
        in_specs=(
            P(AXES, None),
            P(AXES, None),
            P(),
            P(),
            P(dp, mp),
            P(mp, dp),
            P(),
            P(None, mp),
            P(),
            P(None, mp),
            P(),
            P(),
            P(),
        ),
        out_specs=(
            P(AXES, None),
            P(AXES, None),
            P(dp, mp),
            P(AXES, None),
            P(dp, mp),
        ),
        check_vma=False,
    )
```

profile of v0, /device:TPU:0, one launch (start us, length us, event | category | flops | bytes accessed | tf_op | source)
XLA Modules:
  0.0 323.5 jit_solution(1998149945478391591)
XLA Ops:
  0.7 1.0 constant_dynamic-update-slice_fusion.28
  2.7 1.7 collective-permute-start.18
  4.3 1.6 fusion.31
  6.0 1.9 collective-permute-start.6
  7.9 1.6 fusion.32
  9.5 1.6 collective-permute-start
  11.1 1.6 constant_dynamic-update-slice_fusion.18
  12.7 1.6 constant_dynamic-update-slice_fusion.17
  15.5 1.4 add_multiply_fusion
  16.9 1.4 add_convert_fusion
  20.8 2.0 collective-permute-start.7
  22.8 1.6 collective-permute-start.1
  25.1 2.2 collective-permute-start.13
  28.7 1.6 collective-permute-start.8
  30.3 1.3 collective-permute-start.2
  35.7 1.3 collective-permute-start.9
  37.3 1.0 collective-permute-start.3
  39.5 1.3 collective-permute-start.15
  40.8 1.0 pad_maximum_fusion.4
  41.8 7.1 %collective-permute-done.9 = bf16[256,1536]{1,0:T(8,128)(2,1)S(1)} collective-permute-done((bf16[256,1536]{1,0:T(8,128)(2,1)S(1)}, bf16[256,1536]{1,0:T(8,128)(2,1)S(1)}, u32[]{:S(2)}, u32[]{:S(2)}) %collective-permute-start.9) | collective-permute-done | bytes 786464 | tf_op jit(solution)/shard_map/ppermute | solution.py:78
  49.0 1.6 collective-permute-done.3
  50.6 2.2 collective-permute-done.15
  52.9 9.2 %collective-permute-done.10 = bf16[256,1536]{1,0:T(8,128)(2,1)S(1)} collective-permute-done((bf16[256,1536]{1,0:T(8,128)(2,1)S(1)}, bf16[256,1536]{1,0:T(8,128)(2,1)S(1)}, u32[]{:S(2)}, u32[]{:S(2)}) %collective-permute-start.10) | collective-permute-done | bytes 786464 | tf_op jit(solution)/shard_map/ppermute | solution.py:78
  62.1 1.0 constant_dynamic-update-slice_fusion.21
  64.3 1.7 collective-permute-done.16
  67.0 8.4 %collective-permute-done.11 = bf16[256,1536]{1,0:T(8,128)(2,1)S(1)} collective-permute-done((bf16[256,1536]{1,0:T(8,128)(2,1)S(1)}, bf16[256,1536]{1,0:T(8,128)(2,1)S(1)}, u32[]{:S(2)}, u32[]{:S(2)}) %collective-permute-start.11) | collective-permute-done | bytes 786464 | tf_op jit(solution)/shard_map/ppermute | solution.py:78
  75.4 1.6 collective-permute-done.5
  77.0 2.1 collective-permute-done.17
  80.3 1.7 collective-permute-start.27
  84.0 2.5 fusion.27
  86.7 1.2 copy-done.8
  87.9 14.1 %collective-permute-done.27 = bf16[512,1536]{1,0:T(8,128)(2,1)S(1)} collective-permute-done((bf16[512,1536]{1,0:T(8,128)(2,1)S(1)}, bf16[512,1536]{1,0:T(8,128)(2,1)S(1)}, u32[]{:S(2)}, u32[]{:S(2)}) %collective-permute-start.27) | collective-permute-done | bytes 1572896 | tf_op jit(solution)/shard_map/ppermute | solution.py:96
  102.0 1.6 collective-permute-start.35
  103.6 1.2 copy-done.6
  104.8 14.1 %collective-permute-done.19 = bf16[512,1536]{1,0:T(8,128)(2,1)S(1)} collective-permute-done((bf16[512,1536]{1,0:T(8,128)(2,1)S(1)}, bf16[512,1536]{1,0:T(8,128)(2,1)S(1)}, u32[]{:S(2)}, u32[]{:S(2)}) %collective-permute-start.19) | collective-permute-done | bytes 1572896 | tf_op jit(solution)/shard_map/ppermute | solution.py:96
  120.1 1.2 copy-done.18
  121.9 3.3 %collective-permute-done.35 = bf16[512,1536]{1,0:T(8,128)(2,1)} collective-permute-done((bf16[512,1536]{1,0:T(8,128)(2,1)S(1)}, bf16[512,1536]{1,0:T(8,128)(2,1)}, u32[]{:S(2)}, u32[]{:S(2)}) %collective-permute-start.35) | collective-permute-done | bytes 1572896 | tf_op jit(solution)/shard_map/ppermute | solution.py:96
  125.7 14.9 %collective-permute-done.28 = bf16[512,1536]{1,0:T(8,128)(2,1)} collective-permute-done((bf16[512,1536]{1,0:T(8,128)(2,1)S(1)}, bf16[512,1536]{1,0:T(8,128)(2,1)}, u32[]{:S(2)}, u32[]{:S(2)}) %collective-permute-start.28) | collective-permute-done | bytes 1572896 | tf_op jit(solution)/shard_map/ppermute | solution.py:96
  140.6 1.6 collective-permute-start.36
  142.2 15.1 %collective-permute-done.20 = bf16[512,1536]{1,0:T(8,128)(2,1)S(1)} collective-permute-done((bf16[512,1536]{1,0:T(8,128)(2,1)S(1)}, bf16[512,1536]{1,0:T(8,128)(2,1)S(1)}, u32[]{:S(2)}, u32[]{:S(2)}) %collective-permute-start.20) | collective-permute-done | bytes 1572896 | tf_op jit(solution)/shard_map/ppermute | solution.py:96
  157.3 1.2 copy-done.35
  159.4 2.5 convolution_convert_fusion.low.low_gen
  161.9 2.5 pad_maximum_fusion.u
  164.9 1.4 collective-permute-start.37
  166.2 14.2 %collective-permute-done.29 = bf16[512,1536]{1,0:T(8,128)(2,1)} collective-permute-done((bf16[512,1536]{1,0:T(8,128)(2,1)}, bf16[512,1536]{1,0:T(8,128)(2,1)}, u32[]{:S(2)}, u32[]{:S(2)}) %collective-permute-start.29) | collective-permute-done | bytes 1572896 | tf_op jit(solution)/shard_map/ppermute | solution.py:96
  180.4 1.6 collective-permute-start.34
  182.1 2.0 fusion.30
  184.1 1.4 copy-done.19
  185.5 22.3 %load_weights.1 = (bf16[3072,3072]{1,0:T(8,128)(2,1)}, bf16[3072,3072]{1,0:T(8,128)(2,1)}) custom-call(s32[4]{0:T(128)S(1)} %pad_add_fusion.place_ref, bf16[8,64,1536]{2,1,0:T(8,128)(2,1)S(1)} %bitcast.52, bf16[8,64,1536]{2,1,0:T(8,128)(2,1)S(1)} %bitcast.54, bf16[8,64,1536]{2,1,0:T(8,128)(2,1)S(1)} %bitcast.56, bf16[8,64,1536]{2,1,0:T(8,128)(2,1)S(1)} %bitcast.51, ...), custom_call_target="tpu_custom_call" | custom-call | bytes 150994944 | tf_op jit(solution)/shard_map/load_weights/pallas_call | solution.py:202
  208.0 1.1 copy-done.38
  211.0 26.9 %gen_forward.1 = (bf16[3072,3072]{1,0:T(8,128)(2,1)}, bf16[3072,3072]{1,0:T(8,128)(2,1)}, f32[192,3072]{1,0:T(8,128)}, f32[96,3072]{1,0:T(8,128)}, bf16[96,3072]{1,0:T(8,128)(2,1)}) custom-call(s32[4]{0:T(128)} %copy-done.28, bf16[192,3072]{1,0:T(8,128)(2,1)} %pad_maximum_fusion.u, ...), custom_call_target="tpu_custom_call", output_to_operand_aliasing={{0}: (10, {}), {1}: (11, {})} | custom-call | flops 7247757312 | bytes 52428800 | tf_op jit(solution)/shard_map/gen_forward/pallas_call | solution.py:322
  237.9 2.2 collective-permute-done.38.other
  240.2 1.3 copy-done.20
  241.4 1.9 add_noise.1
  243.8 1.9 collective-permute-done.39.u_other
  246.4 20.6 %score_forward.1 = (f32[192,3072]{1,0:T(8,128)}, bf16[192,64]{1,0:T(8,128)(2,1)}, f32[96,3072]{1,0:T(8,128)}, f32[96,3072]{1,0:T(8,128)}, bf16[192,3072]{1,0:T(8,128)(2,1)}) custom-call(bf16[96,3072]{1,0:T(8,128)(2,1)} %copy-done.23, bf16[96,3072]{1,0:T(8,128)(2,1)} %copy-done.41, bf16[64,3072]{1,0:T(8,128)(2,1)} %bitcast.76, ...), custom_call_target="tpu_custom_call" | custom-call | flops 10871635968 | bytes 52428800 | tf_op jit(solution)/shard_map/score_forward/pallas_call | solution.py:394
  267.3 2.9 collective-permute-done.40.others
  270.2 1.3 copy-done.21
  271.5 1.3 copy-done.22
  272.8 1.7 cotangents.1
  274.6 2.7 collective-permute-done.41.cots_other
  277.3 12.0 %backward.1 = (bf16[2,64,3072]{2,1,0:T(8,128)(2,1)S(1)}, f32[2,192,64]{2,1,0:T(8,128)S(1)}) custom-call(bf16[192,3072]{1,0:T(8,128)(2,1)S(1)} %get-tuple-element.63.cots_mine, bf16[192,3072]{1,0:T(8,128)(2,1)S(1)} %collective-permute-done.41.cots_other, f32[192,3072]{1,0:T(8,128)S(1)} %copy-done.14, f32[192,3072]{1,0:T(8,128)S(1)} %copy-done.15, ...), custom_call_target="tpu_custom_call" | custom-call | flops 7247757312 | bytes 31457280 | tf_op jit(solution)/shard_map/backward/pallas_call | solution.py:455
  290.8 1.4 reshape.190
  296.4 25.0 %all_to_all.5 = bf16[64,72,128]{2,1,0:T(8,128)(2,1)S(1)} all-to-all(bf16[64,72,128]{2,1,0:T(8,128)(2,1)S(1)} %pad_maximum_fusion.1), channel_id=1, replica_groups=mesh['z'=4,'y'=4,'xh'=2,'xl'=2,'core'=2] {'z','y','xh','xl'}, dimensions={0} | all-to-all | bytes 2359296 | tf_op jit(solution)/shard_map/all_to_all | solution.py:677
  (204 shorter events, 33.3 us)
Async XLA Ops:
  0.6 158.7 %copy-start = (bf16[3072,64]{0,1:T(8,128)(2,1)S(1)}, bf16[3072,64]{0,1:T(8,128)(2,1)}, u32[]{:S(2)}) copy-start(bf16[3072,64]{0,1:T(8,128)(2,1)} %param.19) | copy-start | bytes 1179652
  0.7 14.2 %copy-start.50 = (s32[12]{0:T(128)S(1)}, s32[12]{0:T(128)}, u32[]{:S(2)}) copy-start(s32[12]{0:T(128)} %param.16) | copy-start | bytes 148
  0.7 14.2 %copy-start.51 = (s32[12]{0:T(128)S(1)}, s32[12]{0:T(128)}, u32[]{:S(2)}) copy-start(s32[12]{0:T(128)} %param.15) | copy-start | bytes 148
  0.7 18.0 %copy-start.49 = (f32[3072]{0:T(1024)S(1)}, f32[3072]{0:T(1024)}, u32[]{:S(2)}) copy-start(f32[3072]{0:T(1024)} %param.24) | copy-start | bytes 36868
  0.7 18.0 %copy-start.48 = (f32[3072]{0:T(1024)S(1)}, f32[3072]{0:T(1024)}, u32[]{:S(2)}) copy-start(f32[3072]{0:T(1024)} %param.23) | copy-start | bytes 36868
  0.7 19.9 %copy-start.10 = (bf16[96,3072]{1,0:T(8,128)(2,1)S(1)}, bf16[96,3072]{1,0:T(8,128)(2,1)}, u32[]{:S(2)}) copy-start(bf16[96,3072]{1,0:T(8,128)(2,1)} %given.1) | copy-start | bytes 1769476
  2.7 30.9 %collective-permute-start.18 = (bf16[128,1536]{1,0:T(8,128)(2,1)S(1)}, bf16[128,1536]{1,0:T(8,128)(2,1)S(1)}, u32[]{:S(2)}, u32[]{:S(2)}) collective-permute-start(bf16[128,1536]{1,0:T(8,128)(2,1)S(1)} %constant_dynamic-update-slice_fusion.27), channel_id=1, source_target_pairs={{0,2},{2,0},{1,3},{3,1},{4,6},{6,4},{5,7},{7,5},{8,10},{10,8},{9,1... | collective-permute-start | bytes 1179656 | tf_op jit(solution)/shard_map/ppermute | solution.py:610
  6.0 14.9 %collective-permute-start.6 = (bf16[64,1536]{1,0:T(8,128)(2,1)S(1)}, bf16[64,1536]{1,0:T(8,128)(2,1)S(1)}, u32[]{:S(2)}, u32[]{:S(2)}) collective-permute-start(bf16[64,1536]{1,0:T(8,128)(2,1)S(1)} %get-tuple-element.87), channel_id=1, source_target_pairs={{0,32},{1,97},{2,34},{3,99},{4,36},{5,101},{6,38},{7,103},{8,40},{... | collective-permute-start | bytes 589832 | tf_op jit(solution)/shard_map/ppermute | solution.py:78
  9.5 13.3 %collective-permute-start = (bf16[64,1536]{1,0:T(8,128)(2,1)S(1)}, bf16[64,1536]{1,0:T(8,128)(2,1)S(1)}, u32[]{:S(2)}, u32[]{:S(2)}) collective-permute-start(bf16[64,1536]{1,0:T(8,128)(2,1)S(1)} %get-tuple-element.89), channel_id=1, source_target_pairs={{0,8},{1,25},{2,10},{3,27},{4,12},{5,29},{6,14},{7,31},{8,16},{9,1... | collective-permute-start | bytes 589832 | tf_op jit(solution)/shard_map/ppermute | solution.py:78
  14.3 10.8 %collective-permute-start.12 = (bf16[64,1536]{1,0:T(8,128)(2,1)S(1)}, bf16[64,1536]{1,0:T(8,128)(2,1)S(1)}, u32[]{:S(2)}, u32[]{:S(2)}) collective-permute-start(bf16[64,1536]{1,0:T(8,128)(2,1)S(1)} %pad_maximum_fusion.5), channel_id=1, source_target_pairs={{0,2},{1,7},{2,4},{3,1},{4,6},{5,3},{6,0},{7,5},{8,10},{9,15},{10,... | collective-permute-start | bytes 589832 | tf_op jit(solution)/shard_map/ppermute | solution.py:78
  20.8 7.9 %collective-permute-start.7 = (bf16[64,1536]{1,0:T(8,128)(2,1)S(1)}, bf16[64,1536]{1,0:T(8,128)(2,1)S(1)}, u32[]{:S(2)}, u32[]{:S(2)}) collective-permute-start(bf16[64,1536]{1,0:T(8,128)(2,1)S(1)} %collective-permute-done.6), channel_id=1, source_target_pairs={{0,32},{1,97},{2,34},{3,99},{4,36},{5,101},{6,38},{7,103},{8,40},{... | collective-permute-start | bytes 589832 | tf_op jit(solution)/shard_map/ppermute | solution.py:78
  22.8 7.5 %collective-permute-start.1 = (bf16[64,1536]{1,0:T(8,128)(2,1)S(1)}, bf16[64,1536]{1,0:T(8,128)(2,1)S(1)}, u32[]{:S(2)}, u32[]{:S(2)}) collective-permute-start(bf16[64,1536]{1,0:T(8,128)(2,1)S(1)} %collective-permute-done), channel_id=1, source_target_pairs={{0,8},{1,25},{2,10},{3,27},{4,12},{5,29},{6,14},{7,31},{8,16},{9,1... | collective-permute-start | bytes 589832 | tf_op jit(solution)/shard_map/ppermute | solution.py:78
  25.1 6.9 %collective-permute-start.13 = (bf16[64,1536]{1,0:T(8,128)(2,1)S(1)}, bf16[64,1536]{1,0:T(8,128)(2,1)S(1)}, u32[]{:S(2)}, u32[]{:S(2)}) collective-permute-start(bf16[64,1536]{1,0:T(8,128)(2,1)S(1)} %collective-permute-done.12), channel_id=1, source_target_pairs={{0,2},{1,7},{2,4},{3,1},{4,6},{5,3},{6,0},{7,5},{8,10},{9,15},{10,... | collective-permute-start | bytes 589832 | tf_op jit(solution)/shard_map/ppermute | solution.py:78
  28.0 5.6 %copy-start.47 = (bf16[256,1536]{1,0:T(8,128)(2,1)S(1)}, bf16[256,1536]{1,0:T(8,128)(2,1)}, u32[]{:S(2)}) copy-start(bf16[256,1536]{1,0:T(8,128)(2,1)} %get-tuple-element.97) | copy-start | bytes 2359300
  28.7 6.9 %collective-permute-start.8 = (bf16[64,1536]{1,0:T(8,128)(2,1)S(1)}, bf16[64,1536]{1,0:T(8,128)(2,1)S(1)}, u32[]{:S(2)}, u32[]{:S(2)}) collective-permute-start(bf16[64,1536]{1,0:T(8,128)(2,1)S(1)} %collective-permute-done.7), channel_id=1, source_target_pairs={{0,32},{1,97},{2,34},{3,99},{4,36},{5,101},{6,38},{7,103},{8,40},{... | collective-permute-start | bytes 589832 | tf_op jit(solution)/shard_map/ppermute | solution.py:78
  30.3 6.9 %collective-permute-start.2 = (bf16[64,1536]{1,0:T(8,128)(2,1)S(1)}, bf16[64,1536]{1,0:T(8,128)(2,1)S(1)}, u32[]{:S(2)}, u32[]{:S(2)}) collective-permute-start(bf16[64,1536]{1,0:T(8,128)(2,1)S(1)} %collective-permute-done.1), channel_id=1, source_target_pairs={{0,8},{1,25},{2,10},{3,27},{4,12},{5,29},{6,14},{7,31},{8,16},{9,1... | collective-permute-start | bytes 589832 | tf_op jit(solution)/shard_map/ppermute | solution.py:78
  32.0 6.9 %collective-permute-start.14 = (bf16[64,1536]{1,0:T(8,128)(2,1)S(1)}, bf16[64,1536]{1,0:T(8,128)(2,1)S(1)}, u32[]{:S(2)}, u32[]{:S(2)}) collective-permute-start(bf16[64,1536]{1,0:T(8,128)(2,1)S(1)} %collective-permute-done.13), channel_id=1, source_target_pairs={{0,2},{1,7},{2,4},{3,1},{4,6},{5,3},{6,0},{7,5},{8,10},{9,15},{10,... | collective-permute-start | bytes 589832 | tf_op jit(solution)/shard_map/ppermute | solution.py:78
  33.7 15.3 %copy-start.31 = (bf16[1024,1536]{1,0:T(8,128)(2,1)S(1)}, bf16[1024,1536]{1,0:T(8,128)(2,1)}, u32[]{:S(2)}) copy-start(bf16[1024,1536]{1,0:T(8,128)(2,1)} %constant_dynamic-update-slice_fusion.11) | copy-start | bytes 9437188
  35.7 14.9 %copy-start.30 = (bf16[1024,1536]{1,0:T(8,128)(2,1)S(1)}, bf16[1024,1536]{1,0:T(8,128)(2,1)}, u32[]{:S(2)}) copy-start(bf16[1024,1536]{1,0:T(8,128)(2,1)} %constant_dynamic-update-slice_fusion.4) | copy-start | bytes 9437188
  35.7 13.3 %collective-permute-start.9 = (bf16[256,1536]{1,0:T(8,128)(2,1)S(1)}, bf16[256,1536]{1,0:T(8,128)(2,1)S(1)}, u32[]{:S(2)}, u32[]{:S(2)}) collective-permute-start(bf16[256,1536]{1,0:T(8,128)(2,1)S(1)} %pad_maximum_fusion.3), channel_id=1, source_target_pairs={{0,2},{1,7},{2,4},{3,1},{4,6},{5,3},{6,0},{7,5},{8,10},{9,15},{10,... | collective-permute-start | bytes 2359304 | tf_op jit(solution)/shard_map/ppermute | solution.py:78
  37.3 13.3 %collective-permute-start.3 = (bf16[256,1536]{1,0:T(8,128)(2,1)S(1)}, bf16[256,1536]{1,0:T(8,128)(2,1)S(1)}, u32[]{:S(2)}, u32[]{:S(2)}) collective-permute-start(bf16[256,1536]{1,0:T(8,128)(2,1)S(1)} %pad_maximum_fusion.2), channel_id=1, source_target_pairs={{0,32},{1,97},{2,34},{3,99},{4,36},{5,101},{6,38},{7,103},{8,40},{... | collective-permute-start | bytes 2359304 | tf_op jit(solution)/shard_map/ppermute | solution.py:78
  39.5 13.2 %collective-permute-start.15 = (bf16[256,1536]{1,0:T(8,128)(2,1)S(1)}, bf16[256,1536]{1,0:T(8,128)(2,1)S(1)}, u32[]{:S(2)}, u32[]{:S(2)}) collective-permute-start(bf16[256,1536]{1,0:T(8,128)(2,1)S(1)} %get-tuple-element.93), channel_id=1, source_target_pairs={{0,8},{1,25},{2,10},{3,27},{4,12},{5,29},{6,14},{7,31},{8,16},{9,1... | collective-permute-start | bytes 2359304 | tf_op jit(solution)/shard_map/ppermute | solution.py:78
  48.9 13.2 %collective-permute-start.10 = (bf16[256,1536]{1,0:T(8,128)(2,1)S(1)}, bf16[256,1536]{1,0:T(8,128)(2,1)S(1)}, u32[]{:S(2)}, u32[]{:S(2)}) collective-permute-start(bf16[256,1536]{1,0:T(8,128)(2,1)S(1)} %collective-permute-done.9), channel_id=1, source_target_pairs={{0,2},{1,7},{2,4},{3,1},{4,6},{5,3},{6,0},{7,5},{8,10},{9,15},{10,... | collective-permute-start | bytes 2359304 | tf_op jit(solution)/shard_map/ppermute | solution.py:78
  50.6 13.2 %collective-permute-start.4 = (bf16[256,1536]{1,0:T(8,128)(2,1)S(1)}, bf16[256,1536]{1,0:T(8,128)(2,1)S(1)}, u32[]{:S(2)}, u32[]{:S(2)}) collective-permute-start(bf16[256,1536]{1,0:T(8,128)(2,1)S(1)} %collective-permute-done.3), channel_id=1, source_target_pairs={{0,32},{1,97},{2,34},{3,99},{4,36},{5,101},{6,38},{7,103},{8,40},{... | collective-permute-start | bytes 2359304 | tf_op jit(solution)/shard_map/ppermute | solution.py:78
  52.7 13.2 %collective-permute-start.16 = (bf16[256,1536]{1,0:T(8,128)(2,1)S(1)}, bf16[256,1536]{1,0:T(8,128)(2,1)S(1)}, u32[]{:S(2)}, u32[]{:S(2)}) collective-permute-start(bf16[256,1536]{1,0:T(8,128)(2,1)S(1)} %collective-permute-done.15), channel_id=1, source_target_pairs={{0,8},{1,25},{2,10},{3,27},{4,12},{5,29},{6,14},{7,31},{8,16},{9,1... | collective-permute-start | bytes 2359304 | tf_op jit(solution)/shard_map/ppermute | solution.py:78
  62.1 13.2 %collective-permute-start.11 = (bf16[256,1536]{1,0:T(8,128)(2,1)S(1)}, bf16[256,1536]{1,0:T(8,128)(2,1)S(1)}, u32[]{:S(2)}, u32[]{:S(2)}) collective-permute-start(bf16[256,1536]{1,0:T(8,128)(2,1)S(1)} %collective-permute-done.10), channel_id=1, source_target_pairs={{0,2},{1,7},{2,4},{3,1},{4,6},{5,3},{6,0},{7,5},{8,10},{9,15},{10,... | collective-permute-start | bytes 2359304 | tf_op jit(solution)/shard_map/ppermute | solution.py:78
  63.8 13.2 %collective-permute-start.5 = (bf16[256,1536]{1,0:T(8,128)(2,1)S(1)}, bf16[256,1536]{1,0:T(8,128)(2,1)S(1)}, u32[]{:S(2)}, u32[]{:S(2)}) collective-permute-start(bf16[256,1536]{1,0:T(8,128)(2,1)S(1)} %collective-permute-done.4), channel_id=1, source_target_pairs={{0,32},{1,97},{2,34},{3,99},{4,36},{5,101},{6,38},{7,103},{8,40},{... | collective-permute-start | bytes 2359304 | tf_op jit(solution)/shard_map/ppermute | solution.py:78
  65.9 13.2 %collective-permute-start.17 = (bf16[256,1536]{1,0:T(8,128)(2,1)S(1)}, bf16[256,1536]{1,0:T(8,128)(2,1)S(1)}, u32[]{:S(2)}, u32[]{:S(2)}) collective-permute-start(bf16[256,1536]{1,0:T(8,128)(2,1)S(1)} %collective-permute-done.16), channel_id=1, source_target_pairs={{0,8},{1,25},{2,10},{3,27},{4,12},{5,29},{6,14},{7,31},{8,16},{9,1... | collective-permute-start | bytes 2359304 | tf_op jit(solution)/shard_map/ppermute | solution.py:78
  80.3 21.7 %collective-permute-start.27 = (bf16[512,1536]{1,0:T(8,128)(2,1)S(1)}, bf16[512,1536]{1,0:T(8,128)(2,1)S(1)}, u32[]{:S(2)}, u32[]{:S(2)}) collective-permute-start(bf16[512,1536]{1,0:T(8,128)(2,1)S(1)} %get-tuple-element.75), channel_id=1, source_target_pairs={{0,2},{1,7},{2,4},{3,1},{4,6},{5,3},{6,0},{7,5},{8,10},{9,15},{10,... | collective-permute-start | bytes 4718600 | tf_op jit(solution)/shard_map/ppermute | solution.py:96
  82.0 36.8 %collective-permute-start.19 = (bf16[512,1536]{1,0:T(8,128)(2,1)S(1)}, bf16[512,1536]{1,0:T(8,128)(2,1)S(1)}, u32[]{:S(2)}, u32[]{:S(2)}) collective-permute-start(bf16[512,1536]{1,0:T(8,128)(2,1)S(1)} %get-tuple-element.76), channel_id=1, source_target_pairs={{0,2},{1,7},{2,4},{3,1},{4,6},{5,3},{6,0},{7,5},{8,10},{9,15},{10,... | collective-permute-start | bytes 4718600 | tf_op jit(solution)/shard_map/ppermute | solution.py:96
  83.1 36.1 %collective-permute-start.31 = (bf16[512,1536]{1,0:T(8,128)(2,1)S(1)}, bf16[512,1536]{1,0:T(8,128)(2,1)}, u32[]{:S(2)}, u32[]{:S(2)}) collective-permute-start(bf16[512,1536]{1,0:T(8,128)(2,1)S(1)} %get-tuple-element.73), channel_id=1, source_target_pairs={{0,8},{1,25},{2,10},{3,27},{4,12},{5,29},{6,14},{7,31},{8,16},{9,1... | collective-permute-start | bytes 4718600 | tf_op jit(solution)/shard_map/ppermute | solution.py:96
  83.6 2.9 collective-permute-start.25
  83.7 38.1 %collective-permute-start.21 = (bf16[512,1536]{1,0:T(8,128)(2,1)S(1)}, bf16[512,1536]{1,0:T(8,128)(2,1)}, u32[]{:S(2)}, u32[]{:S(2)}) collective-permute-start(bf16[512,1536]{1,0:T(8,128)(2,1)S(1)} %get-tuple-element.74), channel_id=1, source_target_pairs={{0,8},{1,25},{2,10},{3,27},{4,12},{5,29},{6,14},{7,31},{8,16},{9,1... | collective-permute-start | bytes 4718600 | tf_op jit(solution)/shard_map/ppermute | solution.py:96
  86.5 70.8 %copy-start.43 = (bf16[96,3072]{1,0:T(8,128)(2,1)}, bf16[96,3072]{1,0:T(8,128)(2,1)S(1)}, u32[]{:S(2)}) copy-start(bf16[96,3072]{1,0:T(8,128)(2,1)S(1)} %collective-permute-done.25) | copy-start | bytes 1769476
  86.5 35.3 %collective-permute-start.23 = (bf16[512,1536]{1,0:T(8,128)(2,1)S(1)}, bf16[512,1536]{1,0:T(8,128)(2,1)}, u32[]{:S(2)}, u32[]{:S(2)}) collective-permute-start(bf16[512,1536]{1,0:T(8,128)(2,1)S(1)} %get-tuple-element.72), channel_id=1, source_target_pairs={{0,32},{1,97},{2,34},{3,99},{4,36},{5,101},{6,38},{7,103},{8,40},{... | collective-permute-start | bytes 4718600 | tf_op jit(solution)/shard_map/ppermute | solution.py:96
  102.0 55.3 %copy-start.34 = (bf16[512,1536]{1,0:T(8,128)(2,1)}, bf16[512,1536]{1,0:T(8,128)(2,1)S(1)}, u32[]{:S(2)}) copy-start(bf16[512,1536]{1,0:T(8,128)(2,1)S(1)} %collective-permute-done.27) | copy-start | bytes 4718596
  102.0 23.2 %collective-permute-start.35 = (bf16[512,1536]{1,0:T(8,128)(2,1)S(1)}, bf16[512,1536]{1,0:T(8,128)(2,1)}, u32[]{:S(2)}, u32[]{:S(2)}) collective-permute-start(bf16[512,1536]{1,0:T(8,128)(2,1)S(1)} %get-tuple-element.71), channel_id=1, source_target_pairs={{0,32},{1,97},{2,34},{3,99},{4,36},{5,101},{6,38},{7,103},{8,40},{... | collective-permute-start | bytes 4718600 | tf_op jit(solution)/shard_map/ppermute | solution.py:96
  118.8 21.7 %collective-permute-start.28 = (bf16[512,1536]{1,0:T(8,128)(2,1)S(1)}, bf16[512,1536]{1,0:T(8,128)(2,1)}, u32[]{:S(2)}, u32[]{:S(2)}) collective-permute-start(bf16[512,1536]{1,0:T(8,128)(2,1)S(1)} %collective-permute-done.27), channel_id=1, source_target_pairs={{0,2},{1,7},{2,4},{3,1},{4,6},{5,3},{6,0},{7,5},{8,10},{9,15},{10,... | collective-permute-start | bytes 4718600 | tf_op jit(solution)/shard_map/ppermute | solution.py:96
  119.3 38.1 %collective-permute-start.20 = (bf16[512,1536]{1,0:T(8,128)(2,1)S(1)}, bf16[512,1536]{1,0:T(8,128)(2,1)S(1)}, u32[]{:S(2)}, u32[]{:S(2)}) collective-permute-start(bf16[512,1536]{1,0:T(8,128)(2,1)S(1)} %collective-permute-done.19), channel_id=1, source_target_pairs={{0,2},{1,7},{2,4},{3,1},{4,6},{5,3},{6,0},{7,5},{8,10},{9,15},{10,... | collective-permute-start | bytes 4718600 | tf_op jit(solution)/shard_map/ppermute | solution.py:96
  121.8 42.6 %collective-permute-start.22 = (bf16[512,1536]{1,0:T(8,128)(2,1)}, bf16[512,1536]{1,0:T(8,128)(2,1)}, u32[]{:S(2)}, u32[]{:S(2)}) collective-permute-start(bf16[512,1536]{1,0:T(8,128)(2,1)} %collective-permute-done.21), channel_id=1, source_target_pairs={{0,8},{1,25},{2,10},{3,27},{4,12},{5,29},{6,14},{7,31},{8,16},{9,1... | collective-permute-start | bytes 4718600 | tf_op jit(solution)/shard_map/ppermute | solution.py:96
  121.8 42.6 %collective-permute-start.24 = (bf16[512,1536]{1,0:T(8,128)(2,1)}, bf16[512,1536]{1,0:T(8,128)(2,1)}, u32[]{:S(2)}, u32[]{:S(2)}) collective-permute-start(bf16[512,1536]{1,0:T(8,128)(2,1)} %collective-permute-done.23), channel_id=1, source_target_pairs={{0,32},{1,97},{2,34},{3,99},{4,36},{5,101},{6,38},{7,103},{8,40},{... | collective-permute-start | bytes 4718600 | tf_op jit(solution)/shard_map/ppermute | solution.py:96
  125.2 39.3 %collective-permute-start.32 = (bf16[512,1536]{1,0:T(8,128)(2,1)}, bf16[512,1536]{1,0:T(8,128)(2,1)}, u32[]{:S(2)}, u32[]{:S(2)}) collective-permute-start(bf16[512,1536]{1,0:T(8,128)(2,1)} %collective-permute-done.31), channel_id=1, source_target_pairs={{0,8},{1,25},{2,10},{3,27},{4,12},{5,29},{6,14},{7,31},{8,16},{9,1... | collective-permute-start | bytes 4718600 | tf_op jit(solution)/shard_map/ppermute | solution.py:96
  140.6 24.3 %collective-permute-start.36 = (bf16[512,1536]{1,0:T(8,128)(2,1)}, bf16[512,1536]{1,0:T(8,128)(2,1)}, u32[]{:S(2)}, u32[]{:S(2)}) collective-permute-start(bf16[512,1536]{1,0:T(8,128)(2,1)} %collective-permute-done.35), channel_id=1, source_target_pairs={{0,32},{1,97},{2,34},{3,99},{4,36},{5,101},{6,38},{7,103},{8,40},{... | collective-permute-start | bytes 4718600 | tf_op jit(solution)/shard_map/ppermute | solution.py:96
  158.5 21.9 %collective-permute-start.29 = (bf16[512,1536]{1,0:T(8,128)(2,1)}, bf16[512,1536]{1,0:T(8,128)(2,1)}, u32[]{:S(2)}, u32[]{:S(2)}) collective-permute-start(bf16[512,1536]{1,0:T(8,128)(2,1)} %collective-permute-done.28), channel_id=1, source_target_pairs={{0,2},{1,7},{2,4},{3,1},{4,6},{5,3},{6,0},{7,5},{8,10},{9,15},{10,... | collective-permute-start | bytes 4718600 | tf_op jit(solution)/shard_map/ppermute | solution.py:96
  158.6 25.5 %copy-start.28 = (s32[4]{0:T(128)}, s32[4]{0:T(128)S(1)}, u32[]{:S(2)}) copy-start(s32[4]{0:T(128)S(1)} %pad_add_fusion.place_ref) | copy-start | bytes 52
  159.4 24.7 %copy-start.7 = (bf16[512,1536]{1,0:T(8,128)(2,1)S(1)}, bf16[512,1536]{1,0:T(8,128)(2,1)}, u32[]{:S(2)}) copy-start(bf16[512,1536]{1,0:T(8,128)(2,1)} %copy-done.6) | copy-start | bytes 4718596
  159.4 24.7 %copy-start.9 = (bf16[512,1536]{1,0:T(8,128)(2,1)S(1)}, bf16[512,1536]{1,0:T(8,128)(2,1)}, u32[]{:S(2)}) copy-start(bf16[512,1536]{1,0:T(8,128)(2,1)} %copy-done.8) | copy-start | bytes 4718596
  161.9 22.3 %copy-start.3 = (bf16[512,1536]{1,0:T(8,128)(2,1)S(1)}, bf16[512,1536]{1,0:T(8,128)(2,1)}, u32[]{:S(2)}) copy-start(bf16[512,1536]{1,0:T(8,128)(2,1)} %copy-done.2) | copy-start | bytes 4718596
  161.9 22.3 %copy-start.5 = (bf16[512,1536]{1,0:T(8,128)(2,1)S(1)}, bf16[512,1536]{1,0:T(8,128)(2,1)}, u32[]{:S(2)}) copy-start(bf16[512,1536]{1,0:T(8,128)(2,1)} %copy-done.4) | copy-start | bytes 4718596
  164.4 43.5 %collective-permute-start.26 = (bf16[512,1536]{1,0:T(8,128)(2,1)}, bf16[512,1536]{1,0:T(8,128)(2,1)S(1)}, u32[]{:S(2)}, u32[]{:S(2)}) collective-permute-start(bf16[512,1536]{1,0:T(8,128)(2,1)} %copy-done.35), channel_id=1, source_target_pairs={{0,2},{1,7},{2,4},{3,1},{4,6},{5,3},{6,0},{7,5},{8,10},{9,15},{10,... | collective-permute-start | bytes 4718600 | tf_op jit(solution)/shard_map/ppermute | solution.py:96
  164.4 43.5 %collective-permute-start.30 = (bf16[512,1536]{1,0:T(8,128)(2,1)}, bf16[512,1536]{1,0:T(8,128)(2,1)S(1)}, u32[]{:S(2)}, u32[]{:S(2)}) collective-permute-start(bf16[512,1536]{1,0:T(8,128)(2,1)} %collective-permute-done.22), channel_id=1, source_target_pairs={{0,8},{1,25},{2,10},{3,27},{4,12},{5,29},{6,14},{7,31},{8,16},{9,1... | collective-permute-start | bytes 4718600 | tf_op jit(solution)/shard_map/ppermute | solution.py:96
  164.5 43.4 %collective-permute-start.33 = (bf16[512,1536]{1,0:T(8,128)(2,1)}, bf16[512,1536]{1,0:T(8,128)(2,1)S(1)}, u32[]{:S(2)}, u32[]{:S(2)}) collective-permute-start(bf16[512,1536]{1,0:T(8,128)(2,1)} %collective-permute-done.32), channel_id=1, source_target_pairs={{0,8},{1,25},{2,10},{3,27},{4,12},{5,29},{6,14},{7,31},{8,16},{9,1... | collective-permute-start | bytes 4718600 | tf_op jit(solution)/shard_map/ppermute | solution.py:96
  164.9 43.0 %collective-permute-start.37 = (bf16[512,1536]{1,0:T(8,128)(2,1)}, bf16[512,1536]{1,0:T(8,128)(2,1)S(1)}, u32[]{:S(2)}, u32[]{:S(2)}) collective-permute-start(bf16[512,1536]{1,0:T(8,128)(2,1)} %collective-permute-done.36), channel_id=1, source_target_pairs={{0,32},{1,97},{2,34},{3,99},{4,36},{5,101},{6,38},{7,103},{8,40},{... | collective-permute-start | bytes 4718600 | tf_op jit(solution)/shard_map/ppermute | solution.py:96
  180.4 27.5 %collective-permute-start.34 = (bf16[512,1536]{1,0:T(8,128)(2,1)}, bf16[512,1536]{1,0:T(8,128)(2,1)S(1)}, u32[]{:S(2)}, u32[]{:S(2)}) collective-permute-start(bf16[512,1536]{1,0:T(8,128)(2,1)} %collective-permute-done.24), channel_id=1, source_target_pairs={{0,32},{1,97},{2,34},{3,99},{4,36},{5,101},{6,38},{7,103},{8,40},{... | collective-permute-start | bytes 4718600 | tf_op jit(solution)/shard_map/ppermute | solution.py:96
  211.0 29.2 %copy-start.12 = (bf16[96,3072]{1,0:T(8,128)(2,1)S(1)}, bf16[96,3072]{1,0:T(8,128)(2,1)}, u32[]{:S(2)}) copy-start(bf16[96,3072]{1,0:T(8,128)(2,1)} %given.1) | copy-start | bytes 1769476
  211.0 29.2 %copy-start.16 = (bf16[96,3072]{1,0:T(8,128)(2,1)S(1)}, bf16[96,3072]{1,0:T(8,128)(2,1)}, u32[]{:S(2)}) copy-start(bf16[96,3072]{1,0:T(8,128)(2,1)} %noise.3) | copy-start | bytes 1769476
  211.0 29.2 %copy-start.27 = (f32[3072]{0:T(1024)S(1)}, f32[3072]{0:T(1024)}, u32[]{:S(2)}) copy-start(f32[3072]{0:T(1024)} %param.25) | copy-start | bytes 36868
  237.9 2.3 collective-permute-start.38
  243.3 2.3 collective-permute-start.39
  246.4 30.9 %copy-start.17 = (bf16[64,3072]{1,0:T(8,128)(2,1)S(1)}, bf16[64,3072]{1,0:T(8,128)(2,1)}, u32[]{:S(2)}) copy-start(bf16[64,3072]{1,0:T(8,128)(2,1)} %get-tuple-element.77.adapt_out.fake_out) | copy-start | bytes 1179652
  267.1 3.1 collective-permute-start.40
  274.4 2.8 collective-permute-start.41
  289.4 2.8 collective-permute-start.42
  296.1 27.4 %copy-start.1 = (bf16[3072,64]{0,1:T(8,128)(2,1)S(1)}, bf16[3072,64]{0,1:T(8,128)(2,1)}, u32[]{:S(2)}) copy-start(bf16[3072,64]{0,1:T(8,128)(2,1)} %param.19) | copy-start | bytes 1179652
  (31 other events, 66.6 us)
where the time goes:
time: 324 us
  waiting for transfers between devices  122 us (38%)
  Pallas kernels  85.3 us (26%)
  local copies, waits for them, and re-layouts  43.8 us (14%)
  starting transfers between devices  32.3 us (10%)
  blocking collectives  25 us (8%)
  other arithmetic  9.95 us (3%)
  matrix products  3.64 us (1%)
    ppermute x18, waiting for transfers between devices, ring_slots(): lax.ppermute(slots[h][i][-1], AXES, chip_ring(RING_AXES[i][2]))  76.2 us
    ppermute x18, waiting for transfers between devices, ring(): held.append(lax.ppermute(held[-1], AXES, chip_ring(RING_AXES[i][phase])))  36.2 us
    pallas_call x1, Pallas kernels, gen_forward(): pl.pallas_call(gen_body, out_shape=(shape, shape, jax.ShapeDtypeStruct((g...  26.9 us
    unnamed x121, local copies, waits for them, and re-layouts  25.8 us
    all_to_all x1, blocking collectives, local(): received = lax.all_to_all(packed, CHIPS, 0, 0, tiled=True)  25 us
    pallas_call x1, Pallas kernels, load_weights(): pl.pallas_call(load_body, out_shape=(shape, shape), in_specs=[IN_SMEM] +...  22.3 us
    pallas_call x1, Pallas kernels, score_forward(): pl.pallas_call(score_body, out_shape=(jax.ShapeDtypeStruct((group, hidden...  20.6 us
    ppermute x18, starting transfers between devices, ring(): held.append(lax.ppermute(held[-1], AXES, chip_ring(RING_AXES[i][phase])))  17.8 us
  transfers between devices with their start and end apart: 43, of which 24 were waited for; matrix products, arithmetic and copies ran while one was open for 11% of the time, Pallas kernels for 7%

commit v1 on v0

--- a/solution.py
+++ b/solution.py
@@ -79,22 +79,27 @@
     return slots
 
 
-def ring_slots(pieces, early, middle):
-    for phase in range(2):
-        pieces = [jnp.concatenate(held, axis=0) for held in ring(pieces, phase)]
-    pieces, early = lax.optimization_barrier((pieces, early))
+def ring_slots(pieces, adapters, exchange, inputs, prepare):
+    pieces = [jnp.concatenate(held, axis=0) for held in ring(pieces, 0)]
+    pieces, adapters = lax.optimization_barrier((pieces, adapters))
+    exchanged = exchange(adapters)
+    pieces = [jnp.concatenate(held, axis=0) for held in ring(pieces, 1)]
+    pieces, exchanged = lax.optimization_barrier((pieces, exchanged))
     count = pieces[0].shape[0] // 2
     slots = [[[piece[h * count : (h + 1) * count]] for piece in pieces] for h in range(2)]
     for step in range(1, RING):
         if step == RING - 1:
             held = [slots[0][i][-1] for i in range(3)]
-            held, middle = lax.optimization_barrier((held, middle))
+            held, prepared = lax.optimization_barrier((held, prepared))
             for i in range(3):
                 slots[0][i][-1] = held[i]
         for h in range(2):
             for i in range(3):
                 slots[h][i].append(lax.ppermute(slots[h][i][-1], AXES, chip_ring(RING_AXES[i][2])))
-    return slots, early, middle
+        if step == 1:
+            slots[0][0][1], inputs = lax.optimization_barrier((slots[0][0][1], inputs))
+            prepared = prepare(*inputs)
+    return slots, exchanged, prepared
 
 
 SHARD = 96
@@ -202,7 +207,7 @@
     return pl.pallas_call(
         load_body,
         out_shape=(shape, shape),
-        in_specs=[IN_SMEM] + [ANYWHERE] * 18,
+        in_specs=[IN_SMEM] + [IN_HBM] * 18,
         out_specs=(IN_HBM, IN_HBM),
         scratch_shapes=[
             pltpu.VMEM(shape.shape, shape.dtype),
@@ -254,32 +259,36 @@
     for n in (0, 1, 4, 5):
         fetches[n].wait()
 
+    hidden = last.shape[3]
+
     def hidden_tile(n):
-        column_copy(up_in, up, up_sems, n).wait()
         cols = tile_at(n)
-        part = pl.ds(pl.multiple_of(lax.rem(n, per_quarter) * TILE, TILE), TILE)
-
-        def place(k):
-            for i in (0, 2):
-                quarter, row = piece_place(place_ref, i, 3, k)
-
-                @pl.when(quarter == lax.div(n, per_quarter))
-                def _(i=i, row=row):
-                    if i == 0:
-                        up[pl.ds(row, PIECE), cols] = last[0, k, :, part]
-                    else:
-                        up[pl.ds(pl.multiple_of(row + PIECE, 32), REST), cols] = last[2, k, :REST, part]
-
-        each(pieces, place, 1)
         pre = dot(u[...], up[:, cols]) + dot(low[...], adapt[:, cols])
         value, slope[:, cols] = gelu_and_slope(pre)
         act[:, cols] = value.astype(act.dtype)
 
-    each(tiles, hidden_tile, 1)
+    for q in range(2):
+        quarter_cols = pl.ds(q * hidden, hidden)
+        for n in range(q * per_quarter, (q + 1) * per_quarter):
+            column_copy(up_in, up, up_sems, n).wait()
+
+        def place(k, q=q, quarter_cols=quarter_cols):
+            for i in (0, 2):
+                quarter, row = piece_place(place_ref, i, 3, k)
+
+                @pl.when(quarter == q)
+                def _(i=i, row=row):
+                    if i == 0:
+                        up[pl.ds(row, PIECE), quarter_cols] = last[0, k]
+                    else:
+                        rest = pl.ds(pl.multiple_of(row + PIECE, 32), REST)
+                        up[rest, quarter_cols] = last[2, k, :REST]
+
+        each(pieces, place, 1)
+        each(per_quarter, lambda n, q=q: hidden_tile(q * per_quarter + n), 1)
     for n in (2, 3):
         fetches[n].wait()
     whole_down.wait()
-    hidden = last.shape[3]
 
     def place_down(k):
         for i in (1, 2):
@@ -328,7 +337,7 @@
             jax.ShapeDtypeStruct((rows, width), f32),
             jax.ShapeDtypeStruct((rows, width), bf16),
         ),
-        in_specs=[IN_SMEM] + [IN_VMEM] * 3 + [ANYWHERE] * 6 + [IN_HBM] * 2,
+        in_specs=[IN_SMEM] + [IN_VMEM] * 3 + [IN_HBM] * 8,
         out_specs=(IN_HBM, IN_HBM) + (IN_VMEM,) * 3,
         scratch_shapes=[
             pltpu.VMEM(shape.shape, bf16),
@@ -596,41 +605,37 @@
     def both_rows(mine):
         return jnp.concatenate([mine, swap_cores(mine)], axis=0)
 
-    coords = jnp.stack(
-        [
-            lax.axis_index("z"),
-            lax.axis_index("y"),
-            lax.axis_index("xh") * 2 + xl,
-            1 - 2 * core,
-        ]
-    ).astype(jnp.int32)
-    down_rows = base_down.T
-
     def both_quarters(mine):
         theirs = lax.ppermute(mine, "xl", [(0, 1), (1, 0)])
         quarters = [jnp.where(xl == 0, mine, theirs), jnp.where(xl == 0, theirs, mine)]
         return jnp.concatenate(quarters, axis=1)
 
-    adapt_out = both_quarters(jnp.concatenate([gen_adapt_out, fake_adapt_out], axis=0))
-    gen_scale, gen_shift = modulation(gen_steps)
-    u_mine = modulate(
-        gen_input,
-        jnp.where(in_last, gen_scale[1:], gen_scale[:1]),
-        jnp.where(in_last, gen_shift[1:], gen_shift[:1]),
-    )
-    u_gen = both_rows(u_mine)
-    low_gen = matmul(u_gen, gen_adapt_in).astype(bf16)
-    mods = jnp.concatenate(modulation(score_steps), axis=0)
-    blends = (two_steps(score_steps).astype(f32) + 0.5) / 1000.0
-    ends = (last_image * IMG_TOK - first_row).astype(jnp.int32).reshape(1)
+    def prepare(given, gen_steps, score_steps):
+        gen_scale, gen_shift = modulation(gen_steps)
+        u_mine = modulate(
+            given,
+            jnp.where(in_last, gen_scale[1:], gen_scale[:1]),
+            jnp.where(in_last, gen_shift[1:], gen_shift[:1]),
+        )
+        u_gen = both_rows(u_mine)
+        low_gen = matmul(u_gen, gen_adapt_in).astype(bf16)
+        mods = jnp.concatenate(modulation(score_steps), axis=0)
+        blends = (two_steps(score_steps).astype(f32) + 0.5) / 1000.0
+        ends = (last_image * IMG_TOK - first_row).astype(jnp.int32).reshape(1)
+        place = [lax.axis_index("z"), lax.axis_index("y"), lax.axis_index("xh") * 2 + xl, 1 - 2 * core]
+        return u_gen, low_gen, mods, blends, ends, jnp.stack(place).astype(jnp.int32)
+
+    down_rows = base_down.T
     slots, adapt_out, prepared = ring_slots(
         [
             base_up[:PIECE],
             down_rows[:PIECE],
             jnp.concatenate([base_up[PIECE:], down_rows[PIECE:]], axis=0),
         ],
-        adapt_out,
-        (u_gen, low_gen, mods, blends, ends, coords),
+        jnp.concatenate([gen_adapt_out, fake_adapt_out], axis=0),
+        both_quarters,
+        (gen_input, gen_steps, score_steps),
+        prepare,
     )
     u_gen, low_gen, mods, blends, ends, coords = prepared
     gen_out, fake_out = adapt_out[:rank], adapt_out[rank:]

time: 324 us -> 333 us (1.028)
  waiting for transfers between devices: 122 us -> 143 us
  local copies, waits for them, and re-layouts: 43.8 us -> 24.4 us
  other arithmetic: 9.95 us -> 19.2 us
    unnamed x121 -> x98, local copies, waits for them, and re-layouts: 25.8 us -> 9.25 us
    ppermute x18, waiting for transfers between devices: 36.2 us -> 46.1 us  [ring(): held.append(lax.ppermute(held[-1], AXES, chip_ring(RING_AXES[i][phase])))]
    ppermute x18, waiting for transfers between devices: 76.2 us -> 85.4 us  [ring_slots(): lax.ppermute(slots[h][i][-1], AXES, chip_ring(RING_AXES[i][2]))]
    concatenate x3 -> x7, other arithmetic: 0.89 us -> 8.46 us  [the longest x3 7.55 us: ring_slots(): pieces = [jnp.concatenate(held, axis=0) for held in ring(pieces, 1)]]
  transfers between devices with their start and end apart: 43 -> 43, of which waited for: 24 -> 28; matrix products, arithmetic and copies ran while one was open for 11% -> 8% of each run, Pallas kernels for 7% -> 7%
where the time goes in v1:
time: 333 us; the launch traced here: 332 us
  waiting for transfers between devices  143 us (43%)
  Pallas kernels  85.4 us (26%)
  starting transfers between devices  29.6 us (9%)
  blocking collectives  24.9 us (7%)
  local copies, waits for them, and re-layouts  24.4 us (7%)
  other arithmetic  19.2 us (6%)
  matrix products  4.48 us (1%)
    ppermute x18, waiting for transfers between devices, ring_slots(): lax.ppermute(slots[h][i][-1], AXES, chip_ring(RING_AXES[i][2]))  85.4 us
    ppermute x18, waiting for transfers between devices, ring(): held.append(lax.ppermute(held[-1], AXES, chip_ring(RING_AXES[i][phase])))  46.1 us
    pallas_call x1, Pallas kernels, gen_forward(): pl.pallas_call(gen_body, out_shape=(shape, shape, jax.ShapeDtypeStruct((g...  26.9 us
    all_to_all x1, blocking collectives, local(): received = lax.all_to_all(packed, CHIPS, 0, 0, tiled=True)  24.9 us
    pallas_call x1, Pallas kernels, load_weights(): pl.pallas_call(load_body, out_shape=(shape, shape), in_specs=[IN_SMEM] +...  22.3 us
    pallas_call x1, Pallas kernels, score_forward(): pl.pallas_call(score_body, out_shape=(jax.ShapeDtypeStruct((group, hidden...  20.7 us
    ppermute x18, starting transfers between devices, ring(): held.append(lax.ppermute(held[-1], AXES, chip_ring(RING_AXES[i][phase])))  16.4 us
    ppermute x18, starting transfers between devices, ring_slots(): lax.ppermute(slots[h][i][-1], AXES, chip_ring(RING_AXES[i][2]))  12.1 us
  transfers between devices with their start and end apart: 43, of which 28 were waited for; matrix products, arithmetic and copies ran while one was open for 8% of the time, Pallas kernels for 7%

profile of v1, /device:TPU:0, one launch (start us, length us, event | category | flops | bytes accessed | tf_op | source)
XLA Modules:
  0.0 332.2 jit_solution(15576532211460425608)
XLA Ops:
  1.7 1.7 collective-permute-start
  4.4 2.0 collective-permute-start.3
  8.2 1.6 collective-permute-start.6
  9.8 1.6 collective-permute-start.1
  12.1 1.2 collective-permute-start.4
  13.4 1.8 collective-permute-done.6
  15.4 1.3 collective-permute-done.1
  17.1 1.9 collective-permute-done.4
  19.0 3.0 collective-permute-done.7
  22.0 1.6 collective-permute-done.2
  23.7 2.2 collective-permute-done.5
  25.9 3.0 collective-permute-done.8
  28.9 2.0 collective-permute-start.9
  30.9 1.6 collective-permute-start.15
  32.5 9.8 %collective-permute-done.9 = bf16[256,1536]{1,0:T(8,128)(2,1)} collective-permute-done((bf16[256,1536]{1,0:T(8,128)(2,1)S(1)}, bf16[256,1536]{1,0:T(8,128)(2,1)}, u32[]{:S(2)}, u32[]{:S(2)}) %collective-permute-start.9) | collective-permute-done | bytes 786464 | tf_op jit(solution)/shard_map/ppermute | solution.py:78
  43.0 1.2 collective-permute-done.12
  44.2 1.6 collective-permute-start.16
  45.9 9.9 %collective-permute-done.10 = bf16[256,1536]{1,0:T(8,128)(2,1)} collective-permute-done((bf16[256,1536]{1,0:T(8,128)(2,1)}, bf16[256,1536]{1,0:T(8,128)(2,1)}, u32[]{:S(2)}, u32[]{:S(2)}) %collective-permute-start.10) | collective-permute-done | bytes 786464 | tf_op jit(solution)/shard_map/ppermute | solution.py:78
  55.8 1.9 collective-permute-done.13
  57.7 1.6 collective-permute-start.14
  59.3 1.6 collective-permute-done.18
  63.0 6.2 %collective-permute-done.11 = bf16[256,1536]{1,0:T(8,128)(2,1)S(1)} collective-permute-done((bf16[256,1536]{1,0:T(8,128)(2,1)}, bf16[256,1536]{1,0:T(8,128)(2,1)S(1)}, u32[]{:S(2)}, u32[]{:S(2)}) %collective-permute-start.11) | collective-permute-done | bytes 786464 | tf_op jit(solution)/shard_map/ppermute | solution.py:78
  69.2 1.5 pad_maximum_fusion
  71.1 3.0 pad_maximum_fusion.1
  74.2 1.3 collective-permute-done.17
  75.5 3.0 pad_maximum_fusion.2
  78.7 2.7 collective-permute-start.19
  81.5 2.2 fusion.28
  85.4 1.7 collective-permute-start.35
  87.1 13.4 %collective-permute-done.19 = bf16[512,1536]{1,0:T(8,128)(2,1)} collective-permute-done((bf16[512,1536]{1,0:T(8,128)(2,1)S(1)}, bf16[512,1536]{1,0:T(8,128)(2,1)}, u32[]{:S(2)}, u32[]{:S(2)}) %collective-permute-start.19) | collective-permute-done | bytes 1572896 | tf_op jit(solution)/shard_map/ppermute | solution.py:98
  100.5 1.7 collective-permute-start.23
  104.0 1.4 add_multiply_fusion
  105.3 1.4 add_convert_fusion
  107.9 9.3 %collective-permute-done.27 = bf16[512,1536]{1,0:T(8,128)(2,1)S(1)} collective-permute-done((bf16[512,1536]{1,0:T(8,128)(2,1)S(1)}, bf16[512,1536]{1,0:T(8,128)(2,1)S(1)}, u32[]{:S(2)}, u32[]{:S(2)}) %collective-permute-start.27) | collective-permute-done | bytes 1572896 | tf_op jit(solution)/shard_map/ppermute | solution.py:98
  117.3 1.4 collective-permute-start.20
  119.3 3.1 collective-permute-done.21
  122.5 1.5 collective-permute-done.23
  124.5 31.5 %collective-permute-done.28 = bf16[512,1536]{1,0:T(8,128)(2,1)} collective-permute-done((bf16[512,1536]{1,0:T(8,128)(2,1)S(1)}, bf16[512,1536]{1,0:T(8,128)(2,1)}, u32[]{:S(2)}, u32[]{:S(2)}) %collective-permute-start.28) | collective-permute-done | bytes 1572896 | tf_op jit(solution)/shard_map/ppermute | solution.py:98
  156.1 1.7 collective-permute-start.36
  158.8 2.5 convolution_convert_fusion.low.low_gen
  161.2 2.5 pad_maximum_fusion.3.u
  163.9 1.3 collective-permute-start.33
  165.2 12.8 %collective-permute-done.36 = bf16[512,1536]{1,0:T(8,128)(2,1)} collective-permute-done((bf16[512,1536]{1,0:T(8,128)(2,1)}, bf16[512,1536]{1,0:T(8,128)(2,1)}, u32[]{:S(2)}, u32[]{:S(2)}) %collective-permute-start.36) | collective-permute-done | bytes 1572896 | tf_op jit(solution)/shard_map/ppermute | solution.py:98
  178.4 1.2 collective-permute-done.29
  179.7 2.1 fusion.30
  181.8 22.3 %load_weights.1 = (bf16[3072,3072]{1,0:T(8,128)(2,1)}, bf16[3072,3072]{1,0:T(8,128)(2,1)}) custom-call(s32[4]{0:T(128)S(1)} %pad_add_fusion.place_ref, bf16[8,64,1536]{2,1,0:T(8,128)(2,1)S(1)} %bitcast.52, bf16[8,64,1536]{2,1,0:T(8,128)(2,1)S(1)} %bitcast.54, bf16[8,64,1536]{2,1,0:T(8,128)(2,1)S(1)} %bitcast.56, bf16[8,64,1536]{2,1,0:T(8,128)(2,1)S(1)} %bitcast.51, ...), custom_call_target="tpu_custom_call" | custom-call | bytes 150994944 | tf_op jit(solution)/shard_map/load_weights/pallas_call | solution.py:207
  204.3 12.4 %collective-permute-done.34 = bf16[512,1536]{1,0:T(8,128)(2,1)S(1)} collective-permute-done((bf16[512,1536]{1,0:T(8,128)(2,1)}, bf16[512,1536]{1,0:T(8,128)(2,1)S(1)}, u32[]{:S(2)}, u32[]{:S(2)}) %collective-permute-start.34) | collective-permute-done | bytes 1572896 | tf_op jit(solution)/shard_map/ppermute | solution.py:98
  216.7 1.2 copy-done.36
  217.9 26.9 %gen_forward.1 = (bf16[3072,3072]{1,0:T(8,128)(2,1)}, bf16[3072,3072]{1,0:T(8,128)(2,1)}, f32[192,3072]{1,0:T(8,128)}, f32[96,3072]{1,0:T(8,128)}, bf16[96,3072]{1,0:T(8,128)(2,1)}) custom-call(s32[4]{0:T(128)} %copy-done.25, bf16[192,3072]{1,0:T(8,128)(2,1)} %pad_maximum_fusion.3.u, ...), custom_call_target="tpu_custom_call", output_to_operand_aliasing={{0}: (10, {}), {1}: (11, {})} | custom-call | flops 7247757312 | bytes 52428800 | tf_op jit(solution)/shard_map/gen_forward/pallas_call | solution.py:331
  244.9 2.2 collective-permute-done.38.other
  247.1 1.3 copy-done.17
  248.4 1.9 add_noise.1
  250.8 1.9 collective-permute-done.39.u_other
  253.4 20.7 %score_forward.1 = (f32[192,3072]{1,0:T(8,128)}, bf16[192,64]{1,0:T(8,128)(2,1)}, f32[96,3072]{1,0:T(8,128)}, f32[96,3072]{1,0:T(8,128)}, bf16[192,3072]{1,0:T(8,128)(2,1)}) custom-call(bf16[96,3072]{1,0:T(8,128)(2,1)} %copy-done.20, bf16[96,3072]{1,0:T(8,128)(2,1)} %copy-done.39, bf16[64,3072]{1,0:T(8,128)(2,1)} %bitcast.74, ...), custom_call_target="tpu_custom_call" | custom-call | flops 10871635968 | bytes 52428800 | tf_op jit(solution)/shard_map/score_forward/pallas_call | solution.py:403
  274.3 3.0 collective-permute-done.40.others
  277.2 1.3 copy-done.18
  278.5 1.3 copy-done.19
  279.8 1.7 cotangents.1
  281.6 2.7 collective-permute-done.41.cots_other
  284.4 12.0 %backward.1 = (bf16[2,64,3072]{2,1,0:T(8,128)(2,1)S(1)}, f32[2,192,64]{2,1,0:T(8,128)S(1)}) custom-call(bf16[192,3072]{1,0:T(8,128)(2,1)S(1)} %get-tuple-element.79.cots_mine, bf16[192,3072]{1,0:T(8,128)(2,1)S(1)} %collective-permute-done.41.cots_other, f32[192,3072]{1,0:T(8,128)S(1)} %copy-done.13, f32[192,3072]{1,0:T(8,128)S(1)} %copy-done.14, ...), custom_call_target="tpu_custom_call" | custom-call | flops 7247757312 | bytes 31457280 | tf_op jit(solution)/shard_map/backward/pallas_call | solution.py:464
  297.9 1.4 reshape.190
  300.9 1.2 copy.26
  302.0 1.4 fusion.4
  305.2 24.9 %all_to_all.5 = bf16[64,72,128]{2,1,0:T(8,128)(2,1)S(1)} all-to-all(bf16[64,72,128]{2,1,0:T(8,128)(2,1)S(1)} %pad_maximum_fusion.4), channel_id=1, replica_groups=mesh['z'=4,'y'=4,'xh'=2,'xl'=2,'core'=2] {'z','y','xh','xl'}, dimensions={0} | all-to-all | bytes 2359296 | tf_op jit(solution)/shard_map/all_to_all | solution.py:682
  (183 shorter events, 25.1 us)
Async XLA Ops:
  0.6 158.1 %copy-start = (bf16[3072,64]{0,1:T(8,128)(2,1)S(1)}, bf16[3072,64]{0,1:T(8,128)(2,1)}, u32[]{:S(2)}) copy-start(bf16[3072,64]{0,1:T(8,128)(2,1)} %param.19) | copy-start | bytes 1179652
  1.7 8.1 %collective-permute-start = (bf16[64,1536]{1,0:T(8,128)(2,1)S(1)}, bf16[64,1536]{1,0:T(8,128)(2,1)S(1)}, u32[]{:S(2)}, u32[]{:S(2)}) collective-permute-start(bf16[64,1536]{1,0:T(8,128)(2,1)S(1)} %slice.113), channel_id=1, source_target_pairs={{0,8},{1,25},{2,10},{3,27},{4,12},{5,29},{6,14},{7,31},{8,16},{9,1... | collective-permute-start | bytes 589832 | tf_op jit(solution)/shard_map/ppermute | solution.py:78
  4.4 7.8 %collective-permute-start.3 = (bf16[64,1536]{1,0:T(8,128)(2,1)S(1)}, bf16[64,1536]{1,0:T(8,128)(2,1)S(1)}, u32[]{:S(2)}, u32[]{:S(2)}) collective-permute-start(bf16[64,1536]{1,0:T(8,128)(2,1)S(1)} %slice.149), channel_id=1, source_target_pairs={{0,32},{1,97},{2,34},{3,99},{4,36},{5,101},{6,38},{7,103},{8,40},{... | collective-permute-start | bytes 589832 | tf_op jit(solution)/shard_map/ppermute | solution.py:78
  8.2 6.9 %collective-permute-start.6 = (bf16[64,1536]{1,0:T(8,128)(2,1)S(1)}, bf16[64,1536]{1,0:T(8,128)(2,1)S(1)}, u32[]{:S(2)}, u32[]{:S(2)}) collective-permute-start(bf16[64,1536]{1,0:T(8,128)(2,1)S(1)} %pad_maximum_fusion.9), channel_id=1, source_target_pairs={{0,2},{1,7},{2,4},{3,1},{4,6},{5,3},{6,0},{7,5},{8,10},{9,15},{10,... | collective-permute-start | bytes 589832 | tf_op jit(solution)/shard_map/ppermute | solution.py:78
  9.8 6.9 %collective-permute-start.1 = (bf16[64,1536]{1,0:T(8,128)(2,1)S(1)}, bf16[64,1536]{1,0:T(8,128)(2,1)S(1)}, u32[]{:S(2)}, u32[]{:S(2)}) collective-permute-start(bf16[64,1536]{1,0:T(8,128)(2,1)S(1)} %collective-permute-done), channel_id=1, source_target_pairs={{0,8},{1,25},{2,10},{3,27},{4,12},{5,29},{6,14},{7,31},{8,16},{9,1... | collective-permute-start | bytes 589832 | tf_op jit(solution)/shard_map/ppermute | solution.py:78
  12.1 6.9 %collective-permute-start.4 = (bf16[64,1536]{1,0:T(8,128)(2,1)S(1)}, bf16[64,1536]{1,0:T(8,128)(2,1)S(1)}, u32[]{:S(2)}, u32[]{:S(2)}) collective-permute-start(bf16[64,1536]{1,0:T(8,128)(2,1)S(1)} %collective-permute-done.3), channel_id=1, source_target_pairs={{0,32},{1,97},{2,34},{3,99},{4,36},{5,101},{6,38},{7,103},{8,40},{... | collective-permute-start | bytes 589832 | tf_op jit(solution)/shard_map/ppermute | solution.py:78
  15.1 6.9 %collective-permute-start.7 = (bf16[64,1536]{1,0:T(8,128)(2,1)S(1)}, bf16[64,1536]{1,0:T(8,128)(2,1)S(1)}, u32[]{:S(2)}, u32[]{:S(2)}) collective-permute-start(bf16[64,1536]{1,0:T(8,128)(2,1)S(1)} %collective-permute-done.6), channel_id=1, source_target_pairs={{0,2},{1,7},{2,4},{3,1},{4,6},{5,3},{6,0},{7,5},{8,10},{9,15},{10,... | collective-permute-start | bytes 589832 | tf_op jit(solution)/shard_map/ppermute | solution.py:78
  16.7 6.9 %collective-permute-start.2 = (bf16[64,1536]{1,0:T(8,128)(2,1)S(1)}, bf16[64,1536]{1,0:T(8,128)(2,1)S(1)}, u32[]{:S(2)}, u32[]{:S(2)}) collective-permute-start(bf16[64,1536]{1,0:T(8,128)(2,1)S(1)} %collective-permute-done.1), channel_id=1, source_target_pairs={{0,8},{1,25},{2,10},{3,27},{4,12},{5,29},{6,14},{7,31},{8,16},{9,1... | collective-permute-start | bytes 589832 | tf_op jit(solution)/shard_map/ppermute | solution.py:78
  19.0 6.9 %collective-permute-start.5 = (bf16[64,1536]{1,0:T(8,128)(2,1)S(1)}, bf16[64,1536]{1,0:T(8,128)(2,1)S(1)}, u32[]{:S(2)}, u32[]{:S(2)}) collective-permute-start(bf16[64,1536]{1,0:T(8,128)(2,1)S(1)} %collective-permute-done.4), channel_id=1, source_target_pairs={{0,32},{1,97},{2,34},{3,99},{4,36},{5,101},{6,38},{7,103},{8,40},{... | collective-permute-start | bytes 589832 | tf_op jit(solution)/shard_map/ppermute | solution.py:78
  22.0 6.9 %collective-permute-start.8 = (bf16[64,1536]{1,0:T(8,128)(2,1)S(1)}, bf16[64,1536]{1,0:T(8,128)(2,1)S(1)}, u32[]{:S(2)}, u32[]{:S(2)}) collective-permute-start(bf16[64,1536]{1,0:T(8,128)(2,1)S(1)} %collective-permute-done.7), channel_id=1, source_target_pairs={{0,2},{1,7},{2,4},{3,1},{4,6},{5,3},{6,0},{7,5},{8,10},{9,15},{10,... | collective-permute-start | bytes 589832 | tf_op jit(solution)/shard_map/ppermute | solution.py:78
  28.9 30.4 %copy-start.37 = (bf16[256,1536]{1,0:T(8,128)(2,1)}, bf16[256,1536]{1,0:T(8,128)(2,1)S(1)}, u32[]{:S(2)}) copy-start(bf16[256,1536]{1,0:T(8,128)(2,1)S(1)} %constant_dynamic-update-slice_fusion) | copy-start | bytes 2359300
  28.9 13.4 %collective-permute-start.9 = (bf16[256,1536]{1,0:T(8,128)(2,1)S(1)}, bf16[256,1536]{1,0:T(8,128)(2,1)}, u32[]{:S(2)}, u32[]{:S(2)}) collective-permute-start(bf16[256,1536]{1,0:T(8,128)(2,1)S(1)} %pad_maximum_fusion.5), channel_id=1, source_target_pairs={{0,32},{1,97},{2,34},{3,99},{4,36},{5,101},{6,38},{7,103},{8,40},{... | collective-permute-start | bytes 2359304 | tf_op jit(solution)/shard_map/ppermute | solution.py:78
  30.9 13.3 %collective-permute-start.12 = (bf16[256,1536]{1,0:T(8,128)(2,1)S(1)}, bf16[256,1536]{1,0:T(8,128)(2,1)}, u32[]{:S(2)}, u32[]{:S(2)}) collective-permute-start(bf16[256,1536]{1,0:T(8,128)(2,1)S(1)} %pad_maximum_fusion.6), channel_id=1, source_target_pairs={{0,2},{1,7},{2,4},{3,1},{4,6},{5,3},{6,0},{7,5},{8,10},{9,15},{10,... | collective-permute-start | bytes 2359304 | tf_op jit(solution)/shard_map/ppermute | solution.py:78
  30.9 13.3 %collective-permute-start.15 = (bf16[256,1536]{1,0:T(8,128)(2,1)S(1)}, bf16[256,1536]{1,0:T(8,128)(2,1)}, u32[]{:S(2)}, u32[]{:S(2)}) collective-permute-start(bf16[256,1536]{1,0:T(8,128)(2,1)S(1)} %constant_dynamic-update-slice_fusion), channel_id=1, source_target_pairs={{0,8},{1,25},{2,10},{3,27},{4,12},{5,29},{6,14},{7,31},{8,16},{9,1... | collective-permute-start | bytes 2359304 | tf_op jit(solution)/shard_map/ppermute | solution.py:78
  42.3 13.5 %collective-permute-start.10 = (bf16[256,1536]{1,0:T(8,128)(2,1)}, bf16[256,1536]{1,0:T(8,128)(2,1)}, u32[]{:S(2)}, u32[]{:S(2)}) collective-permute-start(bf16[256,1536]{1,0:T(8,128)(2,1)} %collective-permute-done.9), channel_id=1, source_target_pairs={{0,32},{1,97},{2,34},{3,99},{4,36},{5,101},{6,38},{7,103},{8,40},{... | collective-permute-start | bytes 2359304 | tf_op jit(solution)/shard_map/ppermute | solution.py:78
  44.2 13.5 %collective-permute-start.13 = (bf16[256,1536]{1,0:T(8,128)(2,1)}, bf16[256,1536]{1,0:T(8,128)(2,1)}, u32[]{:S(2)}, u32[]{:S(2)}) collective-permute-start(bf16[256,1536]{1,0:T(8,128)(2,1)} %collective-permute-done.12), channel_id=1, source_target_pairs={{0,2},{1,7},{2,4},{3,1},{4,6},{5,3},{6,0},{7,5},{8,10},{9,15},{10,... | collective-permute-start | bytes 2359304 | tf_op jit(solution)/shard_map/ppermute | solution.py:78
  44.2 16.7 %collective-permute-start.18 = (bf16[128,1536]{1,0:T(8,128)(2,1)S(1)}, bf16[128,1536]{1,0:T(8,128)(2,1)}, u32[]{:S(2)}, u32[]{:S(2)}) collective-permute-start(bf16[128,1536]{1,0:T(8,128)(2,1)S(1)} %pad_maximum_fusion.8), channel_id=1, source_target_pairs={{0,2},{2,0},{1,3},{3,1},{4,6},{6,4},{5,7},{7,5},{8,10},{10,8},{9,1... | collective-permute-start | bytes 1179656 | tf_op jit(solution)/shard_map/ppermute | solution.py:609
  44.2 17.8 %collective-permute-start.16 = (bf16[256,1536]{1,0:T(8,128)(2,1)}, bf16[256,1536]{1,0:T(8,128)(2,1)}, u32[]{:S(2)}, u32[]{:S(2)}) collective-permute-start(bf16[256,1536]{1,0:T(8,128)(2,1)} %collective-permute-done.15), channel_id=1, source_target_pairs={{0,8},{1,25},{2,10},{3,27},{4,12},{5,29},{6,14},{7,31},{8,16},{9,1... | collective-permute-start | bytes 2359304 | tf_op jit(solution)/shard_map/ppermute | solution.py:78
  55.8 13.4 %collective-permute-start.11 = (bf16[256,1536]{1,0:T(8,128)(2,1)}, bf16[256,1536]{1,0:T(8,128)(2,1)S(1)}, u32[]{:S(2)}, u32[]{:S(2)}) collective-permute-start(bf16[256,1536]{1,0:T(8,128)(2,1)} %collective-permute-done.10), channel_id=1, source_target_pairs={{0,32},{1,97},{2,34},{3,99},{4,36},{5,101},{6,38},{7,103},{8,40},{... | collective-permute-start | bytes 2359304 | tf_op jit(solution)/shard_map/ppermute | solution.py:78
  57.7 13.4 %collective-permute-start.14 = (bf16[256,1536]{1,0:T(8,128)(2,1)}, bf16[256,1536]{1,0:T(8,128)(2,1)S(1)}, u32[]{:S(2)}, u32[]{:S(2)}) collective-permute-start(bf16[256,1536]{1,0:T(8,128)(2,1)} %collective-permute-done.13), channel_id=1, source_target_pairs={{0,2},{1,7},{2,4},{3,1},{4,6},{5,3},{6,0},{7,5},{8,10},{9,15},{10,... | collective-permute-start | bytes 2359304 | tf_op jit(solution)/shard_map/ppermute | solution.py:78
  62.0 13.5 %collective-permute-start.17 = (bf16[256,1536]{1,0:T(8,128)(2,1)}, bf16[256,1536]{1,0:T(8,128)(2,1)S(1)}, u32[]{:S(2)}, u32[]{:S(2)}) collective-permute-start(bf16[256,1536]{1,0:T(8,128)(2,1)} %collective-permute-done.16), channel_id=1, source_target_pairs={{0,8},{1,25},{2,10},{3,27},{4,12},{5,29},{6,14},{7,31},{8,16},{9,1... | collective-permute-start | bytes 2359304 | tf_op jit(solution)/shard_map/ppermute | solution.py:78
  78.7 21.8 %collective-permute-start.19 = (bf16[512,1536]{1,0:T(8,128)(2,1)S(1)}, bf16[512,1536]{1,0:T(8,128)(2,1)}, u32[]{:S(2)}, u32[]{:S(2)}) collective-permute-start(bf16[512,1536]{1,0:T(8,128)(2,1)S(1)} %get-tuple-element.92), channel_id=1, source_target_pairs={{0,2},{1,7},{2,4},{3,1},{4,6},{5,3},{6,0},{7,5},{8,10},{9,15},{10,... | collective-permute-start | bytes 4718600 | tf_op jit(solution)/shard_map/ppermute | solution.py:98
  81.4 35.9 %collective-permute-start.27 = (bf16[512,1536]{1,0:T(8,128)(2,1)S(1)}, bf16[512,1536]{1,0:T(8,128)(2,1)S(1)}, u32[]{:S(2)}, u32[]{:S(2)}) collective-permute-start(bf16[512,1536]{1,0:T(8,128)(2,1)S(1)} %get-tuple-element.91), channel_id=1, source_target_pairs={{0,2},{1,7},{2,4},{3,1},{4,6},{5,3},{6,0},{7,5},{8,10},{9,15},{10,... | collective-permute-start | bytes 4718600 | tf_op jit(solution)/shard_map/ppermute | solution.py:98
  83.8 34.9 %collective-permute-start.31 = (bf16[512,1536]{1,0:T(8,128)(2,1)S(1)}, bf16[512,1536]{1,0:T(8,128)(2,1)}, u32[]{:S(2)}, u32[]{:S(2)}) collective-permute-start(bf16[512,1536]{1,0:T(8,128)(2,1)S(1)} %get-tuple-element.89), channel_id=1, source_target_pairs={{0,8},{1,25},{2,10},{3,27},{4,12},{5,29},{6,14},{7,31},{8,16},{9,1... | collective-permute-start | bytes 4718600 | tf_op jit(solution)/shard_map/ppermute | solution.py:98
  83.9 19.5 %copy-start.46 = (s32[12]{0:T(128)S(1)}, s32[12]{0:T(128)}, u32[]{:S(2)}) copy-start(s32[12]{0:T(128)} %param.16) | copy-start | bytes 148
  83.9 19.5 %copy-start.47 = (s32[12]{0:T(128)S(1)}, s32[12]{0:T(128)}, u32[]{:S(2)}) copy-start(s32[12]{0:T(128)} %param.15) | copy-start | bytes 148
  83.9 23.3 %copy-start.44 = (f32[3072]{0:T(1024)S(1)}, f32[3072]{0:T(1024)}, u32[]{:S(2)}) copy-start(f32[3072]{0:T(1024)} %param.23) | copy-start | bytes 36868
  83.9 23.3 %copy-start.45 = (f32[3072]{0:T(1024)S(1)}, f32[3072]{0:T(1024)}, u32[]{:S(2)}) copy-start(f32[3072]{0:T(1024)} %param.24) | copy-start | bytes 36868
  83.9 34.8 %copy-start.10 = (bf16[96,3072]{1,0:T(8,128)(2,1)S(1)}, bf16[96,3072]{1,0:T(8,128)(2,1)}, u32[]{:S(2)}) copy-start(bf16[96,3072]{1,0:T(8,128)(2,1)} %given.1) | copy-start | bytes 1769476
  83.9 38.5 %collective-permute-start.21 = (bf16[512,1536]{1,0:T(8,128)(2,1)S(1)}, bf16[512,1536]{1,0:T(8,128)(2,1)}, u32[]{:S(2)}, u32[]{:S(2)}) collective-permute-start(bf16[512,1536]{1,0:T(8,128)(2,1)S(1)} %get-tuple-element.90), channel_id=1, source_target_pairs={{0,8},{1,25},{2,10},{3,27},{4,12},{5,29},{6,14},{7,31},{8,16},{9,1... | collective-permute-start | bytes 4718600 | tf_op jit(solution)/shard_map/ppermute | solution.py:98
  85.4 37.0 %copy-start.6 = (bf16[512,1536]{1,0:T(8,128)(2,1)}, bf16[512,1536]{1,0:T(8,128)(2,1)S(1)}, u32[]{:S(2)}) copy-start(bf16[512,1536]{1,0:T(8,128)(2,1)S(1)} %get-tuple-element.87) | copy-start | bytes 4718596
  85.4 37.0 %collective-permute-start.35 = (bf16[512,1536]{1,0:T(8,128)(2,1)S(1)}, bf16[512,1536]{1,0:T(8,128)(2,1)}, u32[]{:S(2)}, u32[]{:S(2)}) collective-permute-start(bf16[512,1536]{1,0:T(8,128)(2,1)S(1)} %get-tuple-element.87), channel_id=1, source_target_pairs={{0,32},{1,97},{2,34},{3,99},{4,36},{5,101},{6,38},{7,103},{8,40},{... | collective-permute-start | bytes 4718600 | tf_op jit(solution)/shard_map/ppermute | solution.py:98
  100.5 23.5 %collective-permute-start.23 = (bf16[512,1536]{1,0:T(8,128)(2,1)S(1)}, bf16[512,1536]{1,0:T(8,128)(2,1)}, u32[]{:S(2)}, u32[]{:S(2)}) collective-permute-start(bf16[512,1536]{1,0:T(8,128)(2,1)S(1)} %get-tuple-element.88), channel_id=1, source_target_pairs={{0,32},{1,97},{2,34},{3,99},{4,36},{5,101},{6,38},{7,103},{8,40},{... | collective-permute-start | bytes 4718600 | tf_op jit(solution)/shard_map/ppermute | solution.py:98
  117.3 40.5 %collective-permute-start.20 = (bf16[512,1536]{1,0:T(8,128)(2,1)}, bf16[512,1536]{1,0:T(8,128)(2,1)}, u32[]{:S(2)}, u32[]{:S(2)}) collective-permute-start(bf16[512,1536]{1,0:T(8,128)(2,1)} %collective-permute-done.19), channel_id=1, source_target_pairs={{0,2},{1,7},{2,4},{3,1},{4,6},{5,3},{6,0},{7,5},{8,10},{9,15},{10,... | collective-permute-start | bytes 4718600 | tf_op jit(solution)/shard_map/ppermute | solution.py:98
  118.6 37.4 %collective-permute-start.28 = (bf16[512,1536]{1,0:T(8,128)(2,1)S(1)}, bf16[512,1536]{1,0:T(8,128)(2,1)}, u32[]{:S(2)}, u32[]{:S(2)}) collective-permute-start(bf16[512,1536]{1,0:T(8,128)(2,1)S(1)} %collective-permute-done.27), channel_id=1, source_target_pairs={{0,2},{1,7},{2,4},{3,1},{4,6},{5,3},{6,0},{7,5},{8,10},{9,15},{10,... | collective-permute-start | bytes 4718600 | tf_op jit(solution)/shard_map/ppermute | solution.py:98
  122.4 2.0 collective-permute-start.25
  122.4 41.3 %collective-permute-start.22 = (bf16[512,1536]{1,0:T(8,128)(2,1)}, bf16[512,1536]{1,0:T(8,128)(2,1)}, u32[]{:S(2)}, u32[]{:S(2)}) collective-permute-start(bf16[512,1536]{1,0:T(8,128)(2,1)} %collective-permute-done.21), channel_id=1, source_target_pairs={{0,8},{1,25},{2,10},{3,27},{4,12},{5,29},{6,14},{7,31},{8,16},{9,1... | collective-permute-start | bytes 4718600 | tf_op jit(solution)/shard_map/ppermute | solution.py:98
  124.0 39.7 %collective-permute-start.24 = (bf16[512,1536]{1,0:T(8,128)(2,1)}, bf16[512,1536]{1,0:T(8,128)(2,1)}, u32[]{:S(2)}, u32[]{:S(2)}) collective-permute-start(bf16[512,1536]{1,0:T(8,128)(2,1)} %collective-permute-done.23), channel_id=1, source_target_pairs={{0,32},{1,97},{2,34},{3,99},{4,36},{5,101},{6,38},{7,103},{8,40},{... | collective-permute-start | bytes 4718600 | tf_op jit(solution)/shard_map/ppermute | solution.py:98
  124.5 31.6 %copy-start.41 = (bf16[96,3072]{1,0:T(8,128)(2,1)}, bf16[96,3072]{1,0:T(8,128)(2,1)S(1)}, u32[]{:S(2)}) copy-start(bf16[96,3072]{1,0:T(8,128)(2,1)S(1)} %collective-permute-done.25) | copy-start | bytes 1769476
  124.5 39.5 %collective-permute-start.32 = (bf16[512,1536]{1,0:T(8,128)(2,1)}, bf16[512,1536]{1,0:T(8,128)(2,1)}, u32[]{:S(2)}, u32[]{:S(2)}) collective-permute-start(bf16[512,1536]{1,0:T(8,128)(2,1)} %collective-permute-done.31), channel_id=1, source_target_pairs={{0,8},{1,25},{2,10},{3,27},{4,12},{5,29},{6,14},{7,31},{8,16},{9,1... | collective-permute-start | bytes 4718600 | tf_op jit(solution)/shard_map/ppermute | solution.py:98
  156.1 21.9 %collective-permute-start.36 = (bf16[512,1536]{1,0:T(8,128)(2,1)}, bf16[512,1536]{1,0:T(8,128)(2,1)}, u32[]{:S(2)}, u32[]{:S(2)}) collective-permute-start(bf16[512,1536]{1,0:T(8,128)(2,1)} %collective-permute-done.35), channel_id=1, source_target_pairs={{0,32},{1,97},{2,34},{3,99},{4,36},{5,101},{6,38},{7,103},{8,40},{... | collective-permute-start | bytes 4718600 | tf_op jit(solution)/shard_map/ppermute | solution.py:98
  157.7 21.9 %collective-permute-start.29 = (bf16[512,1536]{1,0:T(8,128)(2,1)}, bf16[512,1536]{1,0:T(8,128)(2,1)}, u32[]{:S(2)}, u32[]{:S(2)}) collective-permute-start(bf16[512,1536]{1,0:T(8,128)(2,1)} %collective-permute-done.28), channel_id=1, source_target_pairs={{0,2},{1,7},{2,4},{3,1},{4,6},{5,3},{6,0},{7,5},{8,10},{9,15},{10,... | collective-permute-start | bytes 4718600 | tf_op jit(solution)/shard_map/ppermute | solution.py:98
  158.0 23.8 %copy-start.25 = (s32[4]{0:T(128)}, s32[4]{0:T(128)S(1)}, u32[]{:S(2)}) copy-start(s32[4]{0:T(128)S(1)} %pad_add_fusion.place_ref) | copy-start | bytes 52
  158.8 23.0 %copy-start.7 = (bf16[512,1536]{1,0:T(8,128)(2,1)S(1)}, bf16[512,1536]{1,0:T(8,128)(2,1)}, u32[]{:S(2)}) copy-start(bf16[512,1536]{1,0:T(8,128)(2,1)} %copy-done.6) | copy-start | bytes 4718596
  158.8 23.0 %copy-start.9 = (bf16[512,1536]{1,0:T(8,128)(2,1)S(1)}, bf16[512,1536]{1,0:T(8,128)(2,1)}, u32[]{:S(2)}) copy-start(bf16[512,1536]{1,0:T(8,128)(2,1)} %copy-done.8) | copy-start | bytes 4718596
  161.2 20.6 %copy-start.3 = (bf16[512,1536]{1,0:T(8,128)(2,1)S(1)}, bf16[512,1536]{1,0:T(8,128)(2,1)}, u32[]{:S(2)}) copy-start(bf16[512,1536]{1,0:T(8,128)(2,1)} %copy-done.2) | copy-start | bytes 4718596
  161.2 20.6 %copy-start.5 = (bf16[512,1536]{1,0:T(8,128)(2,1)S(1)}, bf16[512,1536]{1,0:T(8,128)(2,1)}, u32[]{:S(2)}) copy-start(bf16[512,1536]{1,0:T(8,128)(2,1)} %copy-done.4) | copy-start | bytes 4718596
  163.7 40.5 %collective-permute-start.26 = (bf16[512,1536]{1,0:T(8,128)(2,1)}, bf16[512,1536]{1,0:T(8,128)(2,1)S(1)}, u32[]{:S(2)}, u32[]{:S(2)}) collective-permute-start(bf16[512,1536]{1,0:T(8,128)(2,1)} %collective-permute-done.20), channel_id=1, source_target_pairs={{0,2},{1,7},{2,4},{3,1},{4,6},{5,3},{6,0},{7,5},{8,10},{9,15},{10,... | collective-permute-start | bytes 4718600 | tf_op jit(solution)/shard_map/ppermute | solution.py:98
  163.7 40.5 %collective-permute-start.30 = (bf16[512,1536]{1,0:T(8,128)(2,1)}, bf16[512,1536]{1,0:T(8,128)(2,1)S(1)}, u32[]{:S(2)}, u32[]{:S(2)}) collective-permute-start(bf16[512,1536]{1,0:T(8,128)(2,1)} %collective-permute-done.22), channel_id=1, source_target_pairs={{0,8},{1,25},{2,10},{3,27},{4,12},{5,29},{6,14},{7,31},{8,16},{9,1... | collective-permute-start | bytes 4718600 | tf_op jit(solution)/shard_map/ppermute | solution.py:98
  163.9 40.3 %collective-permute-start.33 = (bf16[512,1536]{1,0:T(8,128)(2,1)}, bf16[512,1536]{1,0:T(8,128)(2,1)S(1)}, u32[]{:S(2)}, u32[]{:S(2)}) collective-permute-start(bf16[512,1536]{1,0:T(8,128)(2,1)} %collective-permute-done.32), channel_id=1, source_target_pairs={{0,8},{1,25},{2,10},{3,27},{4,12},{5,29},{6,14},{7,31},{8,16},{9,1... | collective-permute-start | bytes 4718600 | tf_op jit(solution)/shard_map/ppermute | solution.py:98
  178.0 26.2 %collective-permute-start.37 = (bf16[512,1536]{1,0:T(8,128)(2,1)}, bf16[512,1536]{1,0:T(8,128)(2,1)S(1)}, u32[]{:S(2)}, u32[]{:S(2)}) collective-permute-start(bf16[512,1536]{1,0:T(8,128)(2,1)} %collective-permute-done.36), channel_id=1, source_target_pairs={{0,32},{1,97},{2,34},{3,99},{4,36},{5,101},{6,38},{7,103},{8,40},{... | collective-permute-start | bytes 4718600 | tf_op jit(solution)/shard_map/ppermute | solution.py:98
  179.7 37.0 %collective-permute-start.34 = (bf16[512,1536]{1,0:T(8,128)(2,1)}, bf16[512,1536]{1,0:T(8,128)(2,1)S(1)}, u32[]{:S(2)}, u32[]{:S(2)}) collective-permute-start(bf16[512,1536]{1,0:T(8,128)(2,1)} %collective-permute-done.24), channel_id=1, source_target_pairs={{0,32},{1,97},{2,34},{3,99},{4,36},{5,101},{6,38},{7,103},{8,40},{... | collective-permute-start | bytes 4718600 | tf_op jit(solution)/shard_map/ppermute | solution.py:98
  204.2 13.7 %copy-start.34 = (bf16[512,1536]{1,0:T(8,128)(2,1)}, bf16[512,1536]{1,0:T(8,128)(2,1)S(1)}, u32[]{:S(2)}) copy-start(bf16[512,1536]{1,0:T(8,128)(2,1)S(1)} %collective-permute-done.33) | copy-start | bytes 4718596
  204.2 13.7 %copy-start.32 = (bf16[512,1536]{1,0:T(8,128)(2,1)}, bf16[512,1536]{1,0:T(8,128)(2,1)S(1)}, u32[]{:S(2)}) copy-start(bf16[512,1536]{1,0:T(8,128)(2,1)S(1)} %collective-permute-done.26) | copy-start | bytes 4718596
  217.9 29.2 %copy-start.11 = (bf16[96,3072]{1,0:T(8,128)(2,1)S(1)}, bf16[96,3072]{1,0:T(8,128)(2,1)}, u32[]{:S(2)}) copy-start(bf16[96,3072]{1,0:T(8,128)(2,1)} %given.1) | copy-start | bytes 1769476
  217.9 29.2 %copy-start.15 = (bf16[96,3072]{1,0:T(8,128)(2,1)S(1)}, bf16[96,3072]{1,0:T(8,128)(2,1)}, u32[]{:S(2)}) copy-start(bf16[96,3072]{1,0:T(8,128)(2,1)} %noise.3) | copy-start | bytes 1769476
  217.9 29.2 %copy-start.24 = (f32[3072]{0:T(1024)S(1)}, f32[3072]{0:T(1024)}, u32[]{:S(2)}) copy-start(f32[3072]{0:T(1024)} %param.25) | copy-start | bytes 36868
  244.8 2.3 collective-permute-start.38
  250.3 2.3 collective-permute-start.39
  253.4 30.9 %copy-start.16 = (bf16[64,3072]{1,0:T(8,128)(2,1)S(1)}, bf16[64,3072]{1,0:T(8,128)(2,1)}, u32[]{:S(2)}) copy-start(bf16[64,3072]{1,0:T(8,128)(2,1)} %get-tuple-element.93.adapt_out.fake_out) | copy-start | bytes 1179652
  274.1 3.1 collective-permute-start.40
  281.5 2.8 collective-permute-start.41
  296.5 2.8 collective-permute-start.42
  305.0 27.3 %copy-start.1 = (bf16[3072,64]{0,1:T(8,128)(2,1)S(1)}, bf16[3072,64]{0,1:T(8,128)(2,1)}, u32[]{:S(2)}) copy-start(bf16[3072,64]{0,1:T(8,128)(2,1)} %param.19) | copy-start | bytes 1179652
  (27 other events, 106.0 us)

commit v2 on v1

--- a/solution.py
+++ b/solution.py
@@ -27,13 +27,6 @@
     return 0.5 * (1.0 + tanh_val) + 0.5 * pre * (1.0 - tanh_val * tanh_val) * root_two_pi * (
         1.0 + 3.0 * gelu_coef * pre * pre
     )
-
-
-def embedding(steps, feature_count):
-    half_width = feature_count // 2
-    frequency = jnp.exp(-math.log(10000.0) * jnp.arange(half_width, dtype=jnp.float32) / half_width)
-    phase_angle = steps.astype(jnp.float32)[:, None] * frequency[None, :]
-    return jnp.concatenate([jnp.sin(phase_angle), jnp.cos(phase_angle)], axis=1)
 
 
 def modulate(rows, scale_rows, shift_rows):
@@ -71,33 +64,38 @@
     return pairs
 
 
-def ring(pieces, phase):
+def send(piece, i, phase):
+    return lax.ppermute(piece, AXES, chip_ring(RING_AXES[i][phase]))
+
+
+def gathered(pieces, phase):
+    rows = pieces[0].shape[0]
+    whole = [jnp.zeros((RING * rows, piece.shape[1]), piece.dtype) for piece in pieces]
+    for step in range(RING):
+        if step:
+            pieces = [send(piece, i, phase) for i, piece in enumerate(pieces)]
+        whole = [
+            lax.dynamic_update_slice(buffer, piece, (step * rows, 0))
+            for buffer, piece in zip(whole, pieces)
+        ]
+    return whole
+
+
+def ring_slots(pieces, adapters, exchange, inputs, prepare):
+    pieces = gathered(pieces, 0)
+    pieces[2], adapters = lax.optimization_barrier((pieces[2], adapters))
+    exchanged = exchange(adapters)
+    pieces = gathered(pieces, 1)
+    pieces[2], exchanged = lax.optimization_barrier((pieces[2], exchanged))
     slots = [[piece] for piece in pieces]
-    for _ in range(RING - 1):
-        for i, held in enumerate(slots):
-            held.append(lax.ppermute(held[-1], AXES, chip_ring(RING_AXES[i][phase])))
-    return slots
-
-
-def ring_slots(pieces, adapters, exchange, inputs, prepare):
-    pieces = [jnp.concatenate(held, axis=0) for held in ring(pieces, 0)]
-    pieces, adapters = lax.optimization_barrier((pieces, adapters))
-    exchanged = exchange(adapters)
-    pieces = [jnp.concatenate(held, axis=0) for held in ring(pieces, 1)]
-    pieces, exchanged = lax.optimization_barrier((pieces, exchanged))
-    count = pieces[0].shape[0] // 2
-    slots = [[[piece[h * count : (h + 1) * count]] for piece in pieces] for h in range(2)]
     for step in range(1, RING):
         if step == RING - 1:
-            held = [slots[0][i][-1] for i in range(3)]
-            held, prepared = lax.optimization_barrier((held, prepared))
-            for i in range(3):
-                slots[0][i][-1] = held[i]
-        for h in range(2):
-            for i in range(3):
-                slots[h][i].append(lax.ppermute(slots[h][i][-1], AXES, chip_ring(RING_AXES[i][2])))
+            slots[2][-1], prepared = lax.optimization_barrier((slots[2][-1], prepared))
+        for i in range(3):
+            slots[i].append(send(slots[i][-1], i, 2))
         if step == 1:
-            slots[0][0][1], inputs = lax.optimization_barrier((slots[0][0][1], inputs))
+            arrived = [slots[i][1] for i in range(3)]
+            _, inputs = lax.optimization_barrier((arrived, inputs))
             prepared = prepare(*inputs)
     return slots, exchanged, prepared
 
@@ -137,15 +135,16 @@
     first, second, third = RING_AXES[i]
 
     def source(axis, distance):
-        return lax.rem(me[axis] - distance * direction + RING, RING)
-
+        return (me[axis] - distance * direction + RING) & (RING - 1)
+
+    zero = k - k
     at = {
-        first: source(first, lax.rem(k, RING)),
-        second: source(second, lax.div(k, RING)),
-        third: source(third, step),
+        first: source(first, k & (RING - 1)),
+        second: source(second, k >> 2),
+        third: source(third, step + zero),
     }
-    group = (at["z"] * 4 + at["y"]) * 2 + lax.div(at["x"], 2)
-    return lax.rem(at["x"], 2), pl.multiple_of(group * SHARD, 32)
+    group = (at["z"] * 4 + at["y"]) * 2 + (at["x"] >> 1)
+    return at["x"] & 1, group * SHARD
 
 
 def each(count, one, unroll=4):
@@ -173,24 +172,24 @@
 
 
 def load_body(place_ref, *refs):
-    slots, (up_out, down_out, up, down, sems) = refs[:18], refs[18:]
+    slots, (up_out, down_out, up, down, sems) = refs[:9], refs[9:]
     for n, slot in enumerate(slots):
-        step, half, i = n // 6, n // 3 % 2, n % 3
-
-        def one(k, slot=slot, step=step, half=half, i=i, n=n):
-            quarter, row = piece_place(place_ref, i, step, 2 * RING * half + k)
-            start_piece(i, slot.at[k], quarter, row, up, down, sems.at[n])
-
-        each(2 * RING, one)
+        step, i = n // 3, n % 3
+
+        def one(k, slot=slot, step=step, i=i, n=n):
+            quarter, row = piece_place(place_ref, i, step, k)
+            start_piece(i, slot.at[k], quarter, pl.multiple_of(row, 32), up, down, sems.at[n])
+
+        each(RING * RING, one)
     for n, slot in enumerate(slots):
         if n % 3 != 1:
             wait_all(slot, sems.at[n])
-    up_copy = pltpu.make_async_copy(up, up_out, sems.at[18])
+    up_copy = pltpu.make_async_copy(up, up_out, sems.at[9])
     up_copy.start()
     for n, slot in enumerate(slots):
         if n % 3 == 1:
             wait_all(slot, sems.at[n])
-    down_copy = pltpu.make_async_copy(down, down_out, sems.at[19])
+    down_copy = pltpu.make_async_copy(down, down_out, sems.at[10])
     down_copy.start()
     up_copy.wait()
     down_copy.wait()
@@ -198,21 +197,18 @@
 
 def load_weights(coords, slots, width, hidden):
     flat = [
-        slots[half][i][step].reshape(2 * RING, PIECE, hidden)
-        for step in range(3)
-        for half in range(2)
-        for i in range(3)
+        slots[i][step].reshape(RING * RING, PIECE, hidden) for step in range(3) for i in range(3)
     ]
     shape = jax.ShapeDtypeStruct((width, 2 * hidden), jnp.bfloat16)
     return pl.pallas_call(
         load_body,
         out_shape=(shape, shape),
-        in_specs=[IN_SMEM] + [IN_HBM] * 18,
+        in_specs=[IN_SMEM] + [IN_HBM] * 9,
         out_specs=(IN_HBM, IN_HBM),
         scratch_shapes=[
             pltpu.VMEM(shape.shape, shape.dtype),
             pltpu.VMEM(shape.shape, shape.dtype),
-            pltpu.SemaphoreType.DMA((20,)),
+            pltpu.SemaphoreType.DMA((11,)),
         ],
         compiler_params=pltpu.CompilerParams(vmem_limit_bytes=40 * MIB),
         cost_estimate=pl.CostEstimate(
@@ -236,28 +232,28 @@
     return pl.ds(pl.multiple_of(n * TILE, TILE), TILE)
 
 
-def gen_body(place_ref, u, low, adapt, *refs):
-    slots, (up_in, down_in, up_out, down_out, slope, mine, other) = refs[:6], refs[6:13]
-    up, down, last, act, sems, up_sems, down_sems = refs[13:]
+def gen_body(table, u_mine, u_other, adapt_in, adapt, *refs):
+    slots, (up_in, down_in, up_out, down_out, slope, low, mine, other) = refs[:3], refs[3:11]
+    up, down, last, u, act, sems, up_sems, down_sems = refs[11:]
     rows = mine.shape[0]
     tiles = up.shape[1] // TILE
     per_quarter = tiles // 2
     pieces = RING * RING
-    fetches = {}
-    for i in (0, 2, 1):
-        for half in range(2):
-            n = 2 * i + half
-            target = last.at[i, pl.ds(half * 2 * RING, 2 * RING)]
-            fetches[n] = pltpu.make_async_copy(slots[n], target, sems.at[n])
-    for n in (0, 1, 4, 5):
-        fetches[n].start()
+    fetches = [pltpu.make_async_copy(slots[i], last.at[i], sems.at[i]) for i in range(3)]
+    fetches[0].start()
+    fetches[2].start()
     each(tiles, lambda n: column_copy(up_in, up, up_sems, n).start(), 1)
-    for n in (2, 3):
-        fetches[n].start()
+    fetches[1].start()
     whole_down = pltpu.make_async_copy(down_in, down, down_sems.at[0])
     whole_down.start()
-    for n in (0, 1, 4, 5):
-        fetches[n].wait()
+    u[:rows] = u_mine[...]
+    u[rows:] = u_other[...]
+    low[...] = dot(u[...], adapt_in[...], NT).astype(low.dtype)
+    fetches[0].wait()
+    fetches[2].wait()
+
+    def spot(i, k):
+        return table[0, i * pieces + k], pl.multiple_of(table[1, i * pieces + k], 32)
 
     hidden = last.shape[3]
 
@@ -274,7 +270,7 @@
 
         def place(k, q=q, quarter_cols=quarter_cols):
             for i in (0, 2):
-                quarter, row = piece_place(place_ref, i, 3, k)
+                quarter, row = spot(i, k)
 
                 @pl.when(quarter == q)
                 def _(i=i, row=row):
@@ -284,27 +280,26 @@
                         rest = pl.ds(pl.multiple_of(row + PIECE, 32), REST)
                         up[rest, quarter_cols] = last[2, k, :REST]
 
-        each(pieces, place, 1)
+        each(pieces, place, 2)
         each(per_quarter, lambda n, q=q: hidden_tile(q * per_quarter + n), 1)
-    for n in (2, 3):
-        fetches[n].wait()
+    fetches[1].wait()
     whole_down.wait()
 
     def place_down(k):
         for i in (1, 2):
-            quarter, row = piece_place(place_ref, i, 3, k)
+            quarter, row = spot(i, k)
             cols = pl.ds(pl.multiple_of(quarter * hidden, 128), hidden)
             if i == 1:
                 down[pl.ds(row, PIECE), cols] = last[1, k]
             else:
                 down[pl.ds(pl.multiple_of(row + PIECE, 32), REST), cols] = last[2, k, REST:]
 
-    each(pieces, place_down, 1)
+    each(pieces, place_down, 4)
     for i in range(3):
 
         def store(k, i=i):
-            quarter, row = piece_place(place_ref, i, 3, k)
-            start_piece(i, last.at[i, k], quarter, row, up_out, down_out, sems.at[6 + i])
+            quarter, row = spot(i, k)
+            start_piece(i, last.at[i, k], quarter, row, up_out, down_out, sems.at[3 + i])
 
         each(pieces, store)
 
@@ -316,47 +311,47 @@
 
     each(down.shape[0] // TILE, width_tile, 1)
     for i in range(3):
-        wait_all(last.at[i], sems.at[6 + i])
-
-
-def gen_forward(coords, u, low, adapt, slots, up, down):
-    group, width = u.shape
+        wait_all(last.at[i], sems.at[3 + i])
+
+
+def gen_forward(table, u_mine, u_other, adapt_in, adapt, slots, up, down):
+    rows, width = u_mine.shape
     hidden = up.shape[1]
-    rows = group // 2
+    group = 2 * rows
     f32, bf16 = jnp.float32, jnp.bfloat16
     shape = jax.ShapeDtypeStruct((width, hidden), bf16)
-    last = [
-        slots[half][i][3].reshape(2 * RING, PIECE, hidden // 2) for i in range(3) for half in range(2)
-    ]
+    last = [slots[i][3].reshape(RING * RING, PIECE, hidden // 2) for i in range(3)]
     return pl.pallas_call(
         gen_body,
         out_shape=(
             shape,
             shape,
             jax.ShapeDtypeStruct((group, hidden), f32),
+            jax.ShapeDtypeStruct((group, adapt_in.shape[0]), bf16),
             jax.ShapeDtypeStruct((rows, width), f32),
             jax.ShapeDtypeStruct((rows, width), bf16),
         ),
-        in_specs=[IN_SMEM] + [IN_VMEM] * 3 + [IN_HBM] * 8,
-        out_specs=(IN_HBM, IN_HBM) + (IN_VMEM,) * 3,
+        in_specs=[IN_SMEM] + [IN_VMEM] * 4 + [IN_HBM] * 5,
+        out_specs=(IN_HBM, IN_HBM) + (IN_VMEM,) * 4,
         scratch_shapes=[
             pltpu.VMEM(shape.shape, bf16),
             pltpu.VMEM(shape.shape, bf16),
             pltpu.VMEM((3, RING * RING, PIECE, hidden // 2), bf16),
+            pltpu.VMEM((group, width), bf16),
             pltpu.VMEM((group, hidden), bf16),
-            pltpu.SemaphoreType.DMA((9,)),
+            pltpu.SemaphoreType.DMA((6,)),
             pltpu.SemaphoreType.DMA((hidden // TILE,)),
             pltpu.SemaphoreType.DMA((1,)),
         ],
-        input_output_aliases={10: 0, 11: 1},
-        compiler_params=pltpu.CompilerParams(vmem_limit_bytes=56 * MIB),
+        input_output_aliases={8: 0, 9: 1},
+        compiler_params=pltpu.CompilerParams(vmem_limit_bytes=57 * MIB),
         cost_estimate=pl.CostEstimate(
             flops=4 * group * width * hidden,
             bytes_accessed=50 * MIB,
             transcendentals=group * hidden,
         ),
         name="gen_forward",
-    )(coords, u, low, adapt, *last, up, down)
+    )(table, u_mine, u_other, adapt_in, adapt, *last, up, down)
 
 
 def score_body(
@@ -483,6 +478,50 @@
 
 
 STRIP = 16
+
+
+def embed_body(ends, steps, given, scale_ref, shift_ref, u_ref, mods_ref):
+    half = given.shape[1] // 2
+    place = lax.broadcasted_iota(jnp.int32, (1, half), 1).astype(jnp.float32)
+    frequency = jnp.exp(-math.log(10000.0) * place / half)
+    row = lax.broadcasted_iota(jnp.int32, (4, 1), 0)
+    column = jnp.where(
+        row < 2, jnp.where(row == 0, steps[0], steps[1]), jnp.where(row == 2, steps[2], steps[3])
+    )
+    phase = column * frequency
+    embed = jnp.concatenate([jnp.sin(phase), jnp.cos(phase)], axis=1)
+    scale = 1.0 + scale_ref[...] * embed
+    shift = shift_ref[...] * embed
+    mods_ref[0:2] = scale[2:4]
+    mods_ref[2:4] = shift[2:4]
+
+    def strip(n, carry):
+        rows = pl.ds(pl.multiple_of(n * STRIP, STRIP), STRIP)
+        in_last = n * STRIP + lax.broadcasted_iota(jnp.int32, (STRIP, 1), 0) >= ends[0]
+        u_ref[rows] = modulate(
+            given[rows],
+            jnp.where(in_last, scale[1:2], scale[0:1]),
+            jnp.where(in_last, shift[1:2], shift[0:1]),
+        )
+        return carry
+
+    lax.fori_loop(0, given.shape[0] // STRIP, strip, 0)
+
+
+def first_modulation(ends, steps, given, scale, shift):
+    width = given.shape[1]
+    return pl.pallas_call(
+        embed_body,
+        out_shape=(
+            jax.ShapeDtypeStruct(given.shape, given.dtype),
+            jax.ShapeDtypeStruct((4, width), jnp.float32),
+        ),
+        in_specs=[IN_SMEM] * 2 + [IN_VMEM] * 3,
+        out_specs=(IN_VMEM,) * 2,
+        compiler_params=pltpu.CompilerParams(vmem_limit_bytes=8 * MIB),
+        cost_estimate=pl.CostEstimate(flops=0, bytes_accessed=2 * MIB, transcendentals=0),
+        name="first_modulation",
+    )(ends, steps, given, scale.reshape(1, width), shift.reshape(1, width))
 
 
 def noise_body(ends, blends, given, noise, mine, other, mods, gate, latents_ref, noised_ref, u_ref):
@@ -592,38 +631,25 @@
     first_row = lax.axis_index(AXES) * shard_rows
     first_image = first_row // IMG_TOK
     last_image = (first_row + shard_rows - 1) // IMG_TOK
-    row_ids = first_row + jnp.arange(shard_rows, dtype=jnp.int32)
-    in_last = (row_ids >= last_image * IMG_TOK)[:, None]
-
     def two_steps(steps):
         return jnp.stack([steps[first_image], steps[last_image]])
-
-    def modulation(steps):
-        embed = embedding(two_steps(steps), width)
-        return 1.0 + modulation_scale[None, :] * embed, modulation_shift[None, :] * embed
-
-    def both_rows(mine):
-        return jnp.concatenate([mine, swap_cores(mine)], axis=0)
 
     def both_quarters(mine):
         theirs = lax.ppermute(mine, "xl", [(0, 1), (1, 0)])
         quarters = [jnp.where(xl == 0, mine, theirs), jnp.where(xl == 0, theirs, mine)]
         return jnp.concatenate(quarters, axis=1)
 
-    def prepare(given, gen_steps, score_steps):
-        gen_scale, gen_shift = modulation(gen_steps)
-        u_mine = modulate(
-            given,
-            jnp.where(in_last, gen_scale[1:], gen_scale[:1]),
-            jnp.where(in_last, gen_shift[1:], gen_shift[:1]),
-        )
-        u_gen = both_rows(u_mine)
-        low_gen = matmul(u_gen, gen_adapt_in).astype(bf16)
-        mods = jnp.concatenate(modulation(score_steps), axis=0)
-        blends = (two_steps(score_steps).astype(f32) + 0.5) / 1000.0
-        ends = (last_image * IMG_TOK - first_row).astype(jnp.int32).reshape(1)
-        place = [lax.axis_index("z"), lax.axis_index("y"), lax.axis_index("xh") * 2 + xl, 1 - 2 * core]
-        return u_gen, low_gen, mods, blends, ends, jnp.stack(place).astype(jnp.int32)
+    blends = (two_steps(score_steps).astype(f32) + 0.5) / 1000.0
+    ends = (last_image * IMG_TOK - first_row).astype(jnp.int32).reshape(1)
+    steps = jnp.concatenate([two_steps(gen_steps), two_steps(score_steps)]).astype(f32)
+    place = [lax.axis_index("z"), lax.axis_index("y"), lax.axis_index("xh") * 2 + xl, 1 - 2 * core]
+    coords = jnp.stack(place).astype(jnp.int32)
+    spots = [piece_place(coords, i, 3, jnp.arange(RING * RING, dtype=jnp.int32)) for i in range(3)]
+    table = jnp.stack([jnp.concatenate([spot[n] for spot in spots]) for n in range(2)])
+
+    def prepare(given):
+        u_mine, mods = first_modulation(ends, steps, given, modulation_scale, modulation_shift)
+        return u_mine, swap_cores(u_mine), mods
 
     down_rows = base_down.T
     slots, adapt_out, prepared = ring_slots(
@@ -634,15 +660,15 @@
         ],
         jnp.concatenate([gen_adapt_out, fake_adapt_out], axis=0),
         both_quarters,
-        (gen_input, gen_steps, score_steps),
+        (gen_input,),
         prepare,
     )
-    u_gen, low_gen, mods, blends, ends, coords = prepared
+    u_gen, u_gen_other, mods = prepared
     gen_out, fake_out = adapt_out[:rank], adapt_out[rank:]
     up_part, down_part = load_weights(coords, slots, width, hidden)
 
-    up_all, down_all, slope_gen, out_mine, out_other = gen_forward(
-        coords, u_gen, low_gen, gen_out, slots, up_part, down_part
+    up_all, down_all, slope_gen, low_gen, out_mine, out_other = gen_forward(
+        table, u_gen, u_gen_other, gen_adapt_in.T, gen_out, slots, up_part, down_part
     )
     gate = output_gate.reshape(1, width)
     latents, noised, u_score = add_noise(
@@ -668,9 +694,10 @@
         chips = total.reshape(-1, 2, width // 128, rank)
         return jnp.where(core == 0, chips[:, 0], chips[:, 1])
 
+    u_gen_group = jnp.concatenate([u_gen, u_gen_other], axis=0)
     u_score_group = jnp.concatenate([u_score, u_score_other], axis=0)
     in_grads = jnp.concatenate(
-        [in_grad(u_gen, mix[:, :rank]), in_grad(u_score_group, mix[:, rank:])], axis=2
+        [in_grad(u_gen_group, mix[:, :rank]), in_grad(u_score_group, mix[:, rank:])], axis=2
     )
     chips, in_rows = in_grads.shape[0], in_grads.shape[1]
     groups = chips // 2

time: 333 us -> 311 us (0.934)
  waiting for transfers between devices: 143 us -> 111 us
  local copies, waits for them, and re-layouts: 24.4 us -> 43.3 us
  other arithmetic: 19.2 us -> 7.9 us
  blocking collectives: 24.9 us -> 28.9 us
    ppermute x36 -> x27, waiting for transfers between devices: 131 us -> 98.5 us  [send(): return lax.ppermute(piece, AXES, chip_ring(RING_AXES[i][phase]))]
    dynamic_update_slice x0 -> x24, local copies, waits for them, and re-layouts: none -> 17 us  [gathered(): lax.dynamic_update_slice(buffer, piece, (step * rows, 0))]
    concatenate x7 -> x0, other arithmetic: 10.9 us -> none  [the longest x3 7.55 us: ring_slots(): pieces = [jnp.concatenate(held, axis=0) for held in ring(pieces, 1)]]
    unnamed x98 -> x62, local copies, waits for them, and re-layouts: 9.25 us -> 15.5 us
    all_to_all x1, blocking collectives: 24.9 us -> 28.9 us  [local(): received = lax.all_to_all(packed, CHIPS, 0, 0, tiled=True)]
    ppermute x36 -> x27, starting transfers between devices: 28.6 us -> 29.9 us  [send(): return lax.ppermute(piece, AXES, chip_ring(RING_AXES[i][phase]))]
  transfers between devices with their start and end apart: 43 -> 34, of which waited for: 28 -> 21; matrix products, arithmetic and copies ran while one was open for 8% -> 10% of each run, Pallas kernels for 7% -> 8%
where the time goes in v2:
time: 311 us; the launch traced here: 310 us
  waiting for transfers between devices  111 us (36%)
  Pallas kernels  85.9 us (28%)
  local copies, waits for them, and re-layouts  43.3 us (14%)
  starting transfers between devices  31 us (10%)
  blocking collectives  28.9 us (9%)
  other arithmetic  7.9 us (3%)
    ppermute x27, waiting for transfers between devices, send(): return lax.ppermute(piece, AXES, chip_ring(RING_AXES[i][phase]))  98.5 us
    ppermute x27, starting transfers between devices, send(): return lax.ppermute(piece, AXES, chip_ring(RING_AXES[i][phase]))  29.9 us
    all_to_all x1, blocking collectives, local(): received = lax.all_to_all(packed, CHIPS, 0, 0, tiled=True)  28.9 us
    pallas_call x1, Pallas kernels, gen_forward(): pl.pallas_call(gen_body, out_shape=(shape, shape, jax.ShapeDtypeStruct((g...  26.1 us
    pallas_call x1, Pallas kernels, load_weights(): pl.pallas_call(load_body, out_shape=(shape, shape), in_specs=[IN_SMEM] +...  22.1 us
    pallas_call x1, Pallas kernels, score_forward(): pl.pallas_call(score_body, out_shape=(jax.ShapeDtypeStruct((group, hidden...  20.5 us
    dynamic_update_slice x24, local copies, waits for them, and re-layouts, gathered(): lax.dynamic_update_slice(buffer, piece, (step * rows, 0))  17 us
    unnamed x62, local copies, waits for them, and re-layouts  15.5 us
  transfers between devices with their start and end apart: 34, of which 21 were waited for; matrix products, arithmetic and copies ran while one was open for 10% of the time, Pallas kernels for 8%

profile of v2, /device:TPU:0, one launch (start us, length us, event | category | flops | bytes accessed | tf_op | source)
XLA Modules:
  0.0 310.0 jit_solution(12107849281609430014)
XLA Ops:
  0.7 1.0 slice.85
  1.6 1.7 collective-permute-start.9
  3.4 0.9 slice.110
  4.3 2.0 collective-permute-start.16
  8.1 1.6 collective-permute-start
  9.7 1.0 dynamic_update_slice.80
  10.6 0.9 dynamic_update_slice.88
  11.6 0.9 dynamic_update_slice.72
  12.6 1.6 collective-permute-start.10
  14.2 1.9 collective-permute-start.17
  16.1 1.5 collective-permute-start.1
  19.7 1.3 collective-permute-start.11
  21.1 1.5 collective-permute-start.18
  25.9 4.0 %collective-permute-done.2 = bf16[64,1536]{1,0:T(8,128)(2,1)S(1)} collective-permute-done((bf16[64,1536]{1,0:T(8,128)(2,1)S(1)}, bf16[64,1536]{1,0:T(8,128)(2,1)S(1)}, u32[]{:S(2)}, u32[]{:S(2)}) %collective-permute-start.2) | collective-permute-done | bytes 196640 | tf_op jit(solution)/shard_map/ppermute | solution.py:68
  30.6 1.3 collective-permute-start.3
  32.6 2.0 collective-permute-start.19
  35.3 1.6 collective-permute-start.12
  36.9 1.3 dynamic_update_slice.76
  38.3 1.3 dynamic_update_slice.92
  39.6 1.3 dynamic_update_slice.84
  41.0 1.8 collective-permute-done.6
  42.8 1.1 broadcast_select_fusion.1
  44.1 1.1 collective-permute-start.4
  45.2 0.9 collective-permute-done.19
  46.1 2.3 collective-permute-start.20
  48.8 0.9 collective-permute-start.13
  49.8 1.0 pad_maximum_fusion.1
  50.7 1.2 constant_dynamic-update-slice_fusion.14
  51.9 1.2 constant_dynamic-update-slice_fusion.2
  53.1 4.4 %collective-permute-done.4 = bf16[256,1536]{1,0:T(8,128)(2,1)S(1)} collective-permute-done((bf16[256,1536]{1,0:T(8,128)(2,1)}, bf16[256,1536]{1,0:T(8,128)(2,1)S(1)}, u32[]{:S(2)}, u32[]{:S(2)}) %collective-permute-start.4) | collective-permute-done | bytes 786464 | tf_op jit(solution)/shard_map/ppermute | solution.py:68
  57.5 1.2 constant_dynamic-update-slice_fusion.8
  58.7 2.7 collective-permute-done.20
  62.7 8.1 %collective-permute-done.5 = bf16[256,1536]{1,0:T(8,128)(2,1)S(1)} collective-permute-done((bf16[256,1536]{1,0:T(8,128)(2,1)S(1)}, bf16[256,1536]{1,0:T(8,128)(2,1)S(1)}, u32[]{:S(2)}, u32[]{:S(2)}) %collective-permute-start.5) | collective-permute-done | bytes 786464 | tf_op jit(solution)/shard_map/ppermute | solution.py:68
  70.8 4.7 %collective-permute-done.14 = bf16[256,1536]{1,0:T(8,128)(2,1)S(1)} collective-permute-done((bf16[256,1536]{1,0:T(8,128)(2,1)S(1)}, bf16[256,1536]{1,0:T(8,128)(2,1)S(1)}, u32[]{:S(2)}, u32[]{:S(2)}) %collective-permute-start.14) | collective-permute-done | bytes 786464 | tf_op jit(solution)/shard_map/ppermute | solution.py:68
  75.5 1.4 collective-permute-start.15
  77.0 1.6 copy-done.2
  78.7 1.7 copy-done
  80.4 35.1 %collective-permute-done.7 = bf16[1024,1536]{1,0:T(8,128)(2,1)} collective-permute-done((bf16[1024,1536]{1,0:T(8,128)(2,1)S(1)}, bf16[1024,1536]{1,0:T(8,128)(2,1)}, u32[]{:S(2)}, u32[]{:S(2)}) %collective-permute-start.7) | collective-permute-done | bytes 3145760 | tf_op jit(solution)/shard_map/ppermute | solution.py:68
  115.5 2.5 collective-permute-start.24
  118.7 2.6 add_convert_fusion.1.steps
  121.3 1.1 copy-done.8
  122.4 1.7 first_modulation.1
  124.9 2.0 collective-permute-done.23.u_other
  127.7 26.6 %collective-permute-done.8 = bf16[1024,1536]{1,0:T(8,128)(2,1)} collective-permute-done((bf16[1024,1536]{1,0:T(8,128)(2,1)}, bf16[1024,1536]{1,0:T(8,128)(2,1)}, u32[]{:S(2)}, u32[]{:S(2)}) %collective-permute-start.8) | collective-permute-done | bytes 3145760 | tf_op jit(solution)/shard_map/ppermute | solution.py:68
  154.3 2.5 collective-permute-start.25
  157.7 2.1 fusion.28
  159.8 1.9 copy-done.1
  161.7 1.9 copy-done.3
  163.6 22.1 %load_weights.1 = (bf16[3072,3072]{1,0:T(8,128)(2,1)}, bf16[3072,3072]{1,0:T(8,128)(2,1)}) custom-call(s32[4]{0:T(128)S(1)} %pad_add_fusion.1.place_ref, bf16[16,64,1536]{2,1,0:T(8,128)(2,1)S(1)} %bitcast.40, bf16[16,64,1536]{2,1,0:T(8,128)(2,1)S(1)} %bitcast.41, bf16[16,64,1536]{2,1,0:T(8,128)(2,1)S(1)} %bitcast.42, bf16[16,64,1536]{2,1,0:T(8,128)(2,1)} %bitcast.17.refs_3_, ...), custom_call_target="tpu_custom_call" | custom-call | bytes 150994944 | tf_op jit(solution)/shard_map/load_weights/pallas_call | solution.py:203
  185.6 7.5 %collective-permute-done.25 = bf16[1024,1536]{1,0:T(8,128)(2,1)} collective-permute-done((bf16[1024,1536]{1,0:T(8,128)(2,1)}, bf16[1024,1536]{1,0:T(8,128)(2,1)}, u32[]{:S(2)}, u32[]{:S(2)}) %collective-permute-start.25) | collective-permute-done | bytes 3145760 | tf_op jit(solution)/shard_map/ppermute | solution.py:68
  193.1 2.5 collective-permute-done.27
  195.6 26.1 %gen_forward.1 = (bf16[3072,3072]{1,0:T(8,128)(2,1)}, bf16[3072,3072]{1,0:T(8,128)(2,1)}, f32[192,3072]{1,0:T(8,128)}, bf16[192,64]{1,0:T(8,128)(2,1)}, f32[96,3072]{1,0:T(8,128)}, /*index=5*/bf16[96,3072]{1,0:T(8,128)(2,1)}) custom-call(s32[2,48]{1,0:T(2,128)} %pad_add_fusion.table, ...), custom_call_target="tpu_custom_call", output_to_operand_aliasing={{0}: (8, {}), {1}: (9, {})} | custom-call | flops 7247757312 | bytes 52428800 | tf_op jit(solution)/shard_map/gen_forward/pallas_call | solution.py:324
  221.9 1.3 fusion.25.blends
  224.1 1.3 copy-done.13
  225.4 1.9 add_noise.1
  227.5 1.9 collective-permute-done.30.u_other
  230.2 20.5 %score_forward.1 = (f32[192,3072]{1,0:T(8,128)}, bf16[192,64]{1,0:T(8,128)(2,1)}, f32[96,3072]{1,0:T(8,128)}, f32[96,3072]{1,0:T(8,128)}, bf16[192,3072]{1,0:T(8,128)(2,1)}) custom-call(bf16[96,3072]{1,0:T(8,128)(2,1)} %copy-done.16, bf16[96,3072]{1,0:T(8,128)(2,1)} %copy-done.25, bf16[64,3072]{1,0:T(8,128)(2,1)} %bitcast.53, ...), custom_call_target="tpu_custom_call" | custom-call | flops 10871635968 | bytes 52428800 | tf_op jit(solution)/shard_map/score_forward/pallas_call | solution.py:398
  250.9 2.9 collective-permute-done.31.others
  253.8 1.3 copy-done.14
  255.1 1.3 copy-done.15
  256.4 1.7 cotangents.1
  258.2 2.7 collective-permute-done.32.cots_other
  260.9 11.9 %backward.1 = (bf16[2,64,3072]{2,1,0:T(8,128)(2,1)S(1)}, f32[2,192,64]{2,1,0:T(8,128)S(1)}) custom-call(bf16[192,3072]{1,0:T(8,128)(2,1)S(1)} %get-tuple-element.60.cots_mine, bf16[192,3072]{1,0:T(8,128)(2,1)S(1)} %collective-permute-done.32.cots_other, f32[192,3072]{1,0:T(8,128)S(1)} %copy-done.5, f32[192,3072]{1,0:T(8,128)S(1)} %copy-done.6, ...), custom_call_target="tpu_custom_call" | custom-call | flops 7247757312 | bytes 31457280 | tf_op jit(solution)/shard_map/backward/pallas_call | solution.py:459
  279.0 28.9 %all_to_all.5 = bf16[64,72,128]{2,1,0:T(8,128)(2,1)S(1)} all-to-all(bf16[64,72,128]{2,1,0:T(8,128)(2,1)S(1)} %pad_maximum_fusion), channel_id=1, replica_groups=mesh['z'=4,'y'=4,'xh'=2,'xl'=2,'core'=2] {'z','y','xh','xl'}, dimensions={0} | all-to-all | bytes 2359296 | tf_op jit(solution)/shard_map/all_to_all | solution.py:709
  (140 shorter events, 25.1 us)
Async XLA Ops:
  0.6 11.9 %copy-start.27 = (bf16[64,1536]{1,0:T(8,128)(2,1)S(1)}, bf16[64,1536]{1,0:T(8,128)(2,1)}, u32[]{:S(2)}) copy-start(bf16[64,1536]{1,0:T(8,128)(2,1)} %param.22) | copy-start | bytes 589828
  0.6 11.9 %copy-start.28 = (bf16[64,1536]{1,0:T(8,128)(2,1)S(1)}, bf16[64,1536]{1,0:T(8,128)(2,1)}, u32[]{:S(2)}) copy-start(bf16[64,1536]{1,0:T(8,128)(2,1)} %param.20) | copy-start | bytes 589828
  1.6 10.9 %collective-permute-start.9 = (bf16[64,1536]{1,0:T(8,128)(2,1)S(1)}, bf16[64,1536]{1,0:T(8,128)(2,1)S(1)}, u32[]{:S(2)}, u32[]{:S(2)}) collective-permute-start(bf16[64,1536]{1,0:T(8,128)(2,1)S(1)} %slice.85), channel_id=1, source_target_pairs={{0,8},{1,25},{2,10},{3,27},{4,12},{5,29},{6,14},{7,31},{8,16},{9,1... | collective-permute-start | bytes 589832 | tf_op jit(solution)/shard_map/ppermute | solution.py:68
  4.3 9.9 %collective-permute-start.16 = (bf16[64,1536]{1,0:T(8,128)(2,1)S(1)}, bf16[64,1536]{1,0:T(8,128)(2,1)S(1)}, u32[]{:S(2)}, u32[]{:S(2)}) collective-permute-start(bf16[64,1536]{1,0:T(8,128)(2,1)S(1)} %slice.110), channel_id=1, source_target_pairs={{0,32},{1,97},{2,34},{3,99},{4,36},{5,101},{6,38},{7,103},{8,40},{... | collective-permute-start | bytes 589832 | tf_op jit(solution)/shard_map/ppermute | solution.py:68
  8.1 8.0 %collective-permute-start = (bf16[64,1536]{1,0:T(8,128)(2,1)S(1)}, bf16[64,1536]{1,0:T(8,128)(2,1)S(1)}, u32[]{:S(2)}, u32[]{:S(2)}) collective-permute-start(bf16[64,1536]{1,0:T(8,128)(2,1)S(1)} %pad_maximum_fusion.3), channel_id=1, source_target_pairs={{0,2},{1,7},{2,4},{3,1},{4,6},{5,3},{6,0},{7,5},{8,10},{9,15},{10,... | collective-permute-start | bytes 589832 | tf_op jit(solution)/shard_map/ppermute | solution.py:68
  12.6 7.2 %collective-permute-start.10 = (bf16[64,1536]{1,0:T(8,128)(2,1)S(1)}, bf16[64,1536]{1,0:T(8,128)(2,1)S(1)}, u32[]{:S(2)}, u32[]{:S(2)}) collective-permute-start(bf16[64,1536]{1,0:T(8,128)(2,1)S(1)} %collective-permute-done.9), channel_id=1, source_target_pairs={{0,8},{1,25},{2,10},{3,27},{4,12},{5,29},{6,14},{7,31},{8,16},{9,1... | collective-permute-start | bytes 589832 | tf_op jit(solution)/shard_map/ppermute | solution.py:68
  14.2 6.9 %collective-permute-start.17 = (bf16[64,1536]{1,0:T(8,128)(2,1)S(1)}, bf16[64,1536]{1,0:T(8,128)(2,1)S(1)}, u32[]{:S(2)}, u32[]{:S(2)}) collective-permute-start(bf16[64,1536]{1,0:T(8,128)(2,1)S(1)} %collective-permute-done.16), channel_id=1, source_target_pairs={{0,32},{1,97},{2,34},{3,99},{4,36},{5,101},{6,38},{7,103},{8,40},{... | collective-permute-start | bytes 589832 | tf_op jit(solution)/shard_map/ppermute | solution.py:68
  16.1 6.9 %collective-permute-start.1 = (bf16[64,1536]{1,0:T(8,128)(2,1)S(1)}, bf16[64,1536]{1,0:T(8,128)(2,1)S(1)}, u32[]{:S(2)}, u32[]{:S(2)}) collective-permute-start(bf16[64,1536]{1,0:T(8,128)(2,1)S(1)} %collective-permute-done), channel_id=1, source_target_pairs={{0,2},{1,7},{2,4},{3,1},{4,6},{5,3},{6,0},{7,5},{8,10},{9,15},{10,... | collective-permute-start | bytes 589832 | tf_op jit(solution)/shard_map/ppermute | solution.py:68
  19.7 14.9 %collective-permute-start.11 = (bf16[64,1536]{1,0:T(8,128)(2,1)S(1)}, bf16[64,1536]{1,0:T(8,128)(2,1)S(1)}, u32[]{:S(2)}, u32[]{:S(2)}) collective-permute-start(bf16[64,1536]{1,0:T(8,128)(2,1)S(1)} %collective-permute-done.10), channel_id=1, source_target_pairs={{0,8},{1,25},{2,10},{3,27},{4,12},{5,29},{6,14},{7,31},{8,16},{9,1... | collective-permute-start | bytes 589832 | tf_op jit(solution)/shard_map/ppermute | solution.py:68
  21.1 10.8 %collective-permute-start.18 = (bf16[64,1536]{1,0:T(8,128)(2,1)S(1)}, bf16[64,1536]{1,0:T(8,128)(2,1)S(1)}, u32[]{:S(2)}, u32[]{:S(2)}) collective-permute-start(bf16[64,1536]{1,0:T(8,128)(2,1)S(1)} %collective-permute-done.17), channel_id=1, source_target_pairs={{0,32},{1,97},{2,34},{3,99},{4,36},{5,101},{6,38},{7,103},{8,40},{... | collective-permute-start | bytes 589832 | tf_op jit(solution)/shard_map/ppermute | solution.py:68
  23.0 6.9 %collective-permute-start.2 = (bf16[64,1536]{1,0:T(8,128)(2,1)S(1)}, bf16[64,1536]{1,0:T(8,128)(2,1)S(1)}, u32[]{:S(2)}, u32[]{:S(2)}) collective-permute-start(bf16[64,1536]{1,0:T(8,128)(2,1)S(1)} %collective-permute-done.1), channel_id=1, source_target_pairs={{0,2},{1,7},{2,4},{3,1},{4,6},{5,3},{6,0},{7,5},{8,10},{9,15},{10,... | collective-permute-start | bytes 589832 | tf_op jit(solution)/shard_map/ppermute | solution.py:68
  30.6 12.2 %collective-permute-start.6 = (bf16[128,1536]{1,0:T(8,128)(2,1)S(1)}, bf16[128,1536]{1,0:T(8,128)(2,1)}, u32[]{:S(2)}, u32[]{:S(2)}) collective-permute-start(bf16[128,1536]{1,0:T(8,128)(2,1)S(1)} %pad_maximum_fusion.2), channel_id=1, source_target_pairs={{0,2},{2,0},{1,3},{3,1},{4,6},{6,4},{5,7},{7,5},{8,10},{10,8},{9,1... | collective-permute-start | bytes 1179656 | tf_op jit(solution)/shard_map/ppermute | solution.py:638
  30.6 13.5 %collective-permute-start.3 = (bf16[256,1536]{1,0:T(8,128)(2,1)}, bf16[256,1536]{1,0:T(8,128)(2,1)}, u32[]{:S(2)}, u32[]{:S(2)}) collective-permute-start(bf16[256,1536]{1,0:T(8,128)(2,1)} %constant_dynamic-update-slice_fusion.15), channel_id=1, source_target_pairs={{0,8},{1,25},{2,10},{3,27},{4,12},{5,29},{6,14},{7,31},{8,16},{9,1... | collective-permute-start | bytes 2359304 | tf_op jit(solution)/shard_map/ppermute | solution.py:68
  32.6 13.5 %collective-permute-start.19 = (bf16[256,1536]{1,0:T(8,128)(2,1)}, bf16[256,1536]{1,0:T(8,128)(2,1)}, u32[]{:S(2)}, u32[]{:S(2)}) collective-permute-start(bf16[256,1536]{1,0:T(8,128)(2,1)} %constant_dynamic-update-slice_fusion.3), channel_id=1, source_target_pairs={{0,2},{1,7},{2,4},{3,1},{4,6},{5,3},{6,0},{7,5},{8,10},{9,15},{10,... | collective-permute-start | bytes 2359304 | tf_op jit(solution)/shard_map/ppermute | solution.py:68
  35.3 13.5 %collective-permute-start.12 = (bf16[256,1536]{1,0:T(8,128)(2,1)}, bf16[256,1536]{1,0:T(8,128)(2,1)}, u32[]{:S(2)}, u32[]{:S(2)}) collective-permute-start(bf16[256,1536]{1,0:T(8,128)(2,1)} %constant_dynamic-update-slice_fusion.9), channel_id=1, source_target_pairs={{0,32},{1,97},{2,34},{3,99},{4,36},{5,101},{6,38},{7,103},{8,40},{... | collective-permute-start | bytes 2359304 | tf_op jit(solution)/shard_map/ppermute | solution.py:68
  44.1 13.4 %collective-permute-start.4 = (bf16[256,1536]{1,0:T(8,128)(2,1)}, bf16[256,1536]{1,0:T(8,128)(2,1)S(1)}, u32[]{:S(2)}, u32[]{:S(2)}) collective-permute-start(bf16[256,1536]{1,0:T(8,128)(2,1)} %collective-permute-done.3), channel_id=1, source_target_pairs={{0,8},{1,25},{2,10},{3,27},{4,12},{5,29},{6,14},{7,31},{8,16},{9,1... | collective-permute-start | bytes 2359304 | tf_op jit(solution)/shard_map/ppermute | solution.py:68
  46.1 15.3 %collective-permute-start.20 = (bf16[256,1536]{1,0:T(8,128)(2,1)}, bf16[256,1536]{1,0:T(8,128)(2,1)S(1)}, u32[]{:S(2)}, u32[]{:S(2)}) collective-permute-start(bf16[256,1536]{1,0:T(8,128)(2,1)} %collective-permute-done.19), channel_id=1, source_target_pairs={{0,2},{1,7},{2,4},{3,1},{4,6},{5,3},{6,0},{7,5},{8,10},{9,15},{10,... | collective-permute-start | bytes 2359304 | tf_op jit(solution)/shard_map/ppermute | solution.py:68
  48.8 13.4 %collective-permute-start.13 = (bf16[256,1536]{1,0:T(8,128)(2,1)}, bf16[256,1536]{1,0:T(8,128)(2,1)S(1)}, u32[]{:S(2)}, u32[]{:S(2)}) collective-permute-start(bf16[256,1536]{1,0:T(8,128)(2,1)} %collective-permute-done.12), channel_id=1, source_target_pairs={{0,32},{1,97},{2,34},{3,99},{4,36},{5,101},{6,38},{7,103},{8,40},{... | collective-permute-start | bytes 2359304 | tf_op jit(solution)/shard_map/ppermute | solution.py:68
  57.5 13.2 %collective-permute-start.5 = (bf16[256,1536]{1,0:T(8,128)(2,1)S(1)}, bf16[256,1536]{1,0:T(8,128)(2,1)S(1)}, u32[]{:S(2)}, u32[]{:S(2)}) collective-permute-start(bf16[256,1536]{1,0:T(8,128)(2,1)S(1)} %collective-permute-done.4), channel_id=1, source_target_pairs={{0,8},{1,25},{2,10},{3,27},{4,12},{5,29},{6,14},{7,31},{8,16},{9,1... | collective-permute-start | bytes 2359304 | tf_op jit(solution)/shard_map/ppermute | solution.py:68
  61.4 17.2 %collective-permute-start.21 = (bf16[256,1536]{1,0:T(8,128)(2,1)S(1)}, bf16[256,1536]{1,0:T(8,128)(2,1)S(1)}, u32[]{:S(2)}, u32[]{:S(2)}) collective-permute-start(bf16[256,1536]{1,0:T(8,128)(2,1)S(1)} %collective-permute-done.20), channel_id=1, source_target_pairs={{0,2},{1,7},{2,4},{3,1},{4,6},{5,3},{6,0},{7,5},{8,10},{9,15},{10,... | collective-permute-start | bytes 2359304 | tf_op jit(solution)/shard_map/ppermute | solution.py:68
  62.2 13.2 %collective-permute-start.14 = (bf16[256,1536]{1,0:T(8,128)(2,1)S(1)}, bf16[256,1536]{1,0:T(8,128)(2,1)S(1)}, u32[]{:S(2)}, u32[]{:S(2)}) collective-permute-start(bf16[256,1536]{1,0:T(8,128)(2,1)S(1)} %collective-permute-done.13), channel_id=1, source_target_pairs={{0,32},{1,97},{2,34},{3,99},{4,36},{5,101},{6,38},{7,103},{8,40},{... | collective-permute-start | bytes 2359304 | tf_op jit(solution)/shard_map/ppermute | solution.py:68
  62.6 55.4 %copy-start.29 = (s32[12]{0:T(128)S(1)}, s32[12]{0:T(128)}, u32[]{:S(2)}) copy-start(s32[12]{0:T(128)} %param.15) | copy-start | bytes 148
  62.6 55.4 %copy-start.30 = (s32[12]{0:T(128)S(1)}, s32[12]{0:T(128)}, u32[]{:S(2)}) copy-start(s32[12]{0:T(128)} %param.16) | copy-start | bytes 148
  62.6 58.7 %copy-start.21 = (f32[3072]{0:T(1024)S(1)}, f32[3072]{0:T(1024)}, u32[]{:S(2)}) copy-start(f32[3072]{0:T(1024)} %param.23) | copy-start | bytes 36868
  62.7 58.7 %copy-start.22 = (f32[3072]{0:T(1024)S(1)}, f32[3072]{0:T(1024)}, u32[]{:S(2)}) copy-start(f32[3072]{0:T(1024)} %param.24) | copy-start | bytes 36868
  75.5 40.0 %collective-permute-start.15 = (bf16[1024,1536]{1,0:T(8,128)(2,1)S(1)}, bf16[1024,1536]{1,0:T(8,128)(2,1)}, u32[]{:S(2)}, u32[]{:S(2)}) collective-permute-start(bf16[1024,1536]{1,0:T(8,128)(2,1)S(1)} %constant_dynamic-update-slice_fusion.6), channel_id=1, source_target_pairs={{0,2},{1,7},{2,4},{3,1},{4,6},{5,3},{6,0},{7,5},{8,10},{9,15},{10,... | collective-permute-start | bytes 9437192 | tf_op jit(solution)/shard_map/ppermute | solution.py:68
  76.9 38.6 %collective-permute-start.7 = (bf16[1024,1536]{1,0:T(8,128)(2,1)S(1)}, bf16[1024,1536]{1,0:T(8,128)(2,1)}, u32[]{:S(2)}, u32[]{:S(2)}) collective-permute-start(bf16[1024,1536]{1,0:T(8,128)(2,1)S(1)} %constant_dynamic-update-slice_fusion.12), channel_id=1, source_target_pairs={{0,32},{1,97},{2,34},{3,99},{4,36},{5,101},{6,38},{7,103},{8,40},{... | collective-permute-start | bytes 9437192 | tf_op jit(solution)/shard_map/ppermute | solution.py:68
  76.9 1.6 copy-start.2
  78.6 39.4 %collective-permute-start.22 = (bf16[1024,1536]{1,0:T(8,128)(2,1)S(1)}, bf16[1024,1536]{1,0:T(8,128)(2,1)}, u32[]{:S(2)}, u32[]{:S(2)}) collective-permute-start(bf16[1024,1536]{1,0:T(8,128)(2,1)S(1)} %constant_dynamic-update-slice_fusion), channel_id=1, source_target_pairs={{0,8},{1,25},{2,10},{3,27},{4,12},{5,29},{6,14},{7,31},{8,16},{9,1... | collective-permute-start | bytes 9437192 | tf_op jit(solution)/shard_map/ppermute | solution.py:68
  78.7 1.7 copy-start
  115.5 38.8 %collective-permute-start.8 = (bf16[1024,1536]{1,0:T(8,128)(2,1)}, bf16[1024,1536]{1,0:T(8,128)(2,1)}, u32[]{:S(2)}, u32[]{:S(2)}) collective-permute-start(bf16[1024,1536]{1,0:T(8,128)(2,1)} %collective-permute-done.7), channel_id=1, source_target_pairs={{0,32},{1,97},{2,34},{3,99},{4,36},{5,101},{6,38},{7,103},{8,40},{... | collective-permute-start | bytes 9437192 | tf_op jit(solution)/shard_map/ppermute | solution.py:68
  115.5 38.8 %collective-permute-start.24 = (bf16[1024,1536]{1,0:T(8,128)(2,1)}, bf16[1024,1536]{1,0:T(8,128)(2,1)}, u32[]{:S(2)}, u32[]{:S(2)}) collective-permute-start(bf16[1024,1536]{1,0:T(8,128)(2,1)} %collective-permute-done.15), channel_id=1, source_target_pairs={{0,2},{1,7},{2,4},{3,1},{4,6},{5,3},{6,0},{7,5},{8,10},{9,15},{10,... | collective-permute-start | bytes 9437192 | tf_op jit(solution)/shard_map/ppermute | solution.py:68
  118.0 38.8 %collective-permute-start.26 = (bf16[1024,1536]{1,0:T(8,128)(2,1)}, bf16[1024,1536]{1,0:T(8,128)(2,1)}, u32[]{:S(2)}, u32[]{:S(2)}) collective-permute-start(bf16[1024,1536]{1,0:T(8,128)(2,1)} %collective-permute-done.22), channel_id=1, source_target_pairs={{0,8},{1,25},{2,10},{3,27},{4,12},{5,29},{6,14},{7,31},{8,16},{9,1... | collective-permute-start | bytes 9437192 | tf_op jit(solution)/shard_map/ppermute | solution.py:68
  121.3 1.1 copy-start.8
  124.1 0.8 copy-start.10
  124.9 2.0 collective-permute-start.23
  126.9 0.8 copy-start.23
  154.3 38.8 %collective-permute-start.25 = (bf16[1024,1536]{1,0:T(8,128)(2,1)}, bf16[1024,1536]{1,0:T(8,128)(2,1)}, u32[]{:S(2)}, u32[]{:S(2)}) collective-permute-start(bf16[1024,1536]{1,0:T(8,128)(2,1)} %collective-permute-done.24), channel_id=1, source_target_pairs={{0,2},{1,7},{2,4},{3,1},{4,6},{5,3},{6,0},{7,5},{8,10},{9,15},{10,... | collective-permute-start | bytes 9437192 | tf_op jit(solution)/shard_map/ppermute | solution.py:68
  156.8 38.8 %collective-permute-start.27 = (bf16[1024,1536]{1,0:T(8,128)(2,1)}, bf16[1024,1536]{1,0:T(8,128)(2,1)}, u32[]{:S(2)}, u32[]{:S(2)}) collective-permute-start(bf16[1024,1536]{1,0:T(8,128)(2,1)} %collective-permute-done.26), channel_id=1, source_target_pairs={{0,8},{1,25},{2,10},{3,27},{4,12},{5,29},{6,14},{7,31},{8,16},{9,1... | collective-permute-start | bytes 9437192 | tf_op jit(solution)/shard_map/ppermute | solution.py:68
  156.8 38.8 %collective-permute-start.28 = (bf16[1024,1536]{1,0:T(8,128)(2,1)}, bf16[1024,1536]{1,0:T(8,128)(2,1)}, u32[]{:S(2)}, u32[]{:S(2)}) collective-permute-start(bf16[1024,1536]{1,0:T(8,128)(2,1)} %collective-permute-done.8), channel_id=1, source_target_pairs={{0,32},{1,97},{2,34},{3,99},{4,36},{5,101},{6,38},{7,103},{8,40},{... | collective-permute-start | bytes 9437192 | tf_op jit(solution)/shard_map/ppermute | solution.py:68
  159.8 1.9 copy-start.1
  161.7 1.9 copy-start.3
  195.6 28.5 %copy-start.7 = (bf16[96,3072]{1,0:T(8,128)(2,1)S(1)}, bf16[96,3072]{1,0:T(8,128)(2,1)}, u32[]{:S(2)}) copy-start(bf16[96,3072]{1,0:T(8,128)(2,1)} %noise.3) | copy-start | bytes 1769476
  195.6 28.5 %copy-start.9 = (bf16[96,3072]{1,0:T(8,128)(2,1)S(1)}, bf16[96,3072]{1,0:T(8,128)(2,1)}, u32[]{:S(2)}) copy-start(bf16[96,3072]{1,0:T(8,128)(2,1)} %given.2) | copy-start | bytes 1769476
  195.6 28.5 %copy-start.20 = (f32[3072]{0:T(1024)S(1)}, f32[3072]{0:T(1024)}, u32[]{:S(2)}) copy-start(f32[3072]{0:T(1024)} %param.25) | copy-start | bytes 36868
  221.8 2.3 collective-permute-start.29
  224.1 1.3 copy-start.13
  227.3 2.1 copy-start.16
  227.3 2.1 collective-permute-start.30
  230.1 30.8 %copy-start.12 = (bf16[64,3072]{1,0:T(8,128)(2,1)S(1)}, bf16[64,3072]{1,0:T(8,128)(2,1)}, u32[]{:S(2)}) copy-start(bf16[64,3072]{1,0:T(8,128)(2,1)} %get-tuple-element.67.adapt_out.fake_out) | copy-start | bytes 1179652
  250.7 3.1 %collective-permute-start.31 = (bf16[192,3072]{1,0:T(8,128)(2,1)}, bf16[192,3072]{1,0:T(8,128)(2,1)S(1)}, u32[]{:S(2)}, u32[]{:S(2)}) collective-permute-start(bf16[192,3072]{1,0:T(8,128)(2,1)} %get-tuple-element.56), channel_id=1, source_target_pairs={{0,1},{1,0},{2,3},{3,2},{4,5},{5,4},{6,7},{7,6},{8,9},{9,8},{10,11... | collective-permute-start | bytes 3538952 | tf_op jit(solution)/shard_map/ppermute | solution.py:49
  253.8 1.3 copy-start.14
  255.1 1.3 copy-start.15
  256.4 4.5 %copy-start.4 = (bf16[64,3072]{1,0:T(8,128)(2,1)S(1)}, bf16[64,3072]{1,0:T(8,128)(2,1)}, u32[]{:S(2)}) copy-start(bf16[64,3072]{1,0:T(8,128)(2,1)} %get-tuple-element.68.adapt.gen_out) | copy-start | bytes 1179652
  256.4 4.5 %copy-start.5 = (f32[192,3072]{1,0:T(8,128)S(1)}, f32[192,3072]{1,0:T(8,128)}, u32[]{:S(2)}) copy-start(f32[192,3072]{1,0:T(8,128)} %get-tuple-element.61.slope_gen) | copy-start | bytes 7077892
  256.4 4.5 %copy-start.6 = (f32[192,3072]{1,0:T(8,128)S(1)}, f32[192,3072]{1,0:T(8,128)}, u32[]{:S(2)}) copy-start(f32[192,3072]{1,0:T(8,128)} %get-tuple-element.62.slope_fake) | copy-start | bytes 7077892
  256.4 4.6 %copy-start.18 = (bf16[192,64]{1,0:T(8,128)(2,1)S(1)}, bf16[192,64]{1,0:T(8,128)(2,1)}, u32[]{:S(2)}) copy-start(bf16[192,64]{1,0:T(8,128)(2,1)} %get-tuple-element.63.low_gen) | copy-start | bytes 73732
  256.4 4.6 %copy-start.19 = (bf16[192,64]{1,0:T(8,128)(2,1)S(1)}, bf16[192,64]{1,0:T(8,128)(2,1)}, u32[]{:S(2)}) copy-start(bf16[192,64]{1,0:T(8,128)(2,1)} %get-tuple-element.64.low_fake) | copy-start | bytes 73732
  258.1 2.8 collective-permute-start.32
  273.0 2.2 collective-permute-start.33
  274.0 1.4 copy-start.11
  274.6 1.1 copy-start.24
  276.3 1.1 copy-start.17
  276.3 1.2 copy-start.26
  (1 other events, 0.8 us)

commit v3 on v2

--- a/solution.py
+++ b/solution.py
@@ -104,6 +104,8 @@
 PIECE = 64
 REST = SHARD - PIECE
 TILE = 512
+WINDOW = 3
+BLOCK = 8 * SHARD
 MIB = 2**20
 ANYWHERE = pl.BlockSpec(memory_space=pl.ANY)
 IN_VMEM = pl.BlockSpec(memory_space=pltpu.VMEM)
@@ -159,20 +161,21 @@
     pltpu.make_async_copy(ref, ref, sem).wait()
 
 
-def start_piece(i, source, quarter, row, up, down, sem):
+def start_piece(i, source, quarter, row, up, down, sem, matrices=(0, 1)):
     hidden = source.shape[1]
     cols = pl.ds(pl.multiple_of(quarter * hidden, 128), hidden)
     if i < 2:
         target = (up, down)[i].at[pl.ds(row, PIECE), cols]
         pltpu.make_async_copy(source, target, sem).start()
     else:
-        for n, matrix in enumerate((up, down)):
+        for n in matrices:
             rows = pl.ds(pl.multiple_of(row + PIECE, 32), REST)
-            pltpu.make_async_copy(source.at[pl.ds(n * REST, REST)], matrix.at[rows, cols], sem).start()
-
-
-def load_body(place_ref, *refs):
-    slots, (up_out, down_out, up, down, sems) = refs[:9], refs[9:]
+            target = (up, down)[n].at[rows, cols]
+            pltpu.make_async_copy(source.at[pl.ds(n * REST, REST)], target, sem).start()
+
+
+def load_body(place_ref, table, u_mine, u_other, adapt_in, adapt, *refs):
+    slots, (up_out, down_out, partial, low, up, down, u, sems) = refs[:9], refs[9:]
     for n, slot in enumerate(slots):
         step, i = n // 3, n % 3
 
@@ -181,6 +184,19 @@
             start_piece(i, slot.at[k], quarter, pl.multiple_of(row, 32), up, down, sems.at[n])
 
         each(RING * RING, one)
+    rows, pieces = u_mine.shape[0], RING * RING
+    u[:rows] = u_mine[...]
+    u[rows:] = u_other[...]
+    low[...] = dot(u[...], adapt_in[...], NT).astype(low.dtype)
+    hidden = up.shape[1] // 2
+
+    def clear(k):
+        for i, first, count in ((0, 0, PIECE), (2, PIECE, REST)):
+            place = pl.ds(pl.multiple_of(table[1, i * pieces + k] + first, 32), count)
+            cols = pl.ds(pl.multiple_of(table[0, i * pieces + k] * hidden, 128), hidden)
+            up[place, cols] = jnp.zeros((count, hidden), up.dtype)
+
+    each(pieces, clear, 2)
     for n, slot in enumerate(slots):
         if n % 3 != 1:
             wait_all(slot, sems.at[n])
@@ -191,31 +207,46 @@
             wait_all(slot, sems.at[n])
     down_copy = pltpu.make_async_copy(down, down_out, sems.at[10])
     down_copy.start()
+
+    def hidden_tile(n):
+        cols = tile_at(n)
+        partial[:, cols] = dot(u[...], up[:, cols]) + dot(low[...], adapt[:, cols])
+
+    each(up.shape[1] // TILE, hidden_tile, 1)
     up_copy.wait()
     down_copy.wait()
 
 
-def load_weights(coords, slots, width, hidden):
+def load_weights(coords, table, u_mine, u_other, adapt_in, adapt, slots):
+    rows, width = u_mine.shape
+    group, rank, hidden = 2 * rows, adapt_in.shape[0], adapt.shape[1]
+    f32, bf16 = jnp.float32, jnp.bfloat16
     flat = [
-        slots[i][step].reshape(RING * RING, PIECE, hidden) for step in range(3) for i in range(3)
+        slots[i][step].reshape(RING * RING, PIECE, hidden // 2) for step in range(3) for i in range(3)
     ]
-    shape = jax.ShapeDtypeStruct((width, 2 * hidden), jnp.bfloat16)
+    shape = jax.ShapeDtypeStruct((width, hidden), bf16)
     return pl.pallas_call(
         load_body,
-        out_shape=(shape, shape),
-        in_specs=[IN_SMEM] + [IN_HBM] * 9,
-        out_specs=(IN_HBM, IN_HBM),
+        out_shape=(
+            shape,
+            shape,
+            jax.ShapeDtypeStruct((group, hidden), f32),
+            jax.ShapeDtypeStruct((group, rank), bf16),
+        ),
+        in_specs=[IN_SMEM] * 2 + [IN_VMEM] * 4 + [IN_HBM] * 9,
+        out_specs=(IN_HBM, IN_HBM, IN_VMEM, IN_VMEM),
         scratch_shapes=[
-            pltpu.VMEM(shape.shape, shape.dtype),
-            pltpu.VMEM(shape.shape, shape.dtype),
+            pltpu.VMEM(shape.shape, bf16),
+            pltpu.VMEM(shape.shape, bf16),
+            pltpu.VMEM((group, width), bf16),
             pltpu.SemaphoreType.DMA((11,)),
         ],
-        compiler_params=pltpu.CompilerParams(vmem_limit_bytes=40 * MIB),
+        compiler_params=pltpu.CompilerParams(vmem_limit_bytes=46 * MIB),
         cost_estimate=pl.CostEstimate(
-            flops=0, bytes_accessed=8 * width * hidden * 4, transcendentals=0
+            flops=2 * group * width * hidden, bytes_accessed=16 * width * hidden, transcendentals=0
         ),
         name="load_weights",
-    )(coords, *flat)
+    )(coords, table, u_mine, u_other, adapt_in, adapt, *flat)
 
 
 def column_copy(source, target, sems, n):
@@ -228,96 +259,108 @@
     return pltpu.make_async_copy(source.at[rows], target.at[rows], sems.at[n])
 
 
+def start_ahead(place, segments):
+    ahead = place + WINDOW
+    for count, copy in segments:
+
+        @pl.when((ahead >= 0) & (ahead < count))
+        def _(ahead=ahead, copy=copy):
+            copy(ahead).start()
+
+        ahead = ahead - count
+
+
 def tile_at(n):
     return pl.ds(pl.multiple_of(n * TILE, TILE), TILE)
 
 
-def gen_body(table, u_mine, u_other, adapt_in, adapt, *refs):
-    slots, (up_in, down_in, up_out, down_out, slope, low, mine, other) = refs[:3], refs[3:11]
-    up, down, last, u, act, sems, up_sems, down_sems = refs[11:]
+def gen_body(table, u_columns, partial, *refs):
+    slots, (up_in, down_in, up_out, down_out, slope, mine, other) = refs[:3], refs[3:10]
+    down, last, u_first, u_rest, up_rest, act, sems, down_sems = refs[10:]
     rows = mine.shape[0]
-    tiles = up.shape[1] // TILE
-    per_quarter = tiles // 2
     pieces = RING * RING
+    hidden = last.shape[3]
     fetches = [pltpu.make_async_copy(slots[i], last.at[i], sems.at[i]) for i in range(3)]
-    fetches[0].start()
-    fetches[2].start()
-    each(tiles, lambda n: column_copy(up_in, up, up_sems, n).start(), 1)
-    fetches[1].start()
-    whole_down = pltpu.make_async_copy(down_in, down, down_sems.at[0])
-    whole_down.start()
-    u[:rows] = u_mine[...]
-    u[rows:] = u_other[...]
-    low[...] = dot(u[...], adapt_in[...], NT).astype(low.dtype)
+
+    def down_copy(n):
+        part = pl.ds(pl.multiple_of(n * BLOCK, BLOCK), BLOCK)
+        return pltpu.make_async_copy(down_in.at[part], down.at[part], down_sems.at[n])
+
+    blocks = down.shape[0] // BLOCK
+    for i in (0, 2, 1):
+        fetches[i].start()
+    for n in range(blocks):
+        down_copy(n).start()
+
+    def spot(i, k):
+        return table[0, i * pieces + k], pl.multiple_of(table[1, i * pieces + k], 32)
+
+    for k in range(pieces):
+        u_first[k * PIECE : (k + 1) * PIECE] = u_columns[pl.ds(spot(0, k)[1], PIECE), :]
+        at = pl.ds(k // 2 * REST, REST)
+        u_rest[k % 2, at] = u_columns[pl.ds(pl.multiple_of(spot(2, k)[1] + PIECE, 32), REST), :]
     fetches[0].wait()
     fetches[2].wait()
-
-    def spot(i, k):
-        return table[0, i * pieces + k], pl.multiple_of(table[1, i * pieces + k], 32)
-
-    hidden = last.shape[3]
-
-    def hidden_tile(n):
-        cols = tile_at(n)
-        pre = dot(u[...], up[:, cols]) + dot(low[...], adapt[:, cols])
+    for k in range(pieces):
+        up_rest[k % 2, pl.ds(k // 2 * REST, REST)] = last[2, k, :REST]
+    first_quarter, rest_quarter = table[0, 0], table[0, 2 * pieces]
+
+    def hidden_tile(quarter, n, with_first):
+        part = tile_at(n)
+        cols = pl.ds(pl.multiple_of(quarter * hidden + n * TILE, TILE), TILE)
+        side = jnp.where(quarter == rest_quarter, 0, 1)
+        pre = partial[:, cols] + dot(u_rest[side], up_rest[side, :, part], TN)
+        if with_first:
+            pre = pre + dot(u_first[...], last[0, :, :, part].reshape(pieces * PIECE, TILE), TN)
         value, slope[:, cols] = gelu_and_slope(pre)
         act[:, cols] = value.astype(act.dtype)
 
-    for q in range(2):
-        quarter_cols = pl.ds(q * hidden, hidden)
-        for n in range(q * per_quarter, (q + 1) * per_quarter):
-            column_copy(up_in, up, up_sems, n).wait()
-
-        def place(k, q=q, quarter_cols=quarter_cols):
-            for i in (0, 2):
+    tiles = hidden // TILE
+    each(tiles, lambda n: hidden_tile(first_quarter, n, True), 1)
+    each(tiles, lambda n: hidden_tile(1 - first_quarter, n, False), 1)
+
+    def store(i, matrices):
+        def one(k):
+            quarter, row = spot(i, k)
+            start_piece(i, last.at[i, k], quarter, row, up_out, down_out, sems.at[3 + i], matrices)
+
+        each(pieces, one)
+
+    fetches[1].wait()
+    store(0, (0,))
+    store(2, (0,))
+
+    for n in range(blocks):
+        down_copy(n).wait()
+        if n == blocks - 1:
+            store(1, (1,))
+            store(2, (1,))
+
+        def place_down(k, n=n):
+            for i in (1, 2):
                 quarter, row = spot(i, k)
-
-                @pl.when(quarter == q)
-                def _(i=i, row=row):
-                    if i == 0:
-                        up[pl.ds(row, PIECE), quarter_cols] = last[0, k]
+                cols = pl.ds(pl.multiple_of(quarter * hidden, 128), hidden)
+
+                @pl.when(table[2, i * pieces + k] == n)
+                def _(i=i, row=row, cols=cols):
+                    if i == 1:
+                        down[pl.ds(row, PIECE), cols] = last[1, k]
                     else:
-                        rest = pl.ds(pl.multiple_of(row + PIECE, 32), REST)
-                        up[rest, quarter_cols] = last[2, k, :REST]
-
-        each(pieces, place, 2)
-        each(per_quarter, lambda n, q=q: hidden_tile(q * per_quarter + n), 1)
-    fetches[1].wait()
-    whole_down.wait()
-
-    def place_down(k):
-        for i in (1, 2):
-            quarter, row = spot(i, k)
-            cols = pl.ds(pl.multiple_of(quarter * hidden, 128), hidden)
-            if i == 1:
-                down[pl.ds(row, PIECE), cols] = last[1, k]
-            else:
-                down[pl.ds(pl.multiple_of(row + PIECE, 32), REST), cols] = last[2, k, REST:]
-
-    each(pieces, place_down, 4)
-    for i in range(3):
-
-        def store(k, i=i):
-            quarter, row = spot(i, k)
-            start_piece(i, last.at[i, k], quarter, row, up_out, down_out, sems.at[3 + i])
-
-        each(pieces, store)
-
-    def width_tile(n):
-        cols = tile_at(n)
+                        down[pl.ds(pl.multiple_of(row + PIECE, 32), REST), cols] = last[2, k, REST:]
+
+        each(pieces, place_down, 2)
+        cols = pl.ds(n * BLOCK, BLOCK)
         out = dot(act[...], down[cols, :], NT)
         mine[:, cols] = out[:rows]
         other[:, cols] = out[rows:].astype(other.dtype)
-
-    each(down.shape[0] // TILE, width_tile, 1)
     for i in range(3):
         wait_all(last.at[i], sems.at[3 + i])
 
 
-def gen_forward(table, u_mine, u_other, adapt_in, adapt, slots, up, down):
-    rows, width = u_mine.shape
+def gen_forward(table, u_columns, partial, slots, up, down):
+    width, group = u_columns.shape
     hidden = up.shape[1]
-    group = 2 * rows
+    rows, rest = group // 2, RING * RING * REST // 2
     f32, bf16 = jnp.float32, jnp.bfloat16
     shape = jax.ShapeDtypeStruct((width, hidden), bf16)
     last = [slots[i][3].reshape(RING * RING, PIECE, hidden // 2) for i in range(3)]
@@ -327,31 +370,30 @@
             shape,
             shape,
             jax.ShapeDtypeStruct((group, hidden), f32),
-            jax.ShapeDtypeStruct((group, adapt_in.shape[0]), bf16),
             jax.ShapeDtypeStruct((rows, width), f32),
             jax.ShapeDtypeStruct((rows, width), bf16),
         ),
-        in_specs=[IN_SMEM] + [IN_VMEM] * 4 + [IN_HBM] * 5,
-        out_specs=(IN_HBM, IN_HBM) + (IN_VMEM,) * 4,
+        in_specs=[IN_SMEM] + [IN_VMEM] * 2 + [IN_HBM] * 5,
+        out_specs=(IN_HBM, IN_HBM) + (IN_VMEM,) * 3,
         scratch_shapes=[
             pltpu.VMEM(shape.shape, bf16),
-            pltpu.VMEM(shape.shape, bf16),
             pltpu.VMEM((3, RING * RING, PIECE, hidden // 2), bf16),
-            pltpu.VMEM((group, width), bf16),
+            pltpu.VMEM((RING * RING * PIECE, group), bf16),
+            pltpu.VMEM((2, rest, group), bf16),
+            pltpu.VMEM((2, rest, hidden // 2), bf16),
             pltpu.VMEM((group, hidden), bf16),
             pltpu.SemaphoreType.DMA((6,)),
-            pltpu.SemaphoreType.DMA((hidden // TILE,)),
-            pltpu.SemaphoreType.DMA((1,)),
+            pltpu.SemaphoreType.DMA((width // BLOCK,)),
         ],
-        input_output_aliases={8: 0, 9: 1},
-        compiler_params=pltpu.CompilerParams(vmem_limit_bytes=57 * MIB),
+        input_output_aliases={6: 0, 7: 1},
+        compiler_params=pltpu.CompilerParams(vmem_limit_bytes=46 * MIB),
         cost_estimate=pl.CostEstimate(
-            flops=4 * group * width * hidden,
-            bytes_accessed=50 * MIB,
+            flops=3 * group * width * hidden,
+            bytes_accessed=40 * MIB,
             transcendentals=group * hidden,
         ),
         name="gen_forward",
-    )(table, u_mine, u_other, adapt_in, adapt, *last, up, down)
+    )(table, u_columns, partial, *last, up, down)
 
 
 def score_body(
@@ -359,8 +401,12 @@
 ):
     u, act, up, down, up_sems, down_sems = scratch
     hidden_tiles, width_tiles = up.shape[1] // TILE, down.shape[0] // TILE
-    each(hidden_tiles, lambda n: column_copy(up_in, up, up_sems, n).start(), 1)
-    each(width_tiles, lambda n: row_copy(down_in, down, down_sems, n).start(), 1)
+    segments = (
+        (hidden_tiles, functools.partial(column_copy, up_in, up, up_sems)),
+        (width_tiles, functools.partial(row_copy, down_in, down, down_sems)),
+    )
+    for n in range(WINDOW):
+        column_copy(up_in, up, up_sems, n).start()
     rows = u_mine.shape[0]
     group = 2 * rows
     u[:rows] = u_mine[...]
@@ -369,6 +415,7 @@
 
     def hidden_tile(n):
         column_copy(up_in, up, up_sems, n).wait()
+        start_ahead(n, segments)
         cols = tile_at(n)
         pre_real = dot(u[...], up[:, cols])
         pre_fake = pre_real + dot(low[...], adapt_out[:, cols])
@@ -380,6 +427,7 @@
 
     def width_tile(n):
         row_copy(down_in, down, down_sems, n).wait()
+        start_ahead(hidden_tiles + n, segments)
         cols = tile_at(n)
         out = dot(act[...], down[cols, :], NT)
         real[:, cols] = out[:rows]
@@ -429,7 +477,8 @@
 ):
     cots, down, sems = scratch
     tiles = down.shape[1] // TILE
-    each(tiles, lambda n: column_copy(down_in, down, sems, n).start(), 1)
+    for n in range(WINDOW):
+        column_copy(down_in, down, sems, n).start()
     group = cots_mine.shape[0]
     rows = group // 2
     for i in range(2):
@@ -439,6 +488,7 @@
 
     def hidden_tile(n):
         column_copy(down_in, down, sems, n).wait()
+        start_ahead(n, ((tiles, functools.partial(column_copy, down_in, down, sems)),))
         cols = tile_at(n)
         raw = dot(cots[...], down[:, cols])
         back_gen = (raw[:group] * slope_gen[:, cols]).astype(jnp.bfloat16)
@@ -645,11 +695,14 @@
     place = [lax.axis_index("z"), lax.axis_index("y"), lax.axis_index("xh") * 2 + xl, 1 - 2 * core]
     coords = jnp.stack(place).astype(jnp.int32)
     spots = [piece_place(coords, i, 3, jnp.arange(RING * RING, dtype=jnp.int32)) for i in range(3)]
-    table = jnp.stack([jnp.concatenate([spot[n] for spot in spots]) for n in range(2)])
+    quarters, rows = [jnp.concatenate([spot[n] for spot in spots]) for n in range(2)]
+    table = jnp.stack([quarters, rows, rows // BLOCK])
 
     def prepare(given):
         u_mine, mods = first_modulation(ends, steps, given, modulation_scale, modulation_shift)
-        return u_mine, swap_cores(u_mine), mods
+        u_other = swap_cores(u_mine)
+        u_columns = jnp.concatenate([u_mine, u_other], axis=0).T
+        return u_mine, u_other, u_columns, mods, blends, coords, table
 
     down_rows = base_down.T
     slots, adapt_out, prepared = ring_slots(
@@ -663,12 +716,13 @@
         (gen_input,),
         prepare,
     )
-    u_gen, u_gen_other, mods = prepared
+    u_gen, u_gen_other, u_columns, mods, blends, coords, table = prepared
     gen_out, fake_out = adapt_out[:rank], adapt_out[rank:]
-    up_part, down_part = load_weights(coords, slots, width, hidden)
-
-    up_all, down_all, slope_gen, low_gen, out_mine, out_other = gen_forward(
-        table, u_gen, u_gen_other, gen_adapt_in.T, gen_out, slots, up_part, down_part
+    up_part, down_part, partial, low_gen = load_weights(
+        coords, table, u_gen, u_gen_other, gen_adapt_in.T, gen_out, slots
+    )
+    up_all, down_all, slope_gen, out_mine, out_other = gen_forward(
+        table, u_columns, partial, slots, up_part, down_part
     )
     gate = output_gate.reshape(1, width)
     latents, noised, u_score = add_noise(

time: 311 us -> 304 us (0.977)
  local copies, waits for them, and re-layouts: 43.3 us -> 37.8 us
  Pallas kernels: 85.9 us -> 81.6 us
    unnamed x62 -> x50, local copies, waits for them, and re-layouts: 15.5 us -> 6.77 us
    pallas_call x1, Pallas kernels: 26.1 us -> 19.8 us  [gen_forward(): pl.pallas_call(gen_body, out_shape=(shape, shape, jax.ShapeDtypeStruct((g...]
  transfers between devices with their start and end apart: 34 -> 34, of which waited for: 21 -> 23; matrix products, arithmetic and copies ran while one was open for 10% -> 12% of each run, Pallas kernels for 8% -> 8%
where the time goes in v3:
time: 304 us; the launch traced here: 303 us
  waiting for transfers between devices  113 us (37%)
  Pallas kernels  81.6 us (27%)
  local copies, waits for them, and re-layouts  37.8 us (12%)
  starting transfers between devices  31.1 us (10%)
  blocking collectives  26.3 us (9%)
  other arithmetic  9.57 us (3%)
    ppermute x27, waiting for transfers between devices, send(): return lax.ppermute(piece, AXES, chip_ring(RING_AXES[i][phase]))  102 us
    ppermute x27, starting transfers between devices, send(): return lax.ppermute(piece, AXES, chip_ring(RING_AXES[i][phase]))  30 us
    all_to_all x1, blocking collectives, local(): received = lax.all_to_all(packed, CHIPS, 0, 0, tiled=True)  26.3 us
    pallas_call x1, Pallas kernels, load_weights(): pl.pallas_call(load_body, out_shape=(shape, shape, jax.ShapeDtypeStruct((...  22.6 us
    pallas_call x1, Pallas kernels, score_forward(): pl.pallas_call(score_body, out_shape=(jax.ShapeDtypeStruct((group, hidden...  21.2 us
    pallas_call x1, Pallas kernels, gen_forward(): pl.pallas_call(gen_body, out_shape=(shape, shape, jax.ShapeDtypeStruct((g...  19.8 us
    dynamic_update_slice x24, local copies, waits for them, and re-layouts, gathered(): lax.dynamic_update_slice(buffer, piece, (step * rows, 0))  17 us
    pallas_call x1, Pallas kernels, backward(): pl.pallas_call(back_body, out_shape=(jax.ShapeDtypeStruct((2, rank, hidde...  11.9 us
  transfers between devices with their start and end apart: 34, of which 23 were waited for; matrix products, arithmetic and copies ran while one was open for 12% of the time, Pallas kernels for 8%

profile of v3, /device:TPU:0, one launch (start us, length us, event | category | flops | bytes accessed | tf_op | source)
XLA Modules:
  0.0 302.7 jit_solution(9858247933137622827)
XLA Ops:
  0.7 1.0 slice.85
  1.6 1.7 collective-permute-start.9
  3.4 0.9 slice.110
  4.3 2.0 collective-permute-start.16
  6.3 0.9 slice.109
  8.1 1.6 collective-permute-start
  9.7 1.0 dynamic_update_slice.80
  10.6 0.9 dynamic_update_slice.88
  11.6 1.0 dynamic_update_slice.72
  12.6 1.6 collective-permute-start.10
  14.2 1.9 collective-permute-start.17
  16.2 1.5 collective-permute-start.1
  19.8 1.3 collective-permute-start.11
  21.1 1.5 collective-permute-start.18
  25.9 4.0 %collective-permute-done.2 = bf16[64,1536]{1,0:T(8,128)(2,1)S(1)} collective-permute-done((bf16[64,1536]{1,0:T(8,128)(2,1)S(1)}, bf16[64,1536]{1,0:T(8,128)(2,1)S(1)}, u32[]{:S(2)}, u32[]{:S(2)}) %collective-permute-start.2) | collective-permute-done | bytes 196640 | tf_op jit(solution)/shard_map/ppermute | solution.py:68
  30.6 1.3 collective-permute-start.3
  32.6 2.0 collective-permute-start.19
  35.3 1.6 collective-permute-start.12
  36.9 1.3 dynamic_update_slice.76
  38.3 1.3 dynamic_update_slice.92
  39.6 1.3 dynamic_update_slice.84
  41.0 1.8 collective-permute-done.6
  42.8 1.1 broadcast_select_fusion.1
  44.1 1.1 collective-permute-start.4
  45.2 0.9 collective-permute-done.19
  46.1 2.3 collective-permute-start.20
  48.8 0.9 collective-permute-start.13
  49.8 1.0 pad_maximum_fusion.1
  50.8 1.2 constant_dynamic-update-slice_fusion.14
  52.0 1.2 constant_dynamic-update-slice_fusion.2
  53.2 4.4 %collective-permute-done.4 = bf16[256,1536]{1,0:T(8,128)(2,1)S(1)} collective-permute-done((bf16[256,1536]{1,0:T(8,128)(2,1)}, bf16[256,1536]{1,0:T(8,128)(2,1)S(1)}, u32[]{:S(2)}, u32[]{:S(2)}) %collective-permute-start.4) | collective-permute-done | bytes 786464 | tf_op jit(solution)/shard_map/ppermute | solution.py:68
  57.5 1.2 constant_dynamic-update-slice_fusion.8
  58.7 2.7 collective-permute-done.20
  62.7 8.1 %collective-permute-done.5 = bf16[256,1536]{1,0:T(8,128)(2,1)S(1)} collective-permute-done((bf16[256,1536]{1,0:T(8,128)(2,1)S(1)}, bf16[256,1536]{1,0:T(8,128)(2,1)S(1)}, u32[]{:S(2)}, u32[]{:S(2)}) %collective-permute-start.5) | collective-permute-done | bytes 786464 | tf_op jit(solution)/shard_map/ppermute | solution.py:68
  70.8 4.6 %collective-permute-done.14 = bf16[256,1536]{1,0:T(8,128)(2,1)S(1)} collective-permute-done((bf16[256,1536]{1,0:T(8,128)(2,1)S(1)}, bf16[256,1536]{1,0:T(8,128)(2,1)S(1)}, u32[]{:S(2)}, u32[]{:S(2)}) %collective-permute-start.14) | collective-permute-done | bytes 786464 | tf_op jit(solution)/shard_map/ppermute | solution.py:68
  75.5 1.5 collective-permute-start.15
  77.1 38.4 %collective-permute-done.7 = bf16[1024,1536]{1,0:T(8,128)(2,1)} collective-permute-done((bf16[1024,1536]{1,0:T(8,128)(2,1)S(1)}, bf16[1024,1536]{1,0:T(8,128)(2,1)}, u32[]{:S(2)}, u32[]{:S(2)}) %collective-permute-start.7) | collective-permute-done | bytes 3145760 | tf_op jit(solution)/shard_map/ppermute | solution.py:68
  115.6 2.5 collective-permute-start.24
  118.9 1.3 fusion.25.blends
  120.2 2.6 add_convert_fusion.steps
  122.9 1.1 copy-done.2
  123.9 2.5 first_modulation.1
  126.8 2.2 copy.35
  129.0 2.2 copy.36
  131.3 2.1 maximum_bitcast_fusion.u_columns
  133.4 20.9 %collective-permute-done.8 = bf16[1024,1536]{1,0:T(8,128)(2,1)} collective-permute-done((bf16[1024,1536]{1,0:T(8,128)(2,1)}, bf16[1024,1536]{1,0:T(8,128)(2,1)}, u32[]{:S(2)}, u32[]{:S(2)}) %collective-permute-start.8) | collective-permute-done | bytes 3145760 | tf_op jit(solution)/shard_map/ppermute | solution.py:68
  154.4 2.4 collective-permute-start.26
  157.8 22.6 %load_weights.1 = (bf16[3072,3072]{1,0:T(8,128)(2,1)}, bf16[3072,3072]{1,0:T(8,128)(2,1)}, f32[192,3072]{1,0:T(8,128)S(1)}, bf16[192,64]{1,0:T(8,128)(2,1)S(1)}) custom-call(s32[4]{0:T(128)S(1)} %pad_add_fusion.1.place_ref, s32[3,48]{1,0:T(4,128)S(1)} %pad_add_fusion.table, bf16[96,3072]{1,0:T(8,128)(2,1)} %get-tuple-element.51.u_mine, ...), custom_call_target="tpu_custom_call" | custom-call | flops 3623878656 | bytes 150994944 | tf_op jit(solution)/shard_map/load_weights/pallas_call | solution.py:228
  180.4 12.7 %collective-permute-done.26 = bf16[1024,1536]{1,0:T(8,128)(2,1)S(1)} collective-permute-done((bf16[1024,1536]{1,0:T(8,128)(2,1)}, bf16[1024,1536]{1,0:T(8,128)(2,1)S(1)}, u32[]{:S(2)}, u32[]{:S(2)}) %collective-permute-start.26) | collective-permute-done | bytes 3145760 | tf_op jit(solution)/shard_map/ppermute | solution.py:68
  193.1 2.5 collective-permute-done.27
  195.7 1.5 copy-done.17
  197.3 19.8 %gen_forward.1 = (bf16[3072,3072]{1,0:T(8,128)(2,1)}, bf16[3072,3072]{1,0:T(8,128)(2,1)}, f32[192,3072]{1,0:T(8,128)S(1)}, f32[96,3072]{1,0:T(8,128)S(1)}, bf16[96,3072]{1,0:T(8,128)(2,1)S(1)}) custom-call(s32[3,48]{1,0:T(4,128)S(1)} %pad_add_fusion.table, ...), custom_call_target="tpu_custom_call", output_to_operand_aliasing={{0}: (6, {}), {1}: (7, {})} | custom-call | flops 5435817984 | bytes 41943040 | tf_op jit(solution)/shard_map/gen_forward/pallas_call | solution.py:367
  217.1 2.0 collective-permute-done.29.other
  219.1 1.9 add_noise.1
  221.5 1.9 collective-permute-done.30.u_other
  224.2 21.2 %score_forward.1 = (f32[192,3072]{1,0:T(8,128)}, bf16[192,64]{1,0:T(8,128)(2,1)}, f32[96,3072]{1,0:T(8,128)}, f32[96,3072]{1,0:T(8,128)}, bf16[192,3072]{1,0:T(8,128)(2,1)}) custom-call(bf16[96,3072]{1,0:T(8,128)(2,1)} %copy-done.7, bf16[96,3072]{1,0:T(8,128)(2,1)} %copy-done.19, bf16[64,3072]{1,0:T(8,128)(2,1)} %bitcast.63, ...), custom_call_target="tpu_custom_call" | custom-call | flops 10871635968 | bytes 52428800 | tf_op jit(solution)/shard_map/score_forward/pallas_call | solution.py:446
  245.6 2.9 collective-permute-done.31.others
  248.5 1.3 copy-done.5
  249.8 1.3 copy-done.6
  251.1 1.7 cotangents.1
  252.9 2.7 collective-permute-done.32.cots_other
  255.6 11.9 %backward.1 = (bf16[2,64,3072]{2,1,0:T(8,128)(2,1)S(1)}, f32[2,192,64]{2,1,0:T(8,128)S(1)}) custom-call(bf16[192,3072]{1,0:T(8,128)(2,1)S(1)} %get-tuple-element.70.cots_mine, bf16[192,3072]{1,0:T(8,128)(2,1)S(1)} %collective-permute-done.32.cots_other, f32[192,3072]{1,0:T(8,128)S(1)} %get-tuple-element.71.slope_gen, f32[192,3072]{1,0:T(8,128)S(1)} %copy-done, ...), custom_call_target="tpu_custom_call" | custom-call | flops 7247757312 | bytes 31457280 | tf_op jit(solution)/shard_map/backward/pallas_call | solution.py:509
  269.8 1.8 fusion
  274.3 26.3 %all_to_all.5 = bf16[64,72,128]{2,1,0:T(8,128)(2,1)S(1)} all-to-all(bf16[64,72,128]{2,1,0:T(8,128)(2,1)S(1)} %pad_maximum_fusion), channel_id=1, replica_groups=mesh['z'=4,'y'=4,'xh'=2,'xl'=2,'core'=2] {'z','y','xh','xl'}, dimensions={0} | all-to-all | bytes 2359296 | tf_op jit(solution)/shard_map/all_to_all | solution.py:763
  (132 shorter events, 21.4 us)
Async XLA Ops:
  0.6 11.9 %copy-start.21 = (bf16[64,1536]{1,0:T(8,128)(2,1)S(1)}, bf16[64,1536]{1,0:T(8,128)(2,1)}, u32[]{:S(2)}) copy-start(bf16[64,1536]{1,0:T(8,128)(2,1)} %param.22) | copy-start | bytes 589828
  0.6 11.9 %copy-start.22 = (bf16[64,1536]{1,0:T(8,128)(2,1)S(1)}, bf16[64,1536]{1,0:T(8,128)(2,1)}, u32[]{:S(2)}) copy-start(bf16[64,1536]{1,0:T(8,128)(2,1)} %param.20) | copy-start | bytes 589828
  1.6 10.9 %collective-permute-start.9 = (bf16[64,1536]{1,0:T(8,128)(2,1)S(1)}, bf16[64,1536]{1,0:T(8,128)(2,1)S(1)}, u32[]{:S(2)}, u32[]{:S(2)}) collective-permute-start(bf16[64,1536]{1,0:T(8,128)(2,1)S(1)} %slice.85), channel_id=1, source_target_pairs={{0,8},{1,25},{2,10},{3,27},{4,12},{5,29},{6,14},{7,31},{8,16},{9,1... | collective-permute-start | bytes 589832 | tf_op jit(solution)/shard_map/ppermute | solution.py:68
  4.3 9.9 %collective-permute-start.16 = (bf16[64,1536]{1,0:T(8,128)(2,1)S(1)}, bf16[64,1536]{1,0:T(8,128)(2,1)S(1)}, u32[]{:S(2)}, u32[]{:S(2)}) collective-permute-start(bf16[64,1536]{1,0:T(8,128)(2,1)S(1)} %slice.110), channel_id=1, source_target_pairs={{0,32},{1,97},{2,34},{3,99},{4,36},{5,101},{6,38},{7,103},{8,40},{... | collective-permute-start | bytes 589832 | tf_op jit(solution)/shard_map/ppermute | solution.py:68
  8.1 8.0 %collective-permute-start = (bf16[64,1536]{1,0:T(8,128)(2,1)S(1)}, bf16[64,1536]{1,0:T(8,128)(2,1)S(1)}, u32[]{:S(2)}, u32[]{:S(2)}) collective-permute-start(bf16[64,1536]{1,0:T(8,128)(2,1)S(1)} %pad_maximum_fusion.3), channel_id=1, source_target_pairs={{0,2},{1,7},{2,4},{3,1},{4,6},{5,3},{6,0},{7,5},{8,10},{9,15},{10,... | collective-permute-start | bytes 589832 | tf_op jit(solution)/shard_map/ppermute | solution.py:68
  12.6 7.2 %collective-permute-start.10 = (bf16[64,1536]{1,0:T(8,128)(2,1)S(1)}, bf16[64,1536]{1,0:T(8,128)(2,1)S(1)}, u32[]{:S(2)}, u32[]{:S(2)}) collective-permute-start(bf16[64,1536]{1,0:T(8,128)(2,1)S(1)} %collective-permute-done.9), channel_id=1, source_target_pairs={{0,8},{1,25},{2,10},{3,27},{4,12},{5,29},{6,14},{7,31},{8,16},{9,1... | collective-permute-start | bytes 589832 | tf_op jit(solution)/shard_map/ppermute | solution.py:68
  14.2 6.9 %collective-permute-start.17 = (bf16[64,1536]{1,0:T(8,128)(2,1)S(1)}, bf16[64,1536]{1,0:T(8,128)(2,1)S(1)}, u32[]{:S(2)}, u32[]{:S(2)}) collective-permute-start(bf16[64,1536]{1,0:T(8,128)(2,1)S(1)} %collective-permute-done.16), channel_id=1, source_target_pairs={{0,32},{1,97},{2,34},{3,99},{4,36},{5,101},{6,38},{7,103},{8,40},{... | collective-permute-start | bytes 589832 | tf_op jit(solution)/shard_map/ppermute | solution.py:68
  16.2 6.9 %collective-permute-start.1 = (bf16[64,1536]{1,0:T(8,128)(2,1)S(1)}, bf16[64,1536]{1,0:T(8,128)(2,1)S(1)}, u32[]{:S(2)}, u32[]{:S(2)}) collective-permute-start(bf16[64,1536]{1,0:T(8,128)(2,1)S(1)} %collective-permute-done), channel_id=1, source_target_pairs={{0,2},{1,7},{2,4},{3,1},{4,6},{5,3},{6,0},{7,5},{8,10},{9,15},{10,... | collective-permute-start | bytes 589832 | tf_op jit(solution)/shard_map/ppermute | solution.py:68
  19.8 14.9 %collective-permute-start.11 = (bf16[64,1536]{1,0:T(8,128)(2,1)S(1)}, bf16[64,1536]{1,0:T(8,128)(2,1)S(1)}, u32[]{:S(2)}, u32[]{:S(2)}) collective-permute-start(bf16[64,1536]{1,0:T(8,128)(2,1)S(1)} %collective-permute-done.10), channel_id=1, source_target_pairs={{0,8},{1,25},{2,10},{3,27},{4,12},{5,29},{6,14},{7,31},{8,16},{9,1... | collective-permute-start | bytes 589832 | tf_op jit(solution)/shard_map/ppermute | solution.py:68
  21.1 10.8 %collective-permute-start.18 = (bf16[64,1536]{1,0:T(8,128)(2,1)S(1)}, bf16[64,1536]{1,0:T(8,128)(2,1)S(1)}, u32[]{:S(2)}, u32[]{:S(2)}) collective-permute-start(bf16[64,1536]{1,0:T(8,128)(2,1)S(1)} %collective-permute-done.17), channel_id=1, source_target_pairs={{0,32},{1,97},{2,34},{3,99},{4,36},{5,101},{6,38},{7,103},{8,40},{... | collective-permute-start | bytes 589832 | tf_op jit(solution)/shard_map/ppermute | solution.py:68
  23.1 6.9 %collective-permute-start.2 = (bf16[64,1536]{1,0:T(8,128)(2,1)S(1)}, bf16[64,1536]{1,0:T(8,128)(2,1)S(1)}, u32[]{:S(2)}, u32[]{:S(2)}) collective-permute-start(bf16[64,1536]{1,0:T(8,128)(2,1)S(1)} %collective-permute-done.1), channel_id=1, source_target_pairs={{0,2},{1,7},{2,4},{3,1},{4,6},{5,3},{6,0},{7,5},{8,10},{9,15},{10,... | collective-permute-start | bytes 589832 | tf_op jit(solution)/shard_map/ppermute | solution.py:68
  30.6 12.2 %collective-permute-start.6 = (bf16[128,1536]{1,0:T(8,128)(2,1)S(1)}, bf16[128,1536]{1,0:T(8,128)(2,1)}, u32[]{:S(2)}, u32[]{:S(2)}) collective-permute-start(bf16[128,1536]{1,0:T(8,128)(2,1)S(1)} %pad_maximum_fusion.2), channel_id=1, source_target_pairs={{0,2},{2,0},{1,3},{3,1},{4,6},{6,4},{5,7},{7,5},{8,10},{10,8},{9,1... | collective-permute-start | bytes 1179656 | tf_op jit(solution)/shard_map/ppermute | solution.py:688
  30.6 13.5 %collective-permute-start.3 = (bf16[256,1536]{1,0:T(8,128)(2,1)}, bf16[256,1536]{1,0:T(8,128)(2,1)}, u32[]{:S(2)}, u32[]{:S(2)}) collective-permute-start(bf16[256,1536]{1,0:T(8,128)(2,1)} %constant_dynamic-update-slice_fusion.15), channel_id=1, source_target_pairs={{0,8},{1,25},{2,10},{3,27},{4,12},{5,29},{6,14},{7,31},{8,16},{9,1... | collective-permute-start | bytes 2359304 | tf_op jit(solution)/shard_map/ppermute | solution.py:68
  32.6 13.5 %collective-permute-start.19 = (bf16[256,1536]{1,0:T(8,128)(2,1)}, bf16[256,1536]{1,0:T(8,128)(2,1)}, u32[]{:S(2)}, u32[]{:S(2)}) collective-permute-start(bf16[256,1536]{1,0:T(8,128)(2,1)} %constant_dynamic-update-slice_fusion.3), channel_id=1, source_target_pairs={{0,2},{1,7},{2,4},{3,1},{4,6},{5,3},{6,0},{7,5},{8,10},{9,15},{10,... | collective-permute-start | bytes 2359304 | tf_op jit(solution)/shard_map/ppermute | solution.py:68
  35.3 13.5 %collective-permute-start.12 = (bf16[256,1536]{1,0:T(8,128)(2,1)}, bf16[256,1536]{1,0:T(8,128)(2,1)}, u32[]{:S(2)}, u32[]{:S(2)}) collective-permute-start(bf16[256,1536]{1,0:T(8,128)(2,1)} %constant_dynamic-update-slice_fusion.9), channel_id=1, source_target_pairs={{0,32},{1,97},{2,34},{3,99},{4,36},{5,101},{6,38},{7,103},{8,40},{... | collective-permute-start | bytes 2359304 | tf_op jit(solution)/shard_map/ppermute | solution.py:68
  44.1 13.4 %collective-permute-start.4 = (bf16[256,1536]{1,0:T(8,128)(2,1)}, bf16[256,1536]{1,0:T(8,128)(2,1)S(1)}, u32[]{:S(2)}, u32[]{:S(2)}) collective-permute-start(bf16[256,1536]{1,0:T(8,128)(2,1)} %collective-permute-done.3), channel_id=1, source_target_pairs={{0,8},{1,25},{2,10},{3,27},{4,12},{5,29},{6,14},{7,31},{8,16},{9,1... | collective-permute-start | bytes 2359304 | tf_op jit(solution)/shard_map/ppermute | solution.py:68
  46.1 15.4 %collective-permute-start.20 = (bf16[256,1536]{1,0:T(8,128)(2,1)}, bf16[256,1536]{1,0:T(8,128)(2,1)S(1)}, u32[]{:S(2)}, u32[]{:S(2)}) collective-permute-start(bf16[256,1536]{1,0:T(8,128)(2,1)} %collective-permute-done.19), channel_id=1, source_target_pairs={{0,2},{1,7},{2,4},{3,1},{4,6},{5,3},{6,0},{7,5},{8,10},{9,15},{10,... | collective-permute-start | bytes 2359304 | tf_op jit(solution)/shard_map/ppermute | solution.py:68
  48.8 13.4 %collective-permute-start.13 = (bf16[256,1536]{1,0:T(8,128)(2,1)}, bf16[256,1536]{1,0:T(8,128)(2,1)S(1)}, u32[]{:S(2)}, u32[]{:S(2)}) collective-permute-start(bf16[256,1536]{1,0:T(8,128)(2,1)} %collective-permute-done.12), channel_id=1, source_target_pairs={{0,32},{1,97},{2,34},{3,99},{4,36},{5,101},{6,38},{7,103},{8,40},{... | collective-permute-start | bytes 2359304 | tf_op jit(solution)/shard_map/ppermute | solution.py:68
  57.5 13.2 %collective-permute-start.5 = (bf16[256,1536]{1,0:T(8,128)(2,1)S(1)}, bf16[256,1536]{1,0:T(8,128)(2,1)S(1)}, u32[]{:S(2)}, u32[]{:S(2)}) collective-permute-start(bf16[256,1536]{1,0:T(8,128)(2,1)S(1)} %collective-permute-done.4), channel_id=1, source_target_pairs={{0,8},{1,25},{2,10},{3,27},{4,12},{5,29},{6,14},{7,31},{8,16},{9,1... | collective-permute-start | bytes 2359304 | tf_op jit(solution)/shard_map/ppermute | solution.py:68
  61.5 15.5 %collective-permute-start.21 = (bf16[256,1536]{1,0:T(8,128)(2,1)S(1)}, bf16[256,1536]{1,0:T(8,128)(2,1)S(1)}, u32[]{:S(2)}, u32[]{:S(2)}) collective-permute-start(bf16[256,1536]{1,0:T(8,128)(2,1)S(1)} %collective-permute-done.20), channel_id=1, source_target_pairs={{0,2},{1,7},{2,4},{3,1},{4,6},{5,3},{6,0},{7,5},{8,10},{9,15},{10,... | collective-permute-start | bytes 2359304 | tf_op jit(solution)/shard_map/ppermute | solution.py:68
  62.2 13.2 %collective-permute-start.14 = (bf16[256,1536]{1,0:T(8,128)(2,1)S(1)}, bf16[256,1536]{1,0:T(8,128)(2,1)S(1)}, u32[]{:S(2)}, u32[]{:S(2)}) collective-permute-start(bf16[256,1536]{1,0:T(8,128)(2,1)S(1)} %collective-permute-done.13), channel_id=1, source_target_pairs={{0,32},{1,97},{2,34},{3,99},{4,36},{5,101},{6,38},{7,103},{8,40},{... | collective-permute-start | bytes 2359304 | tf_op jit(solution)/shard_map/ppermute | solution.py:68
  62.6 55.5 %copy-start.23 = (s32[12]{0:T(128)S(1)}, s32[12]{0:T(128)}, u32[]{:S(2)}) copy-start(s32[12]{0:T(128)} %param.15) | copy-start | bytes 148
  62.7 55.5 %copy-start.24 = (s32[12]{0:T(128)S(1)}, s32[12]{0:T(128)}, u32[]{:S(2)}) copy-start(s32[12]{0:T(128)} %param.16) | copy-start | bytes 148
  62.7 60.2 %copy-start.12 = (f32[3072]{0:T(1024)S(1)}, f32[3072]{0:T(1024)}, u32[]{:S(2)}) copy-start(f32[3072]{0:T(1024)} %param.23) | copy-start | bytes 36868
  62.7 60.2 %copy-start.13 = (f32[3072]{0:T(1024)S(1)}, f32[3072]{0:T(1024)}, u32[]{:S(2)}) copy-start(f32[3072]{0:T(1024)} %param.24) | copy-start | bytes 36868
  70.8 47.3 %copy-start.15 = (bf16[1024,1536]{1,0:T(8,128)(2,1)}, bf16[1024,1536]{1,0:T(8,128)(2,1)S(1)}, u32[]{:S(2)}) copy-start(bf16[1024,1536]{1,0:T(8,128)(2,1)S(1)} %constant_dynamic-update-slice_fusion.12) | copy-start | bytes 9437188
  75.5 40.1 %collective-permute-start.15 = (bf16[1024,1536]{1,0:T(8,128)(2,1)S(1)}, bf16[1024,1536]{1,0:T(8,128)(2,1)}, u32[]{:S(2)}, u32[]{:S(2)}) collective-permute-start(bf16[1024,1536]{1,0:T(8,128)(2,1)S(1)} %constant_dynamic-update-slice_fusion.6), channel_id=1, source_target_pairs={{0,2},{1,7},{2,4},{3,1},{4,6},{5,3},{6,0},{7,5},{8,10},{9,15},{10,... | collective-permute-start | bytes 9437192 | tf_op jit(solution)/shard_map/ppermute | solution.py:68
  77.0 38.6 %collective-permute-start.7 = (bf16[1024,1536]{1,0:T(8,128)(2,1)S(1)}, bf16[1024,1536]{1,0:T(8,128)(2,1)}, u32[]{:S(2)}, u32[]{:S(2)}) collective-permute-start(bf16[1024,1536]{1,0:T(8,128)(2,1)S(1)} %constant_dynamic-update-slice_fusion.12), channel_id=1, source_target_pairs={{0,32},{1,97},{2,34},{3,99},{4,36},{5,101},{6,38},{7,103},{8,40},{... | collective-permute-start | bytes 9437192 | tf_op jit(solution)/shard_map/ppermute | solution.py:68
  77.0 38.5 %copy-start.14 = (bf16[1024,1536]{1,0:T(8,128)(2,1)}, bf16[1024,1536]{1,0:T(8,128)(2,1)S(1)}, u32[]{:S(2)}) copy-start(bf16[1024,1536]{1,0:T(8,128)(2,1)S(1)} %constant_dynamic-update-slice_fusion) | copy-start | bytes 9437188
  77.0 41.1 %collective-permute-start.22 = (bf16[1024,1536]{1,0:T(8,128)(2,1)S(1)}, bf16[1024,1536]{1,0:T(8,128)(2,1)}, u32[]{:S(2)}, u32[]{:S(2)}) collective-permute-start(bf16[1024,1536]{1,0:T(8,128)(2,1)S(1)} %constant_dynamic-update-slice_fusion), channel_id=1, source_target_pairs={{0,8},{1,25},{2,10},{3,27},{4,12},{5,29},{6,14},{7,31},{8,16},{9,1... | collective-permute-start | bytes 9437192 | tf_op jit(solution)/shard_map/ppermute | solution.py:68
  115.6 38.8 %collective-permute-start.8 = (bf16[1024,1536]{1,0:T(8,128)(2,1)}, bf16[1024,1536]{1,0:T(8,128)(2,1)}, u32[]{:S(2)}, u32[]{:S(2)}) collective-permute-start(bf16[1024,1536]{1,0:T(8,128)(2,1)} %collective-permute-done.7), channel_id=1, source_target_pairs={{0,32},{1,97},{2,34},{3,99},{4,36},{5,101},{6,38},{7,103},{8,40},{... | collective-permute-start | bytes 9437192 | tf_op jit(solution)/shard_map/ppermute | solution.py:68
  115.6 38.9 %collective-permute-start.24 = (bf16[1024,1536]{1,0:T(8,128)(2,1)}, bf16[1024,1536]{1,0:T(8,128)(2,1)}, u32[]{:S(2)}, u32[]{:S(2)}) collective-permute-start(bf16[1024,1536]{1,0:T(8,128)(2,1)} %collective-permute-done.15), channel_id=1, source_target_pairs={{0,2},{1,7},{2,4},{3,1},{4,6},{5,3},{6,0},{7,5},{8,10},{9,15},{10,... | collective-permute-start | bytes 9437192 | tf_op jit(solution)/shard_map/ppermute | solution.py:68
  118.1 38.8 %collective-permute-start.25 = (bf16[1024,1536]{1,0:T(8,128)(2,1)}, bf16[1024,1536]{1,0:T(8,128)(2,1)}, u32[]{:S(2)}, u32[]{:S(2)}) collective-permute-start(bf16[1024,1536]{1,0:T(8,128)(2,1)} %collective-permute-done.22), channel_id=1, source_target_pairs={{0,8},{1,25},{2,10},{3,27},{4,12},{5,29},{6,14},{7,31},{8,16},{9,1... | collective-permute-start | bytes 9437192 | tf_op jit(solution)/shard_map/ppermute | solution.py:68
  122.8 1.1 copy-start.2
  126.4 2.6 collective-permute-start.23
  131.3 25.7 %copy-start.18 = (bf16[128,3072]{1,0:T(8,128)(2,1)S(1)}, bf16[128,3072]{1,0:T(8,128)(2,1)}, u32[]{:S(2)}) copy-start(bf16[128,3072]{1,0:T(8,128)(2,1)} %pad_maximum_fusion.1) | copy-start | bytes 2359300
  131.3 26.5 %copy-start.9 = (bf16[3072,64]{0,1:T(8,128)(2,1)S(1)}, bf16[3072,64]{0,1:T(8,128)(2,1)}, u32[]{:S(2)}) copy-start(bf16[3072,64]{0,1:T(8,128)(2,1)} %param.19) | copy-start | bytes 1179652
  154.4 38.7 %collective-permute-start.26 = (bf16[1024,1536]{1,0:T(8,128)(2,1)}, bf16[1024,1536]{1,0:T(8,128)(2,1)S(1)}, u32[]{:S(2)}, u32[]{:S(2)}) collective-permute-start(bf16[1024,1536]{1,0:T(8,128)(2,1)} %collective-permute-done.24), channel_id=1, source_target_pairs={{0,2},{1,7},{2,4},{3,1},{4,6},{5,3},{6,0},{7,5},{8,10},{9,15},{10,... | collective-permute-start | bytes 9437192 | tf_op jit(solution)/shard_map/ppermute | solution.py:68
  156.9 38.7 %collective-permute-start.27 = (bf16[1024,1536]{1,0:T(8,128)(2,1)}, bf16[1024,1536]{1,0:T(8,128)(2,1)S(1)}, u32[]{:S(2)}, u32[]{:S(2)}) collective-permute-start(bf16[1024,1536]{1,0:T(8,128)(2,1)} %collective-permute-done.25), channel_id=1, source_target_pairs={{0,8},{1,25},{2,10},{3,27},{4,12},{5,29},{6,14},{7,31},{8,16},{9,1... | collective-permute-start | bytes 9437192 | tf_op jit(solution)/shard_map/ppermute | solution.py:68
  156.9 38.8 %collective-permute-start.28 = (bf16[1024,1536]{1,0:T(8,128)(2,1)}, bf16[1024,1536]{1,0:T(8,128)(2,1)}, u32[]{:S(2)}, u32[]{:S(2)}) collective-permute-start(bf16[1024,1536]{1,0:T(8,128)(2,1)} %collective-permute-done.8), channel_id=1, source_target_pairs={{0,32},{1,97},{2,34},{3,99},{4,36},{5,101},{6,38},{7,103},{8,40},{... | collective-permute-start | bytes 9437192 | tf_op jit(solution)/shard_map/ppermute | solution.py:68
  193.1 2.6 copy-start.16
  195.6 1.6 copy-start.17
  197.3 21.9 %copy-start.1 = (bf16[96,3072]{1,0:T(8,128)(2,1)S(1)}, bf16[96,3072]{1,0:T(8,128)(2,1)}, u32[]{:S(2)}) copy-start(bf16[96,3072]{1,0:T(8,128)(2,1)} %noise.3) | copy-start | bytes 1769476
  197.3 21.9 %copy-start.3 = (bf16[96,3072]{1,0:T(8,128)(2,1)S(1)}, bf16[96,3072]{1,0:T(8,128)(2,1)}, u32[]{:S(2)}) copy-start(bf16[96,3072]{1,0:T(8,128)(2,1)} %given.2) | copy-start | bytes 1769476
  197.3 21.9 %copy-start.11 = (f32[3072]{0:T(1024)S(1)}, f32[3072]{0:T(1024)}, u32[]{:S(2)}) copy-start(f32[3072]{0:T(1024)} %param.25) | copy-start | bytes 36868
  217.0 2.1 collective-permute-start.29
  221.0 2.3 copy-start.7
  221.0 2.3 collective-permute-start.30
  223.3 0.8 copy-start.19
  245.4 3.1 %collective-permute-start.31 = (bf16[192,3072]{1,0:T(8,128)(2,1)}, bf16[192,3072]{1,0:T(8,128)(2,1)S(1)}, u32[]{:S(2)}, u32[]{:S(2)}) collective-permute-start(bf16[192,3072]{1,0:T(8,128)(2,1)} %get-tuple-element.66), channel_id=1, source_target_pairs={{0,1},{1,0},{2,3},{3,2},{4,5},{5,4},{6,7},{7,6},{8,9},{9,8},{10,11... | collective-permute-start | bytes 3538952 | tf_op jit(solution)/shard_map/ppermute | solution.py:49
  248.5 1.3 copy-start.5
  249.8 1.3 copy-start.6
  251.1 4.5 %copy-start = (f32[192,3072]{1,0:T(8,128)S(1)}, f32[192,3072]{1,0:T(8,128)}, u32[]{:S(2)}) copy-start(f32[192,3072]{1,0:T(8,128)} %get-tuple-element.72.slope_fake) | copy-start | bytes 7077892
  251.1 4.5 %copy-start.4 = (bf16[64,3072]{1,0:T(8,128)(2,1)S(1)}, bf16[64,3072]{1,0:T(8,128)(2,1)}, u32[]{:S(2)}) copy-start(bf16[64,3072]{1,0:T(8,128)(2,1)} %get-tuple-element.77.adapt_out.fake_out) | copy-start | bytes 1179652
  251.1 4.5 %copy-start.10 = (bf16[192,64]{1,0:T(8,128)(2,1)S(1)}, bf16[192,64]{1,0:T(8,128)(2,1)}, u32[]{:S(2)}) copy-start(bf16[192,64]{1,0:T(8,128)(2,1)} %get-tuple-element.74.low_fake) | copy-start | bytes 73732
  252.8 2.8 collective-permute-start.32
  267.6 1.9 collective-permute-start.33
  271.6 1.1 copy-start.8
  271.6 1.2 copy-start.20

commit v4 on v3

--- a/solution.py
+++ b/solution.py
@@ -104,7 +104,6 @@
 PIECE = 64
 REST = SHARD - PIECE
 TILE = 512
-WINDOW = 3
 BLOCK = 8 * SHARD
 MIB = 2**20
 ANYWHERE = pl.BlockSpec(memory_space=pl.ANY)
@@ -259,17 +258,6 @@
     return pltpu.make_async_copy(source.at[rows], target.at[rows], sems.at[n])
 
 
-def start_ahead(place, segments):
-    ahead = place + WINDOW
-    for count, copy in segments:
-
-        @pl.when((ahead >= 0) & (ahead < count))
-        def _(ahead=ahead, copy=copy):
-            copy(ahead).start()
-
-        ahead = ahead - count
-
-
 def tile_at(n):
     return pl.ds(pl.multiple_of(n * TILE, TILE), TILE)
 
@@ -287,10 +275,8 @@
         return pltpu.make_async_copy(down_in.at[part], down.at[part], down_sems.at[n])
 
     blocks = down.shape[0] // BLOCK
-    for i in (0, 2, 1):
-        fetches[i].start()
-    for n in range(blocks):
-        down_copy(n).start()
+    fetches[0].start()
+    fetches[2].start()
 
     def spot(i, k):
         return table[0, i * pieces + k], pl.multiple_of(table[1, i * pieces + k], 32)
@@ -301,6 +287,9 @@
         u_rest[k % 2, at] = u_columns[pl.ds(pl.multiple_of(spot(2, k)[1] + PIECE, 32), REST), :]
     fetches[0].wait()
     fetches[2].wait()
+    fetches[1].start()
+    for n in range(blocks):
+        down_copy(n).start()
     for k in range(pieces):
         up_rest[k % 2, pl.ds(k // 2 * REST, REST)] = last[2, k, :REST]
     first_quarter, rest_quarter = table[0, 0], table[0, 2 * pieces]
@@ -401,12 +390,8 @@
 ):
     u, act, up, down, up_sems, down_sems = scratch
     hidden_tiles, width_tiles = up.shape[1] // TILE, down.shape[0] // TILE
-    segments = (
-        (hidden_tiles, functools.partial(column_copy, up_in, up, up_sems)),
-        (width_tiles, functools.partial(row_copy, down_in, down, down_sems)),
-    )
-    for n in range(WINDOW):
-        column_copy(up_in, up, up_sems, n).start()
+    each(hidden_tiles, lambda n: column_copy(up_in, up, up_sems, n).start(), 1)
+    each(width_tiles, lambda n: row_copy(down_in, down, down_sems, n).start(), 1)
     rows = u_mine.shape[0]
     group = 2 * rows
     u[:rows] = u_mine[...]
@@ -415,7 +400,6 @@
 
     def hidden_tile(n):
         column_copy(up_in, up, up_sems, n).wait()
-        start_ahead(n, segments)
         cols = tile_at(n)
         pre_real = dot(u[...], up[:, cols])
         pre_fake = pre_real + dot(low[...], adapt_out[:, cols])
@@ -427,7 +411,6 @@
 
     def width_tile(n):
         row_copy(down_in, down, down_sems, n).wait()
-        start_ahead(hidden_tiles + n, segments)
         cols = tile_at(n)
         out = dot(act[...], down[cols, :], NT)
         real[:, cols] = out[:rows]
@@ -462,7 +445,7 @@
             pltpu.SemaphoreType.DMA((hidden // TILE,)),
             pltpu.SemaphoreType.DMA((width // TILE,)),
         ],
-        compiler_params=pltpu.CompilerParams(vmem_limit_bytes=56 * MIB),
+        compiler_params=pltpu.CompilerParams(vmem_limit_bytes=50 * MIB),
         cost_estimate=pl.CostEstimate(
             flops=6 * group * width * hidden,
             bytes_accessed=50 * MIB,
@@ -477,8 +460,7 @@
 ):
     cots, down, sems = scratch
     tiles = down.shape[1] // TILE
-    for n in range(WINDOW):
-        column_copy(down_in, down, sems, n).start()
+    each(tiles, lambda n: column_copy(down_in, down, sems, n).start(), 1)
     group = cots_mine.shape[0]
     rows = group // 2
     for i in range(2):
@@ -488,7 +470,6 @@
 
     def hidden_tile(n):
         column_copy(down_in, down, sems, n).wait()
-        start_ahead(n, ((tiles, functools.partial(column_copy, down_in, down, sems)),))
         cols = tile_at(n)
         raw = dot(cots[...], down[:, cols])
         back_gen = (raw[:group] * slope_gen[:, cols]).astype(jnp.bfloat16)

time: 304 us -> 295 us (0.970)
  Pallas kernels: 81.6 us -> 76.2 us
  local copies, waits for them, and re-layouts: 37.8 us -> 32.6 us
    unnamed x50 -> x34, local copies, waits for them, and re-layouts: 6.77 us -> 2.4 us
  transfers between devices with their start and end apart: 34 -> 34, of which waited for: 23 -> 22; matrix products, arithmetic and copies ran while one was open for 12% -> 12% of each run, Pallas kernels for 8% -> 9%
where the time goes in v4:
time: 295 us; the launch traced here: 294 us
  waiting for transfers between devices  114 us (39%)
  Pallas kernels  76.2 us (26%)
  local copies, waits for them, and re-layouts  32.6 us (11%)
  starting transfers between devices  30.9 us (10%)
  blocking collectives  27.8 us (9%)
  other arithmetic  9.68 us (3%)
    ppermute x27, waiting for transfers between devices, send(): return lax.ppermute(piece, AXES, chip_ring(RING_AXES[i][phase]))  102 us
    ppermute x27, starting transfers between devices, send(): return lax.ppermute(piece, AXES, chip_ring(RING_AXES[i][phase]))  29.9 us
    all_to_all x1, blocking collectives, local(): received = lax.all_to_all(packed, CHIPS, 0, 0, tiled=True)  27.8 us
    pallas_call x1, Pallas kernels, load_weights(): pl.pallas_call(load_body, out_shape=(shape, shape, jax.ShapeDtypeStruct((...  22.6 us
    pallas_call x1, Pallas kernels, score_forward(): pl.pallas_call(score_body, out_shape=(jax.ShapeDtypeStruct((group, hidden...  18.7 us
    pallas_call x1, Pallas kernels, gen_forward(): pl.pallas_call(gen_body, out_shape=(shape, shape, jax.ShapeDtypeStruct((g...  17 us
    dynamic_update_slice x24, local copies, waits for them, and re-layouts, gathered(): lax.dynamic_update_slice(buffer, piece, (step * rows, 0))  17 us
    pallas_call x1, Pallas kernels, backward(): pl.pallas_call(back_body, out_shape=(jax.ShapeDtypeStruct((2, rank, hidde...  11.9 us
  transfers between devices with their start and end apart: 34, of which 22 were waited for; matrix products, arithmetic and copies ran while one was open for 12% of the time, Pallas kernels for 9%

profile of v4, /device:TPU:0, one launch (start us, length us, event | category | flops | bytes accessed | tf_op | source)
XLA Modules:
  0.0 294.5 jit_solution(3424029989441549874)
XLA Ops:
  0.7 1.0 slice.85
  1.6 1.7 collective-permute-start.9
  3.4 0.9 slice.110
  4.3 2.0 collective-permute-start.16
  6.3 0.9 slice.109
  7.2 0.9 slice.83
  8.1 1.6 collective-permute-start
  9.7 1.0 dynamic_update_slice.80
  10.6 0.9 dynamic_update_slice.88
  11.6 1.0 dynamic_update_slice.72
  12.6 1.6 collective-permute-start.10
  14.2 1.9 collective-permute-start.17
  16.2 1.5 collective-permute-start.1
  19.7 1.3 collective-permute-start.11
  21.1 1.5 collective-permute-start.18
  25.9 4.0 %collective-permute-done.2 = bf16[64,1536]{1,0:T(8,128)(2,1)S(1)} collective-permute-done((bf16[64,1536]{1,0:T(8,128)(2,1)S(1)}, bf16[64,1536]{1,0:T(8,128)(2,1)S(1)}, u32[]{:S(2)}, u32[]{:S(2)}) %collective-permute-start.2) | collective-permute-done | bytes 196640 | tf_op jit(solution)/shard_map/ppermute | solution.py:68
  30.6 1.3 collective-permute-start.3
  32.6 2.0 collective-permute-start.19
  35.3 1.6 collective-permute-start.12
  37.0 1.3 dynamic_update_slice.76
  38.3 1.3 dynamic_update_slice.92
  39.6 1.3 dynamic_update_slice.84
  41.0 1.8 collective-permute-done.6
  42.8 1.1 broadcast_select_fusion.1
  44.1 1.1 collective-permute-start.4
  45.2 0.9 collective-permute-done.19
  46.1 2.3 collective-permute-start.20
  48.8 0.9 collective-permute-start.13
  49.8 1.0 pad_maximum_fusion.1
  50.8 1.2 constant_dynamic-update-slice_fusion.14
  52.0 1.2 constant_dynamic-update-slice_fusion.2
  53.1 4.4 %collective-permute-done.4 = bf16[256,1536]{1,0:T(8,128)(2,1)S(1)} collective-permute-done((bf16[256,1536]{1,0:T(8,128)(2,1)}, bf16[256,1536]{1,0:T(8,128)(2,1)S(1)}, u32[]{:S(2)}, u32[]{:S(2)}) %collective-permute-start.4) | collective-permute-done | bytes 786464 | tf_op jit(solution)/shard_map/ppermute | solution.py:68
  57.6 1.2 constant_dynamic-update-slice_fusion.8
  58.7 2.7 collective-permute-done.20
  61.4 0.8 collective-permute-done.13
  62.7 8.1 %collective-permute-done.5 = bf16[256,1536]{1,0:T(8,128)(2,1)S(1)} collective-permute-done((bf16[256,1536]{1,0:T(8,128)(2,1)S(1)}, bf16[256,1536]{1,0:T(8,128)(2,1)S(1)}, u32[]{:S(2)}, u32[]{:S(2)}) %collective-permute-start.5) | collective-permute-done | bytes 786464 | tf_op jit(solution)/shard_map/ppermute | solution.py:68
  70.8 4.6 %collective-permute-done.14 = bf16[256,1536]{1,0:T(8,128)(2,1)S(1)} collective-permute-done((bf16[256,1536]{1,0:T(8,128)(2,1)S(1)}, bf16[256,1536]{1,0:T(8,128)(2,1)S(1)}, u32[]{:S(2)}, u32[]{:S(2)}) %collective-permute-start.14) | collective-permute-done | bytes 786464 | tf_op jit(solution)/shard_map/ppermute | solution.py:68
  75.5 1.4 collective-permute-start.15
  77.1 38.4 %collective-permute-done.7 = bf16[1024,1536]{1,0:T(8,128)(2,1)} collective-permute-done((bf16[1024,1536]{1,0:T(8,128)(2,1)S(1)}, bf16[1024,1536]{1,0:T(8,128)(2,1)}, u32[]{:S(2)}, u32[]{:S(2)}) %collective-permute-start.7) | collective-permute-done | bytes 3145760 | tf_op jit(solution)/shard_map/ppermute | solution.py:68
  115.5 2.5 collective-permute-start.24
  118.9 1.4 fusion.25.blends
  120.2 2.7 add_convert_fusion.steps
  123.0 1.1 copy-done.2
  124.0 2.5 first_modulation.1
  126.9 2.2 copy.35
  129.1 2.2 copy.36
  131.4 2.1 maximum_bitcast_fusion.u_columns
  133.5 20.8 %collective-permute-done.8 = bf16[1024,1536]{1,0:T(8,128)(2,1)} collective-permute-done((bf16[1024,1536]{1,0:T(8,128)(2,1)}, bf16[1024,1536]{1,0:T(8,128)(2,1)}, u32[]{:S(2)}, u32[]{:S(2)}) %collective-permute-start.8) | collective-permute-done | bytes 3145760 | tf_op jit(solution)/shard_map/ppermute | solution.py:68
  154.4 2.4 collective-permute-start.26
  157.0 22.6 %load_weights.1 = (bf16[3072,3072]{1,0:T(8,128)(2,1)}, bf16[3072,3072]{1,0:T(8,128)(2,1)}, f32[192,3072]{1,0:T(8,128)S(1)}, bf16[192,64]{1,0:T(8,128)(2,1)S(1)}) custom-call(s32[4]{0:T(128)S(1)} %pad_add_fusion.1.place_ref, s32[3,48]{1,0:T(4,128)S(1)} %pad_add_fusion.table, bf16[96,3072]{1,0:T(8,128)(2,1)} %get-tuple-element.51.u_mine, ...), custom_call_target="tpu_custom_call" | custom-call | flops 3623878656 | bytes 150994944 | tf_op jit(solution)/shard_map/load_weights/pallas_call | solution.py:227
  179.6 13.6 %collective-permute-done.26 = bf16[1024,1536]{1,0:T(8,128)(2,1)} collective-permute-done((bf16[1024,1536]{1,0:T(8,128)(2,1)}, bf16[1024,1536]{1,0:T(8,128)(2,1)}, u32[]{:S(2)}, u32[]{:S(2)}) %collective-permute-start.26) | collective-permute-done | bytes 3145760 | tf_op jit(solution)/shard_map/ppermute | solution.py:68
  193.2 2.5 collective-permute-done.27
  195.7 17.0 %gen_forward.1 = (bf16[3072,3072]{1,0:T(8,128)(2,1)}, bf16[3072,3072]{1,0:T(8,128)(2,1)}, f32[192,3072]{1,0:T(8,128)S(1)}, f32[96,3072]{1,0:T(8,128)S(1)}, bf16[96,3072]{1,0:T(8,128)(2,1)S(1)}) custom-call(s32[3,48]{1,0:T(4,128)S(1)} %pad_add_fusion.table, ...), custom_call_target="tpu_custom_call", output_to_operand_aliasing={{0}: (6, {}), {1}: (7, {})} | custom-call | flops 5435817984 | bytes 41943040 | tf_op jit(solution)/shard_map/gen_forward/pallas_call | solution.py:356
  212.8 2.0 collective-permute-done.29.other
  214.8 1.9 add_noise.1
  217.1 1.9 collective-permute-done.30.u_other
  219.0 18.7 %score_forward.1 = (f32[192,3072]{1,0:T(8,128)}, bf16[192,64]{1,0:T(8,128)(2,1)S(1)}, f32[96,3072]{1,0:T(8,128)S(1)}, f32[96,3072]{1,0:T(8,128)}, bf16[192,3072]{1,0:T(8,128)(2,1)}) custom-call(bf16[96,3072]{1,0:T(8,128)(2,1)S(1)} %get-tuple-element.61.u_mine, bf16[96,3072]{1,0:T(8,128)(2,1)S(1)} %collective-permute-done.30.u_other, ...), custom_call_target="tpu_custom_call" | custom-call | flops 10871635968 | bytes 52428800 | tf_op jit(solution)/shard_map/score_forward/pallas_call | solution.py:429
  237.9 2.9 collective-permute-done.31.others
  240.8 1.3 copy-done.4
  242.1 1.7 cotangents.1
  243.9 2.7 collective-permute-done.32.cots_other
  246.6 11.9 %backward.1 = (bf16[2,64,3072]{2,1,0:T(8,128)(2,1)S(1)}, f32[2,192,64]{2,1,0:T(8,128)S(1)}) custom-call(bf16[192,3072]{1,0:T(8,128)(2,1)S(1)} %get-tuple-element.70.cots_mine, bf16[192,3072]{1,0:T(8,128)(2,1)S(1)} %collective-permute-done.32.cots_other, f32[192,3072]{1,0:T(8,128)S(1)} %get-tuple-element.71.slope_gen, f32[192,3072]{1,0:T(8,128)S(1)} %copy-done, ...), custom_call_target="tpu_custom_call" | custom-call | flops 7247757312 | bytes 31457280 | tf_op jit(solution)/shard_map/backward/pallas_call | solution.py:490
  260.8 1.8 fusion
  264.6 27.8 %all_to_all.5 = bf16[64,72,128]{2,1,0:T(8,128)(2,1)S(1)} all-to-all(bf16[64,72,128]{2,1,0:T(8,128)(2,1)S(1)} %pad_maximum_fusion), channel_id=1, replica_groups=mesh['z'=4,'y'=4,'xh'=2,'xl'=2,'core'=2] {'z','y','xh','xl'}, dimensions={0} | all-to-all | bytes 2359296 | tf_op jit(solution)/shard_map/all_to_all | solution.py:744
  (116 shorter events, 17.3 us)
Async XLA Ops:
  0.6 11.9 %copy-start.13 = (bf16[64,1536]{1,0:T(8,128)(2,1)S(1)}, bf16[64,1536]{1,0:T(8,128)(2,1)}, u32[]{:S(2)}) copy-start(bf16[64,1536]{1,0:T(8,128)(2,1)} %param.22) | copy-start | bytes 589828
  0.6 11.9 %copy-start.14 = (bf16[64,1536]{1,0:T(8,128)(2,1)S(1)}, bf16[64,1536]{1,0:T(8,128)(2,1)}, u32[]{:S(2)}) copy-start(bf16[64,1536]{1,0:T(8,128)(2,1)} %param.20) | copy-start | bytes 589828
  1.6 10.9 %collective-permute-start.9 = (bf16[64,1536]{1,0:T(8,128)(2,1)S(1)}, bf16[64,1536]{1,0:T(8,128)(2,1)S(1)}, u32[]{:S(2)}, u32[]{:S(2)}) collective-permute-start(bf16[64,1536]{1,0:T(8,128)(2,1)S(1)} %slice.85), channel_id=1, source_target_pairs={{0,8},{1,25},{2,10},{3,27},{4,12},{5,29},{6,14},{7,31},{8,16},{9,1... | collective-permute-start | bytes 589832 | tf_op jit(solution)/shard_map/ppermute | solution.py:68
  4.3 9.9 %collective-permute-start.16 = (bf16[64,1536]{1,0:T(8,128)(2,1)S(1)}, bf16[64,1536]{1,0:T(8,128)(2,1)S(1)}, u32[]{:S(2)}, u32[]{:S(2)}) collective-permute-start(bf16[64,1536]{1,0:T(8,128)(2,1)S(1)} %slice.110), channel_id=1, source_target_pairs={{0,32},{1,97},{2,34},{3,99},{4,36},{5,101},{6,38},{7,103},{8,40},{... | collective-permute-start | bytes 589832 | tf_op jit(solution)/shard_map/ppermute | solution.py:68
  8.1 8.0 %collective-permute-start = (bf16[64,1536]{1,0:T(8,128)(2,1)S(1)}, bf16[64,1536]{1,0:T(8,128)(2,1)S(1)}, u32[]{:S(2)}, u32[]{:S(2)}) collective-permute-start(bf16[64,1536]{1,0:T(8,128)(2,1)S(1)} %pad_maximum_fusion.3), channel_id=1, source_target_pairs={{0,2},{1,7},{2,4},{3,1},{4,6},{5,3},{6,0},{7,5},{8,10},{9,15},{10,... | collective-permute-start | bytes 589832 | tf_op jit(solution)/shard_map/ppermute | solution.py:68
  12.6 7.1 %collective-permute-start.10 = (bf16[64,1536]{1,0:T(8,128)(2,1)S(1)}, bf16[64,1536]{1,0:T(8,128)(2,1)S(1)}, u32[]{:S(2)}, u32[]{:S(2)}) collective-permute-start(bf16[64,1536]{1,0:T(8,128)(2,1)S(1)} %collective-permute-done.9), channel_id=1, source_target_pairs={{0,8},{1,25},{2,10},{3,27},{4,12},{5,29},{6,14},{7,31},{8,16},{9,1... | collective-permute-start | bytes 589832 | tf_op jit(solution)/shard_map/ppermute | solution.py:68
  14.2 6.9 %collective-permute-start.17 = (bf16[64,1536]{1,0:T(8,128)(2,1)S(1)}, bf16[64,1536]{1,0:T(8,128)(2,1)S(1)}, u32[]{:S(2)}, u32[]{:S(2)}) collective-permute-start(bf16[64,1536]{1,0:T(8,128)(2,1)S(1)} %collective-permute-done.16), channel_id=1, source_target_pairs={{0,32},{1,97},{2,34},{3,99},{4,36},{5,101},{6,38},{7,103},{8,40},{... | collective-permute-start | bytes 589832 | tf_op jit(solution)/shard_map/ppermute | solution.py:68
  16.2 6.9 %collective-permute-start.1 = (bf16[64,1536]{1,0:T(8,128)(2,1)S(1)}, bf16[64,1536]{1,0:T(8,128)(2,1)S(1)}, u32[]{:S(2)}, u32[]{:S(2)}) collective-permute-start(bf16[64,1536]{1,0:T(8,128)(2,1)S(1)} %collective-permute-done), channel_id=1, source_target_pairs={{0,2},{1,7},{2,4},{3,1},{4,6},{5,3},{6,0},{7,5},{8,10},{9,15},{10,... | collective-permute-start | bytes 589832 | tf_op jit(solution)/shard_map/ppermute | solution.py:68
  19.7 14.9 %collective-permute-start.11 = (bf16[64,1536]{1,0:T(8,128)(2,1)S(1)}, bf16[64,1536]{1,0:T(8,128)(2,1)S(1)}, u32[]{:S(2)}, u32[]{:S(2)}) collective-permute-start(bf16[64,1536]{1,0:T(8,128)(2,1)S(1)} %collective-permute-done.10), channel_id=1, source_target_pairs={{0,8},{1,25},{2,10},{3,27},{4,12},{5,29},{6,14},{7,31},{8,16},{9,1... | collective-permute-start | bytes 589832 | tf_op jit(solution)/shard_map/ppermute | solution.py:68
  21.1 10.8 %collective-permute-start.18 = (bf16[64,1536]{1,0:T(8,128)(2,1)S(1)}, bf16[64,1536]{1,0:T(8,128)(2,1)S(1)}, u32[]{:S(2)}, u32[]{:S(2)}) collective-permute-start(bf16[64,1536]{1,0:T(8,128)(2,1)S(1)} %collective-permute-done.17), channel_id=1, source_target_pairs={{0,32},{1,97},{2,34},{3,99},{4,36},{5,101},{6,38},{7,103},{8,40},{... | collective-permute-start | bytes 589832 | tf_op jit(solution)/shard_map/ppermute | solution.py:68
  23.0 6.9 %collective-permute-start.2 = (bf16[64,1536]{1,0:T(8,128)(2,1)S(1)}, bf16[64,1536]{1,0:T(8,128)(2,1)S(1)}, u32[]{:S(2)}, u32[]{:S(2)}) collective-permute-start(bf16[64,1536]{1,0:T(8,128)(2,1)S(1)} %collective-permute-done.1), channel_id=1, source_target_pairs={{0,2},{1,7},{2,4},{3,1},{4,6},{5,3},{6,0},{7,5},{8,10},{9,15},{10,... | collective-permute-start | bytes 589832 | tf_op jit(solution)/shard_map/ppermute | solution.py:68
  30.6 12.2 %collective-permute-start.6 = (bf16[128,1536]{1,0:T(8,128)(2,1)S(1)}, bf16[128,1536]{1,0:T(8,128)(2,1)}, u32[]{:S(2)}, u32[]{:S(2)}) collective-permute-start(bf16[128,1536]{1,0:T(8,128)(2,1)S(1)} %pad_maximum_fusion.2), channel_id=1, source_target_pairs={{0,2},{2,0},{1,3},{3,1},{4,6},{6,4},{5,7},{7,5},{8,10},{10,8},{9,1... | collective-permute-start | bytes 1179656 | tf_op jit(solution)/shard_map/ppermute | solution.py:669
  30.6 13.5 %collective-permute-start.3 = (bf16[256,1536]{1,0:T(8,128)(2,1)}, bf16[256,1536]{1,0:T(8,128)(2,1)}, u32[]{:S(2)}, u32[]{:S(2)}) collective-permute-start(bf16[256,1536]{1,0:T(8,128)(2,1)} %constant_dynamic-update-slice_fusion.15), channel_id=1, source_target_pairs={{0,8},{1,25},{2,10},{3,27},{4,12},{5,29},{6,14},{7,31},{8,16},{9,1... | collective-permute-start | bytes 2359304 | tf_op jit(solution)/shard_map/ppermute | solution.py:68
  32.6 13.5 %collective-permute-start.19 = (bf16[256,1536]{1,0:T(8,128)(2,1)}, bf16[256,1536]{1,0:T(8,128)(2,1)}, u32[]{:S(2)}, u32[]{:S(2)}) collective-permute-start(bf16[256,1536]{1,0:T(8,128)(2,1)} %constant_dynamic-update-slice_fusion.3), channel_id=1, source_target_pairs={{0,2},{1,7},{2,4},{3,1},{4,6},{5,3},{6,0},{7,5},{8,10},{9,15},{10,... | collective-permute-start | bytes 2359304 | tf_op jit(solution)/shard_map/ppermute | solution.py:68
  35.3 13.5 %collective-permute-start.12 = (bf16[256,1536]{1,0:T(8,128)(2,1)}, bf16[256,1536]{1,0:T(8,128)(2,1)}, u32[]{:S(2)}, u32[]{:S(2)}) collective-permute-start(bf16[256,1536]{1,0:T(8,128)(2,1)} %constant_dynamic-update-slice_fusion.9), channel_id=1, source_target_pairs={{0,32},{1,97},{2,34},{3,99},{4,36},{5,101},{6,38},{7,103},{8,40},{... | collective-permute-start | bytes 2359304 | tf_op jit(solution)/shard_map/ppermute | solution.py:68
  44.1 13.4 %collective-permute-start.4 = (bf16[256,1536]{1,0:T(8,128)(2,1)}, bf16[256,1536]{1,0:T(8,128)(2,1)S(1)}, u32[]{:S(2)}, u32[]{:S(2)}) collective-permute-start(bf16[256,1536]{1,0:T(8,128)(2,1)} %collective-permute-done.3), channel_id=1, source_target_pairs={{0,8},{1,25},{2,10},{3,27},{4,12},{5,29},{6,14},{7,31},{8,16},{9,1... | collective-permute-start | bytes 2359304 | tf_op jit(solution)/shard_map/ppermute | solution.py:68
  46.1 15.3 %collective-permute-start.20 = (bf16[256,1536]{1,0:T(8,128)(2,1)}, bf16[256,1536]{1,0:T(8,128)(2,1)S(1)}, u32[]{:S(2)}, u32[]{:S(2)}) collective-permute-start(bf16[256,1536]{1,0:T(8,128)(2,1)} %collective-permute-done.19), channel_id=1, source_target_pairs={{0,2},{1,7},{2,4},{3,1},{4,6},{5,3},{6,0},{7,5},{8,10},{9,15},{10,... | collective-permute-start | bytes 2359304 | tf_op jit(solution)/shard_map/ppermute | solution.py:68
  48.8 13.4 %collective-permute-start.13 = (bf16[256,1536]{1,0:T(8,128)(2,1)}, bf16[256,1536]{1,0:T(8,128)(2,1)S(1)}, u32[]{:S(2)}, u32[]{:S(2)}) collective-permute-start(bf16[256,1536]{1,0:T(8,128)(2,1)} %collective-permute-done.12), channel_id=1, source_target_pairs={{0,32},{1,97},{2,34},{3,99},{4,36},{5,101},{6,38},{7,103},{8,40},{... | collective-permute-start | bytes 2359304 | tf_op jit(solution)/shard_map/ppermute | solution.py:68
  57.5 13.2 %collective-permute-start.5 = (bf16[256,1536]{1,0:T(8,128)(2,1)S(1)}, bf16[256,1536]{1,0:T(8,128)(2,1)S(1)}, u32[]{:S(2)}, u32[]{:S(2)}) collective-permute-start(bf16[256,1536]{1,0:T(8,128)(2,1)S(1)} %collective-permute-done.4), channel_id=1, source_target_pairs={{0,8},{1,25},{2,10},{3,27},{4,12},{5,29},{6,14},{7,31},{8,16},{9,1... | collective-permute-start | bytes 2359304 | tf_op jit(solution)/shard_map/ppermute | solution.py:68
  61.4 15.5 %collective-permute-start.21 = (bf16[256,1536]{1,0:T(8,128)(2,1)S(1)}, bf16[256,1536]{1,0:T(8,128)(2,1)S(1)}, u32[]{:S(2)}, u32[]{:S(2)}) collective-permute-start(bf16[256,1536]{1,0:T(8,128)(2,1)S(1)} %collective-permute-done.20), channel_id=1, source_target_pairs={{0,2},{1,7},{2,4},{3,1},{4,6},{5,3},{6,0},{7,5},{8,10},{9,15},{10,... | collective-permute-start | bytes 2359304 | tf_op jit(solution)/shard_map/ppermute | solution.py:68
  62.3 13.2 %collective-permute-start.14 = (bf16[256,1536]{1,0:T(8,128)(2,1)S(1)}, bf16[256,1536]{1,0:T(8,128)(2,1)S(1)}, u32[]{:S(2)}, u32[]{:S(2)}) collective-permute-start(bf16[256,1536]{1,0:T(8,128)(2,1)S(1)} %collective-permute-done.13), channel_id=1, source_target_pairs={{0,32},{1,97},{2,34},{3,99},{4,36},{5,101},{6,38},{7,103},{8,40},{... | collective-permute-start | bytes 2359304 | tf_op jit(solution)/shard_map/ppermute | solution.py:68
  62.6 55.5 %copy-start.15 = (s32[12]{0:T(128)S(1)}, s32[12]{0:T(128)}, u32[]{:S(2)}) copy-start(s32[12]{0:T(128)} %param.15) | copy-start | bytes 148
  62.7 55.5 %copy-start.16 = (s32[12]{0:T(128)S(1)}, s32[12]{0:T(128)}, u32[]{:S(2)}) copy-start(s32[12]{0:T(128)} %param.16) | copy-start | bytes 148
  62.7 60.3 %copy-start.7 = (f32[3072]{0:T(1024)S(1)}, f32[3072]{0:T(1024)}, u32[]{:S(2)}) copy-start(f32[3072]{0:T(1024)} %param.23) | copy-start | bytes 36868
  62.7 60.3 %copy-start.8 = (f32[3072]{0:T(1024)S(1)}, f32[3072]{0:T(1024)}, u32[]{:S(2)}) copy-start(f32[3072]{0:T(1024)} %param.24) | copy-start | bytes 36868
  70.8 47.3 %copy-start.11 = (bf16[1024,1536]{1,0:T(8,128)(2,1)}, bf16[1024,1536]{1,0:T(8,128)(2,1)S(1)}, u32[]{:S(2)}) copy-start(bf16[1024,1536]{1,0:T(8,128)(2,1)S(1)} %constant_dynamic-update-slice_fusion.12) | copy-start | bytes 9437188
  75.5 40.0 %collective-permute-start.15 = (bf16[1024,1536]{1,0:T(8,128)(2,1)S(1)}, bf16[1024,1536]{1,0:T(8,128)(2,1)}, u32[]{:S(2)}, u32[]{:S(2)}) collective-permute-start(bf16[1024,1536]{1,0:T(8,128)(2,1)S(1)} %constant_dynamic-update-slice_fusion.6), channel_id=1, source_target_pairs={{0,2},{1,7},{2,4},{3,1},{4,6},{5,3},{6,0},{7,5},{8,10},{9,15},{10,... | collective-permute-start | bytes 9437192 | tf_op jit(solution)/shard_map/ppermute | solution.py:68
  76.9 38.6 %collective-permute-start.7 = (bf16[1024,1536]{1,0:T(8,128)(2,1)S(1)}, bf16[1024,1536]{1,0:T(8,128)(2,1)}, u32[]{:S(2)}, u32[]{:S(2)}) collective-permute-start(bf16[1024,1536]{1,0:T(8,128)(2,1)S(1)} %constant_dynamic-update-slice_fusion.12), channel_id=1, source_target_pairs={{0,32},{1,97},{2,34},{3,99},{4,36},{5,101},{6,38},{7,103},{8,40},{... | collective-permute-start | bytes 9437192 | tf_op jit(solution)/shard_map/ppermute | solution.py:68
  77.0 38.5 %copy-start.10 = (bf16[1024,1536]{1,0:T(8,128)(2,1)}, bf16[1024,1536]{1,0:T(8,128)(2,1)S(1)}, u32[]{:S(2)}) copy-start(bf16[1024,1536]{1,0:T(8,128)(2,1)S(1)} %constant_dynamic-update-slice_fusion) | copy-start | bytes 9437188
  77.0 41.1 %collective-permute-start.22 = (bf16[1024,1536]{1,0:T(8,128)(2,1)S(1)}, bf16[1024,1536]{1,0:T(8,128)(2,1)}, u32[]{:S(2)}, u32[]{:S(2)}) collective-permute-start(bf16[1024,1536]{1,0:T(8,128)(2,1)S(1)} %constant_dynamic-update-slice_fusion), channel_id=1, source_target_pairs={{0,8},{1,25},{2,10},{3,27},{4,12},{5,29},{6,14},{7,31},{8,16},{9,1... | collective-permute-start | bytes 9437192 | tf_op jit(solution)/shard_map/ppermute | solution.py:68
  115.5 38.8 %collective-permute-start.8 = (bf16[1024,1536]{1,0:T(8,128)(2,1)}, bf16[1024,1536]{1,0:T(8,128)(2,1)}, u32[]{:S(2)}, u32[]{:S(2)}) collective-permute-start(bf16[1024,1536]{1,0:T(8,128)(2,1)} %collective-permute-done.7), channel_id=1, source_target_pairs={{0,32},{1,97},{2,34},{3,99},{4,36},{5,101},{6,38},{7,103},{8,40},{... | collective-permute-start | bytes 9437192 | tf_op jit(solution)/shard_map/ppermute | solution.py:68
  115.5 38.9 %collective-permute-start.24 = (bf16[1024,1536]{1,0:T(8,128)(2,1)}, bf16[1024,1536]{1,0:T(8,128)(2,1)}, u32[]{:S(2)}, u32[]{:S(2)}) collective-permute-start(bf16[1024,1536]{1,0:T(8,128)(2,1)} %collective-permute-done.15), channel_id=1, source_target_pairs={{0,2},{1,7},{2,4},{3,1},{4,6},{5,3},{6,0},{7,5},{8,10},{9,15},{10,... | collective-permute-start | bytes 9437192 | tf_op jit(solution)/shard_map/ppermute | solution.py:68
  118.1 38.8 %collective-permute-start.25 = (bf16[1024,1536]{1,0:T(8,128)(2,1)}, bf16[1024,1536]{1,0:T(8,128)(2,1)}, u32[]{:S(2)}, u32[]{:S(2)}) collective-permute-start(bf16[1024,1536]{1,0:T(8,128)(2,1)} %collective-permute-done.22), channel_id=1, source_target_pairs={{0,8},{1,25},{2,10},{3,27},{4,12},{5,29},{6,14},{7,31},{8,16},{9,1... | collective-permute-start | bytes 9437192 | tf_op jit(solution)/shard_map/ppermute | solution.py:68
  123.0 1.1 copy-start.2
  126.5 2.6 collective-permute-start.23
  131.4 25.6 %copy-start.12 = (bf16[128,3072]{1,0:T(8,128)(2,1)S(1)}, bf16[128,3072]{1,0:T(8,128)(2,1)}, u32[]{:S(2)}) copy-start(bf16[128,3072]{1,0:T(8,128)(2,1)} %pad_maximum_fusion.1) | copy-start | bytes 2359300
  131.4 25.6 %copy-start.5 = (bf16[3072,64]{0,1:T(8,128)(2,1)S(1)}, bf16[3072,64]{0,1:T(8,128)(2,1)}, u32[]{:S(2)}) copy-start(bf16[3072,64]{0,1:T(8,128)(2,1)} %param.19) | copy-start | bytes 1179652
  154.4 38.8 %collective-permute-start.26 = (bf16[1024,1536]{1,0:T(8,128)(2,1)}, bf16[1024,1536]{1,0:T(8,128)(2,1)}, u32[]{:S(2)}, u32[]{:S(2)}) collective-permute-start(bf16[1024,1536]{1,0:T(8,128)(2,1)} %collective-permute-done.24), channel_id=1, source_target_pairs={{0,2},{1,7},{2,4},{3,1},{4,6},{5,3},{6,0},{7,5},{8,10},{9,15},{10,... | collective-permute-start | bytes 9437192 | tf_op jit(solution)/shard_map/ppermute | solution.py:68
  156.9 38.8 %collective-permute-start.27 = (bf16[1024,1536]{1,0:T(8,128)(2,1)}, bf16[1024,1536]{1,0:T(8,128)(2,1)}, u32[]{:S(2)}, u32[]{:S(2)}) collective-permute-start(bf16[1024,1536]{1,0:T(8,128)(2,1)} %collective-permute-done.25), channel_id=1, source_target_pairs={{0,8},{1,25},{2,10},{3,27},{4,12},{5,29},{6,14},{7,31},{8,16},{9,1... | collective-permute-start | bytes 9437192 | tf_op jit(solution)/shard_map/ppermute | solution.py:68
  156.9 38.8 %collective-permute-start.28 = (bf16[1024,1536]{1,0:T(8,128)(2,1)}, bf16[1024,1536]{1,0:T(8,128)(2,1)}, u32[]{:S(2)}, u32[]{:S(2)}) collective-permute-start(bf16[1024,1536]{1,0:T(8,128)(2,1)} %collective-permute-done.8), channel_id=1, source_target_pairs={{0,32},{1,97},{2,34},{3,99},{4,36},{5,101},{6,38},{7,103},{8,40},{... | collective-permute-start | bytes 9437192 | tf_op jit(solution)/shard_map/ppermute | solution.py:68
  195.7 19.1 %copy-start.1 = (bf16[96,3072]{1,0:T(8,128)(2,1)S(1)}, bf16[96,3072]{1,0:T(8,128)(2,1)}, u32[]{:S(2)}) copy-start(bf16[96,3072]{1,0:T(8,128)(2,1)} %noise.3) | copy-start | bytes 1769476
  195.7 19.1 %copy-start.3 = (bf16[96,3072]{1,0:T(8,128)(2,1)S(1)}, bf16[96,3072]{1,0:T(8,128)(2,1)}, u32[]{:S(2)}) copy-start(bf16[96,3072]{1,0:T(8,128)(2,1)} %given.2) | copy-start | bytes 1769476
  195.7 19.1 %copy-start.6 = (f32[3072]{0:T(1024)S(1)}, f32[3072]{0:T(1024)}, u32[]{:S(2)}) copy-start(f32[3072]{0:T(1024)} %param.25) | copy-start | bytes 36868
  212.7 6.3 %copy-start.9 = (bf16[3072,64]{0,1:T(8,128)(2,1)S(1)}, bf16[3072,64]{0,1:T(8,128)(2,1)}, u32[]{:S(2)}) copy-start(bf16[3072,64]{0,1:T(8,128)(2,1)} %param.21) | copy-start | bytes 1179652
  212.7 2.1 collective-permute-start.29
  216.7 2.3 collective-permute-start.30
  237.7 3.1 %collective-permute-start.31 = (bf16[192,3072]{1,0:T(8,128)(2,1)}, bf16[192,3072]{1,0:T(8,128)(2,1)S(1)}, u32[]{:S(2)}, u32[]{:S(2)}) collective-permute-start(bf16[192,3072]{1,0:T(8,128)(2,1)} %get-tuple-element.66), channel_id=1, source_target_pairs={{0,1},{1,0},{2,3},{3,2},{4,5},{5,4},{6,7},{7,6},{8,9},{9,8},{10,11... | collective-permute-start | bytes 3538952 | tf_op jit(solution)/shard_map/ppermute | solution.py:49
  240.8 1.3 copy-start.4
  242.1 4.5 %copy-start = (f32[192,3072]{1,0:T(8,128)S(1)}, f32[192,3072]{1,0:T(8,128)}, u32[]{:S(2)}) copy-start(f32[192,3072]{1,0:T(8,128)} %get-tuple-element.72.slope_fake) | copy-start | bytes 7077892
  243.8 2.8 collective-permute-start.32
  258.6 1.9 collective-permute-start.33

commit v5 on v4

--- a/solution.py
+++ b/solution.py
@@ -665,10 +665,8 @@
     def two_steps(steps):
         return jnp.stack([steps[first_image], steps[last_image]])
 
-    def both_quarters(mine):
-        theirs = lax.ppermute(mine, "xl", [(0, 1), (1, 0)])
-        quarters = [jnp.where(xl == 0, mine, theirs), jnp.where(xl == 0, theirs, mine)]
-        return jnp.concatenate(quarters, axis=1)
+    def swap_quarters(mine):
+        return lax.ppermute(mine, "xl", [(0, 1), (1, 0)])
 
     blends = (two_steps(score_steps).astype(f32) + 0.5) / 1000.0
     ends = (last_image * IMG_TOK - first_row).astype(jnp.int32).reshape(1)
@@ -686,18 +684,21 @@
         return u_mine, u_other, u_columns, mods, blends, coords, table
 
     down_rows = base_down.T
-    slots, adapt_out, prepared = ring_slots(
+    adapters = jnp.concatenate([gen_adapt_out, fake_adapt_out], axis=0)
+    slots, theirs, prepared = ring_slots(
         [
             base_up[:PIECE],
             down_rows[:PIECE],
             jnp.concatenate([base_up[PIECE:], down_rows[PIECE:]], axis=0),
         ],
-        jnp.concatenate([gen_adapt_out, fake_adapt_out], axis=0),
-        both_quarters,
+        adapters,
+        swap_quarters,
         (gen_input,),
         prepare,
     )
     u_gen, u_gen_other, u_columns, mods, blends, coords, table = prepared
+    quarters = [jnp.where(xl == 0, adapters, theirs), jnp.where(xl == 0, theirs, adapters)]
+    adapt_out = jnp.concatenate(quarters, axis=1)
     gen_out, fake_out = adapt_out[:rank], adapt_out[rank:]
     up_part, down_part, partial, low_gen = load_weights(
         coords, table, u_gen, u_gen_other, gen_adapt_in.T, gen_out, slots

time: 295 us -> 293 us (level)
  local copies, waits for them, and re-layouts: 32.6 us -> 17.6 us
  waiting for transfers between devices: 114 us -> 129 us
  starting transfers between devices: 30.9 us -> 26.9 us
    ppermute x27, waiting for transfers between devices: 102 us -> 119 us  [send(): return lax.ppermute(piece, AXES, chip_ring(RING_AXES[i][phase]))]
    dynamic_update_slice x24, local copies, waits for them, and re-layouts: 17 us -> 1.38 us  [gathered(): lax.dynamic_update_slice(buffer, piece, (step * rows, 0))]
    ppermute x27, starting transfers between devices: 29.9 us -> 25.7 us  [send(): return lax.ppermute(piece, AXES, chip_ring(RING_AXES[i][phase]))]
  transfers between devices with their start and end apart: 34 -> 34, of which waited for: 22 -> 24; matrix products, arithmetic and copies ran while one was open for 12% -> 7% of each run, Pallas kernels for 9% -> 9%
where the time goes in v5:
time: 293 us; the launch traced here: 292 us
  waiting for transfers between devices  129 us (44%)
  Pallas kernels  76.4 us (26%)
  blocking collectives  29.6 us (10%)
  starting transfers between devices  26.9 us (9%)
  local copies, waits for them, and re-layouts  17.6 us (6%)
  other arithmetic  9.53 us (3%)
    ppermute x27, waiting for transfers between devices, send(): return lax.ppermute(piece, AXES, chip_ring(RING_AXES[i][phase]))  119 us
    all_to_all x1, blocking collectives, local(): received = lax.all_to_all(packed, CHIPS, 0, 0, tiled=True)  29.6 us
    ppermute x27, starting transfers between devices, send(): return lax.ppermute(piece, AXES, chip_ring(RING_AXES[i][phase]))  25.7 us
    pallas_call x1, Pallas kernels, load_weights(): pl.pallas_call(load_body, out_shape=(shape, shape, jax.ShapeDtypeStruct((...  22.7 us
    pallas_call x1, Pallas kernels, score_forward(): pl.pallas_call(score_body, out_shape=(jax.ShapeDtypeStruct((group, hidden...  18.7 us
    pallas_call x1, Pallas kernels, gen_forward(): pl.pallas_call(gen_body, out_shape=(shape, shape, jax.ShapeDtypeStruct((g...  17 us
    pallas_call x1, Pallas kernels, backward(): pl.pallas_call(back_body, out_shape=(jax.ShapeDtypeStruct((2, rank, hidde...  11.9 us
    ppermute x6, waiting for transfers between devices, swap_cores(): return lax.ppermute(value, 'core', [(0, 1), (1, 0)])  9.48 us
  transfers between devices with their start and end apart: 34, of which 24 were waited for; matrix products, arithmetic and copies ran while one was open for 7% of the time, Pallas kernels for 9%

profile of v5, /device:TPU:0, one launch (start us, length us, event | category | flops | bytes accessed | tf_op | source)
XLA Modules:
  0.0 292.3 jit_solution(13804429433826285786)
XLA Ops:
  0.6 1.0 slice.85
  1.6 1.7 collective-permute-start.9
  3.4 0.9 slice.110
  4.3 2.0 collective-permute-start.16
  6.3 0.9 slice.109
  7.2 0.9 slice.83
  8.1 1.6 collective-permute-start
  9.9 1.6 collective-permute-start.10
  12.1 1.4 collective-permute-start.17
  13.5 1.6 collective-permute-done
  15.4 1.5 collective-permute-done.10
  17.2 1.7 collective-permute-done.17
  19.2 2.8 collective-permute-done.1
  22.0 6.8 %collective-permute-done.2 = bf16[64,1536]{1,0:T(8,128)(2,1)S(1)} collective-permute-done((bf16[64,1536]{1,0:T(8,128)(2,1)S(1)}, bf16[64,1536]{1,0:T(8,128)(2,1)S(1)}, u32[]{:S(2)}, u32[]{:S(2)}) %collective-permute-start.2) | collective-permute-done | bytes 196640 | tf_op jit(solution)/shard_map/ppermute | solution.py:68
  28.8 1.6 collective-permute-start.3
  30.6 2.0 collective-permute-start.12
  32.6 9.5 %collective-permute-done.3 = bf16[256,1536]{1,0:T(8,128)(2,1)S(1)} collective-permute-done((bf16[256,1536]{1,0:T(8,128)(2,1)S(1)}, bf16[256,1536]{1,0:T(8,128)(2,1)S(1)}, u32[]{:S(2)}, u32[]{:S(2)}) %collective-permute-start.3) | collective-permute-done | bytes 786464 | tf_op jit(solution)/shard_map/ppermute | solution.py:68
  42.5 1.3 collective-permute-done.19
  43.9 1.8 collective-permute-start.13
  46.6 8.7 %collective-permute-done.4 = bf16[256,1536]{1,0:T(8,128)(2,1)S(1)} collective-permute-done((bf16[256,1536]{1,0:T(8,128)(2,1)S(1)}, bf16[256,1536]{1,0:T(8,128)(2,1)S(1)}, u32[]{:S(2)}, u32[]{:S(2)}) %collective-permute-start.4) | collective-permute-done | bytes 786464 | tf_op jit(solution)/shard_map/ppermute | solution.py:68
  55.4 2.1 collective-permute-done.20
  57.5 2.5 collective-permute-start.21
  60.0 1.7 collective-permute-start.14
  61.9 6.6 %collective-permute-done.5 = bf16[256,1536]{1,0:T(8,128)(2,1)S(1)} collective-permute-done((bf16[256,1536]{1,0:T(8,128)(2,1)S(1)}, bf16[256,1536]{1,0:T(8,128)(2,1)S(1)}, u32[]{:S(2)}, u32[]{:S(2)}) %collective-permute-start.5) | collective-permute-done | bytes 786464 | tf_op jit(solution)/shard_map/ppermute | solution.py:68
  68.6 4.6 %collective-permute-done.14 = bf16[256,1536]{1,0:T(8,128)(2,1)S(1)} collective-permute-done((bf16[256,1536]{1,0:T(8,128)(2,1)S(1)}, bf16[256,1536]{1,0:T(8,128)(2,1)S(1)}, u32[]{:S(2)}, u32[]{:S(2)}) %collective-permute-start.14) | collective-permute-done | bytes 786464 | tf_op jit(solution)/shard_map/ppermute | solution.py:68
  73.9 1.6 collective-permute-start.22
  75.5 36.5 %collective-permute-done.7 = bf16[1024,1536]{1,0:T(8,128)(2,1)} collective-permute-done((bf16[1024,1536]{1,0:T(8,128)(2,1)S(1)}, bf16[1024,1536]{1,0:T(8,128)(2,1)}, u32[]{:S(2)}, u32[]{:S(2)}) %collective-permute-start.7) | collective-permute-done | bytes 3145760 | tf_op jit(solution)/shard_map/ppermute | solution.py:68
  112.0 0.9 collective-permute-start.24
  113.0 1.4 collective-permute-start.25
  114.3 0.6 fusion.32
  114.9 1.2 fusion.26.blends
  116.2 2.4 add_convert_fusion.steps
  118.7 1.1 copy-done.3
  119.7 2.6 first_modulation.1
  122.3 0.6 copy-done.8
  123.3 2.2 copy.35
  125.5 2.3 copy.36
  127.8 3.2 %maximum_bitcast_fusion.u_columns = bf16[3072,192]{1,0:T(8,128)(2,1)} fusion(bf16[96,3072]{0,1:T(8,128)(2,1)} %copy.36, bf16[96,3072]{0,1:T(8,128)(2,1)} %copy.35), kind=kLoop, calls=%fused_computation.1 | loop fusion | flops 2359296 | bytes 2359296 | tf_op jit(solution)/shard_map/transpose | solution.py:683
  131.0 19.8 %collective-permute-done.8 = bf16[1024,1536]{1,0:T(8,128)(2,1)} collective-permute-done((bf16[1024,1536]{1,0:T(8,128)(2,1)}, bf16[1024,1536]{1,0:T(8,128)(2,1)}, u32[]{:S(2)}, u32[]{:S(2)}) %collective-permute-start.8) | collective-permute-done | bytes 3145760 | tf_op jit(solution)/shard_map/ppermute | solution.py:68
  150.9 0.8 collective-permute-start.26
  151.8 1.1 collective-permute-start.27
  153.0 1.2 broadcast_select_fusion
  154.2 22.7 %load_weights.1 = (bf16[3072,3072]{1,0:T(8,128)(2,1)}, bf16[3072,3072]{1,0:T(8,128)(2,1)}, f32[192,3072]{1,0:T(8,128)S(1)}, bf16[192,64]{1,0:T(8,128)(2,1)S(1)}) custom-call(s32[4]{0:T(128)S(1)} %pad_add_fusion.1.place_ref, s32[3,48]{1,0:T(4,128)S(1)} %pad_add_fusion.table, bf16[96,3072]{1,0:T(8,128)(2,1)} %get-tuple-element.51.u_mine, ...), custom_call_target="tpu_custom_call" | custom-call | flops 3623878656 | bytes 150994944 | tf_op jit(solution)/shard_map/load_weights/pallas_call | solution.py:227
  177.0 12.7 %collective-permute-done.26 = bf16[1024,1536]{1,0:T(8,128)(2,1)} collective-permute-done((bf16[1024,1536]{1,0:T(8,128)(2,1)}, bf16[1024,1536]{1,0:T(8,128)(2,1)}, u32[]{:S(2)}, u32[]{:S(2)}) %collective-permute-start.26) | collective-permute-done | bytes 3145760 | tf_op jit(solution)/shard_map/ppermute | solution.py:68
  189.7 1.0 collective-permute-done.27
  190.6 1.1 collective-permute-done.28
  191.8 17.0 %gen_forward.1 = (bf16[3072,3072]{1,0:T(8,128)(2,1)}, bf16[3072,3072]{1,0:T(8,128)(2,1)}, f32[192,3072]{1,0:T(8,128)S(1)}, f32[96,3072]{1,0:T(8,128)S(1)}, bf16[96,3072]{1,0:T(8,128)(2,1)S(1)}) custom-call(s32[3,48]{1,0:T(4,128)S(1)} %pad_add_fusion.table, bf16[3072,192]{1,0:T(8,128)(2,1)S(1)} %copy-done, ...), custom_call_target="tpu_custom_call", output_to_operand_aliasing={{0}: (6, {}), {1}: (7, {})} | custom-call | flops 5435817984 | bytes 41943040 | tf_op jit(solution)/shard_map/gen_forward/pallas_call | solution.py:356
  208.9 2.0 collective-permute-done.29.other
  210.9 1.9 add_noise.1
  213.2 1.9 collective-permute-done.30.u_other
  215.1 18.7 %score_forward.1 = (f32[192,3072]{1,0:T(8,128)}, bf16[192,64]{1,0:T(8,128)(2,1)S(1)}, f32[96,3072]{1,0:T(8,128)S(1)}, f32[96,3072]{1,0:T(8,128)}, bf16[192,3072]{1,0:T(8,128)(2,1)}) custom-call(bf16[96,3072]{1,0:T(8,128)(2,1)S(1)} %get-tuple-element.61.u_mine, bf16[96,3072]{1,0:T(8,128)(2,1)S(1)} %collective-permute-done.30.u_other, ...), custom_call_target="tpu_custom_call" | custom-call | flops 10871635968 | bytes 52428800 | tf_op jit(solution)/shard_map/score_forward/pallas_call | solution.py:429
  234.0 2.9 collective-permute-done.31.others
  236.9 1.3 copy-done.5
  238.1 1.7 cotangents.1
  240.0 2.7 collective-permute-done.32.cots_other
  242.7 11.9 %backward.1 = (bf16[2,64,3072]{2,1,0:T(8,128)(2,1)S(1)}, f32[2,192,64]{2,1,0:T(8,128)S(1)}) custom-call(bf16[192,3072]{1,0:T(8,128)(2,1)S(1)} %get-tuple-element.70.cots_mine, bf16[192,3072]{1,0:T(8,128)(2,1)S(1)} %collective-permute-done.32.cots_other, f32[192,3072]{1,0:T(8,128)S(1)} %get-tuple-element.71.slope_gen, f32[192,3072]{1,0:T(8,128)S(1)} %copy-done.1, ...), custom_call_target="tpu_custom_call" | custom-call | flops 7247757312 | bytes 31457280 | tf_op jit(solution)/shard_map/backward/pallas_call | solution.py:490
  254.9 0.6 reshape.198
  255.5 0.6 copy.41
  256.8 1.8 fusion
  259.2 0.6 fusion.4
  260.6 29.6 %all_to_all.5 = bf16[64,72,128]{2,1,0:T(8,128)(2,1)S(1)} all-to-all(bf16[64,72,128]{2,1,0:T(8,128)(2,1)S(1)} %pad_maximum_fusion), channel_id=1, replica_groups=mesh['z'=4,'y'=4,'xh'=2,'xl'=2,'core'=2] {'z','y','xh','xl'}, dimensions={0} | all-to-all | bytes 2359296 | tf_op jit(solution)/shard_map/all_to_all | solution.py:745
  290.4 0.7 fusion.31
  291.1 0.6 squeeze.19
  291.7 0.6 squeeze.18
  (124 shorter events, 8.3 us)
Async XLA Ops:
  0.6 9.2 %copy-start.17 = (bf16[64,1536]{1,0:T(8,128)(2,1)S(1)}, bf16[64,1536]{1,0:T(8,128)(2,1)}, u32[]{:S(2)}) copy-start(bf16[64,1536]{1,0:T(8,128)(2,1)} %param.20) | copy-start | bytes 589828
  1.6 8.3 %copy-start.18 = (bf16[64,1536]{1,0:T(8,128)(2,1)S(1)}, bf16[64,1536]{1,0:T(8,128)(2,1)}, u32[]{:S(2)}) copy-start(bf16[64,1536]{1,0:T(8,128)(2,1)} %param.22) | copy-start | bytes 589828
  1.6 8.3 %collective-permute-start.9 = (bf16[64,1536]{1,0:T(8,128)(2,1)S(1)}, bf16[64,1536]{1,0:T(8,128)(2,1)S(1)}, u32[]{:S(2)}, u32[]{:S(2)}) collective-permute-start(bf16[64,1536]{1,0:T(8,128)(2,1)S(1)} %slice.85), channel_id=1, source_target_pairs={{0,8},{1,25},{2,10},{3,27},{4,12},{5,29},{6,14},{7,31},{8,16},{9,1... | collective-permute-start | bytes 589832 | tf_op jit(solution)/shard_map/ppermute | solution.py:68
  4.3 7.8 %collective-permute-start.16 = (bf16[64,1536]{1,0:T(8,128)(2,1)S(1)}, bf16[64,1536]{1,0:T(8,128)(2,1)S(1)}, u32[]{:S(2)}, u32[]{:S(2)}) collective-permute-start(bf16[64,1536]{1,0:T(8,128)(2,1)S(1)} %slice.110), channel_id=1, source_target_pairs={{0,32},{1,97},{2,34},{3,99},{4,36},{5,101},{6,38},{7,103},{8,40},{... | collective-permute-start | bytes 589832 | tf_op jit(solution)/shard_map/ppermute | solution.py:68
  8.1 6.9 %collective-permute-start = (bf16[64,1536]{1,0:T(8,128)(2,1)S(1)}, bf16[64,1536]{1,0:T(8,128)(2,1)S(1)}, u32[]{:S(2)}, u32[]{:S(2)}) collective-permute-start(bf16[64,1536]{1,0:T(8,128)(2,1)S(1)} %pad_maximum_fusion.2), channel_id=1, source_target_pairs={{0,2},{1,7},{2,4},{3,1},{4,6},{5,3},{6,0},{7,5},{8,10},{9,15},{10,... | collective-permute-start | bytes 589832 | tf_op jit(solution)/shard_map/ppermute | solution.py:68
  9.9 36.4 %copy-start.15 = (bf16[128,1536]{1,0:T(8,128)(2,1)}, bf16[128,1536]{1,0:T(8,128)(2,1)S(1)}, u32[]{:S(2)}) copy-start(bf16[128,1536]{1,0:T(8,128)(2,1)S(1)} %constant_dynamic-update-slice_fusion) | copy-start | bytes 1179652
  9.9 6.9 %collective-permute-start.10 = (bf16[64,1536]{1,0:T(8,128)(2,1)S(1)}, bf16[64,1536]{1,0:T(8,128)(2,1)S(1)}, u32[]{:S(2)}, u32[]{:S(2)}) collective-permute-start(bf16[64,1536]{1,0:T(8,128)(2,1)S(1)} %collective-permute-done.9), channel_id=1, source_target_pairs={{0,8},{1,25},{2,10},{3,27},{4,12},{5,29},{6,14},{7,31},{8,16},{9,1... | collective-permute-start | bytes 589832 | tf_op jit(solution)/shard_map/ppermute | solution.py:68
  12.1 6.9 %collective-permute-start.17 = (bf16[64,1536]{1,0:T(8,128)(2,1)S(1)}, bf16[64,1536]{1,0:T(8,128)(2,1)S(1)}, u32[]{:S(2)}, u32[]{:S(2)}) collective-permute-start(bf16[64,1536]{1,0:T(8,128)(2,1)S(1)} %collective-permute-done.16), channel_id=1, source_target_pairs={{0,32},{1,97},{2,34},{3,99},{4,36},{5,101},{6,38},{7,103},{8,40},{... | collective-permute-start | bytes 589832 | tf_op jit(solution)/shard_map/ppermute | solution.py:68
  15.1 6.9 %collective-permute-start.1 = (bf16[64,1536]{1,0:T(8,128)(2,1)S(1)}, bf16[64,1536]{1,0:T(8,128)(2,1)S(1)}, u32[]{:S(2)}, u32[]{:S(2)}) collective-permute-start(bf16[64,1536]{1,0:T(8,128)(2,1)S(1)} %collective-permute-done), channel_id=1, source_target_pairs={{0,2},{1,7},{2,4},{3,1},{4,6},{5,3},{6,0},{7,5},{8,10},{9,15},{10,... | collective-permute-start | bytes 589832 | tf_op jit(solution)/shard_map/ppermute | solution.py:68
  16.9 13.7 %collective-permute-start.11 = (bf16[64,1536]{1,0:T(8,128)(2,1)S(1)}, bf16[64,1536]{1,0:T(8,128)(2,1)S(1)}, u32[]{:S(2)}, u32[]{:S(2)}) collective-permute-start(bf16[64,1536]{1,0:T(8,128)(2,1)S(1)} %collective-permute-done.10), channel_id=1, source_target_pairs={{0,8},{1,25},{2,10},{3,27},{4,12},{5,29},{6,14},{7,31},{8,16},{9,1... | collective-permute-start | bytes 589832 | tf_op jit(solution)/shard_map/ppermute | solution.py:68
  18.9 11.5 %collective-permute-start.18 = (bf16[64,1536]{1,0:T(8,128)(2,1)S(1)}, bf16[64,1536]{1,0:T(8,128)(2,1)S(1)}, u32[]{:S(2)}, u32[]{:S(2)}) collective-permute-start(bf16[64,1536]{1,0:T(8,128)(2,1)S(1)} %collective-permute-done.17), channel_id=1, source_target_pairs={{0,32},{1,97},{2,34},{3,99},{4,36},{5,101},{6,38},{7,103},{8,40},{... | collective-permute-start | bytes 589832 | tf_op jit(solution)/shard_map/ppermute | solution.py:68
  21.9 6.9 %collective-permute-start.2 = (bf16[64,1536]{1,0:T(8,128)(2,1)S(1)}, bf16[64,1536]{1,0:T(8,128)(2,1)S(1)}, u32[]{:S(2)}, u32[]{:S(2)}) collective-permute-start(bf16[64,1536]{1,0:T(8,128)(2,1)S(1)} %collective-permute-done.1), channel_id=1, source_target_pairs={{0,2},{1,7},{2,4},{3,1},{4,6},{5,3},{6,0},{7,5},{8,10},{9,15},{10,... | collective-permute-start | bytes 589832 | tf_op jit(solution)/shard_map/ppermute | solution.py:68
  28.8 13.3 %collective-permute-start.3 = (bf16[256,1536]{1,0:T(8,128)(2,1)S(1)}, bf16[256,1536]{1,0:T(8,128)(2,1)S(1)}, u32[]{:S(2)}, u32[]{:S(2)}) collective-permute-start(bf16[256,1536]{1,0:T(8,128)(2,1)S(1)} %constant_dynamic-update-slice_fusion.17), channel_id=1, source_target_pairs={{0,8},{1,25},{2,10},{3,27},{4,12},{5,29},{6,14},{7,31},{8,16},{9,1... | collective-permute-start | bytes 2359304 | tf_op jit(solution)/shard_map/ppermute | solution.py:68
  30.5 13.3 %collective-permute-start.19 = (bf16[256,1536]{1,0:T(8,128)(2,1)S(1)}, bf16[256,1536]{1,0:T(8,128)(2,1)S(1)}, u32[]{:S(2)}, u32[]{:S(2)}) collective-permute-start(bf16[256,1536]{1,0:T(8,128)(2,1)S(1)} %constant_dynamic-update-slice_fusion.5), channel_id=1, source_target_pairs={{0,2},{1,7},{2,4},{3,1},{4,6},{5,3},{6,0},{7,5},{8,10},{9,15},{10,... | collective-permute-start | bytes 2359304 | tf_op jit(solution)/shard_map/ppermute | solution.py:68
  30.6 13.3 %collective-permute-start.12 = (bf16[256,1536]{1,0:T(8,128)(2,1)S(1)}, bf16[256,1536]{1,0:T(8,128)(2,1)S(1)}, u32[]{:S(2)}, u32[]{:S(2)}) collective-permute-start(bf16[256,1536]{1,0:T(8,128)(2,1)S(1)} %constant_dynamic-update-slice_fusion.11), channel_id=1, source_target_pairs={{0,32},{1,97},{2,34},{3,99},{4,36},{5,101},{6,38},{7,103},{8,40},{... | collective-permute-start | bytes 2359304 | tf_op jit(solution)/shard_map/ppermute | solution.py:68
  42.1 13.2 %collective-permute-start.4 = (bf16[256,1536]{1,0:T(8,128)(2,1)S(1)}, bf16[256,1536]{1,0:T(8,128)(2,1)S(1)}, u32[]{:S(2)}, u32[]{:S(2)}) collective-permute-start(bf16[256,1536]{1,0:T(8,128)(2,1)S(1)} %collective-permute-done.3), channel_id=1, source_target_pairs={{0,8},{1,25},{2,10},{3,27},{4,12},{5,29},{6,14},{7,31},{8,16},{9,1... | collective-permute-start | bytes 2359304 | tf_op jit(solution)/shard_map/ppermute | solution.py:68
  43.8 13.7 %collective-permute-start.20 = (bf16[256,1536]{1,0:T(8,128)(2,1)S(1)}, bf16[256,1536]{1,0:T(8,128)(2,1)S(1)}, u32[]{:S(2)}, u32[]{:S(2)}) collective-permute-start(bf16[256,1536]{1,0:T(8,128)(2,1)S(1)} %collective-permute-done.19), channel_id=1, source_target_pairs={{0,2},{1,7},{2,4},{3,1},{4,6},{5,3},{6,0},{7,5},{8,10},{9,15},{10,... | collective-permute-start | bytes 2359304 | tf_op jit(solution)/shard_map/ppermute | solution.py:68
  43.9 16.1 %collective-permute-start.13 = (bf16[256,1536]{1,0:T(8,128)(2,1)S(1)}, bf16[256,1536]{1,0:T(8,128)(2,1)S(1)}, u32[]{:S(2)}, u32[]{:S(2)}) collective-permute-start(bf16[256,1536]{1,0:T(8,128)(2,1)S(1)} %collective-permute-done.12), channel_id=1, source_target_pairs={{0,32},{1,97},{2,34},{3,99},{4,36},{5,101},{6,38},{7,103},{8,40},{... | collective-permute-start | bytes 2359304 | tf_op jit(solution)/shard_map/ppermute | solution.py:68
  46.3 22.2 %collective-permute-start.6 = (bf16[128,1536]{1,0:T(8,128)(2,1)S(1)}, bf16[128,1536]{1,0:T(8,128)(2,1)S(1)}, u32[]{:S(2)}, u32[]{:S(2)}) collective-permute-start(bf16[128,1536]{1,0:T(8,128)(2,1)S(1)} %constant_dynamic-update-slice_fusion), channel_id=1, source_target_pairs={{0,2},{2,0},{1,3},{3,1},{4,6},{6,4},{5,7},{7,5},{8,10},{10,8},{9,1... | collective-permute-start | bytes 1179656 | tf_op jit(solution)/shard_map/ppermute | solution.py:669
  55.3 13.2 %collective-permute-start.5 = (bf16[256,1536]{1,0:T(8,128)(2,1)S(1)}, bf16[256,1536]{1,0:T(8,128)(2,1)S(1)}, u32[]{:S(2)}, u32[]{:S(2)}) collective-permute-start(bf16[256,1536]{1,0:T(8,128)(2,1)S(1)} %collective-permute-done.4), channel_id=1, source_target_pairs={{0,8},{1,25},{2,10},{3,27},{4,12},{5,29},{6,14},{7,31},{8,16},{9,1... | collective-permute-start | bytes 2359304 | tf_op jit(solution)/shard_map/ppermute | solution.py:68
  57.5 16.4 %collective-permute-start.21 = (bf16[256,1536]{1,0:T(8,128)(2,1)S(1)}, bf16[256,1536]{1,0:T(8,128)(2,1)S(1)}, u32[]{:S(2)}, u32[]{:S(2)}) collective-permute-start(bf16[256,1536]{1,0:T(8,128)(2,1)S(1)} %collective-permute-done.20), channel_id=1, source_target_pairs={{0,2},{1,7},{2,4},{3,1},{4,6},{5,3},{6,0},{7,5},{8,10},{9,15},{10,... | collective-permute-start | bytes 2359304 | tf_op jit(solution)/shard_map/ppermute | solution.py:68
  60.0 13.2 %collective-permute-start.14 = (bf16[256,1536]{1,0:T(8,128)(2,1)S(1)}, bf16[256,1536]{1,0:T(8,128)(2,1)S(1)}, u32[]{:S(2)}, u32[]{:S(2)}) collective-permute-start(bf16[256,1536]{1,0:T(8,128)(2,1)S(1)} %collective-permute-done.13), channel_id=1, source_target_pairs={{0,32},{1,97},{2,34},{3,99},{4,36},{5,101},{6,38},{7,103},{8,40},{... | collective-permute-start | bytes 2359304 | tf_op jit(solution)/shard_map/ppermute | solution.py:68
  61.8 52.5 %copy-start.19 = (s32[12]{0:T(128)S(1)}, s32[12]{0:T(128)}, u32[]{:S(2)}) copy-start(s32[12]{0:T(128)} %param.15) | copy-start | bytes 148
  61.9 52.5 %copy-start.20 = (s32[12]{0:T(128)S(1)}, s32[12]{0:T(128)}, u32[]{:S(2)}) copy-start(s32[12]{0:T(128)} %param.16) | copy-start | bytes 148
  61.9 56.8 %copy-start.10 = (f32[3072]{0:T(1024)S(1)}, f32[3072]{0:T(1024)}, u32[]{:S(2)}) copy-start(f32[3072]{0:T(1024)} %param.23) | copy-start | bytes 36868
  61.9 56.8 %copy-start.11 = (f32[3072]{0:T(1024)S(1)}, f32[3072]{0:T(1024)}, u32[]{:S(2)}) copy-start(f32[3072]{0:T(1024)} %param.24) | copy-start | bytes 36868
  68.6 43.4 %copy-start.13 = (bf16[1024,1536]{1,0:T(8,128)(2,1)}, bf16[1024,1536]{1,0:T(8,128)(2,1)S(1)}, u32[]{:S(2)}) copy-start(bf16[1024,1536]{1,0:T(8,128)(2,1)S(1)} %constant_dynamic-update-slice_fusion.14) | copy-start | bytes 9437188
  68.6 44.4 %copy-start.16 = (bf16[128,1536]{1,0:T(8,128)(2,1)}, bf16[128,1536]{1,0:T(8,128)(2,1)S(1)}, u32[]{:S(2)}) copy-start(bf16[128,1536]{1,0:T(8,128)(2,1)S(1)} %collective-permute-done.6) | copy-start | bytes 1179652
  73.2 38.7 %collective-permute-start.15 = (bf16[1024,1536]{1,0:T(8,128)(2,1)S(1)}, bf16[1024,1536]{1,0:T(8,128)(2,1)}, u32[]{:S(2)}, u32[]{:S(2)}) collective-permute-start(bf16[1024,1536]{1,0:T(8,128)(2,1)S(1)} %constant_dynamic-update-slice_fusion.8), channel_id=1, source_target_pairs={{0,2},{1,7},{2,4},{3,1},{4,6},{5,3},{6,0},{7,5},{8,10},{9,15},{10,... | collective-permute-start | bytes 9437192 | tf_op jit(solution)/shard_map/ppermute | solution.py:68
  73.3 38.7 %collective-permute-start.7 = (bf16[1024,1536]{1,0:T(8,128)(2,1)S(1)}, bf16[1024,1536]{1,0:T(8,128)(2,1)}, u32[]{:S(2)}, u32[]{:S(2)}) collective-permute-start(bf16[1024,1536]{1,0:T(8,128)(2,1)S(1)} %constant_dynamic-update-slice_fusion.14), channel_id=1, source_target_pairs={{0,32},{1,97},{2,34},{3,99},{4,36},{5,101},{6,38},{7,103},{8,40},{... | collective-permute-start | bytes 9437192 | tf_op jit(solution)/shard_map/ppermute | solution.py:68
  73.9 39.0 %copy-start.14 = (bf16[1024,1536]{1,0:T(8,128)(2,1)}, bf16[1024,1536]{1,0:T(8,128)(2,1)S(1)}, u32[]{:S(2)}) copy-start(bf16[1024,1536]{1,0:T(8,128)(2,1)S(1)} %constant_dynamic-update-slice_fusion.2) | copy-start | bytes 9437188
  73.9 39.0 %collective-permute-start.22 = (bf16[1024,1536]{1,0:T(8,128)(2,1)S(1)}, bf16[1024,1536]{1,0:T(8,128)(2,1)}, u32[]{:S(2)}, u32[]{:S(2)}) collective-permute-start(bf16[1024,1536]{1,0:T(8,128)(2,1)S(1)} %constant_dynamic-update-slice_fusion.2), channel_id=1, source_target_pairs={{0,8},{1,25},{2,10},{3,27},{4,12},{5,29},{6,14},{7,31},{8,16},{9,1... | collective-permute-start | bytes 9437192 | tf_op jit(solution)/shard_map/ppermute | solution.py:68
  112.0 38.8 %collective-permute-start.8 = (bf16[1024,1536]{1,0:T(8,128)(2,1)}, bf16[1024,1536]{1,0:T(8,128)(2,1)}, u32[]{:S(2)}, u32[]{:S(2)}) collective-permute-start(bf16[1024,1536]{1,0:T(8,128)(2,1)} %collective-permute-done.7), channel_id=1, source_target_pairs={{0,32},{1,97},{2,34},{3,99},{4,36},{5,101},{6,38},{7,103},{8,40},{... | collective-permute-start | bytes 9437192 | tf_op jit(solution)/shard_map/ppermute | solution.py:68
  112.0 38.9 %collective-permute-start.24 = (bf16[1024,1536]{1,0:T(8,128)(2,1)}, bf16[1024,1536]{1,0:T(8,128)(2,1)}, u32[]{:S(2)}, u32[]{:S(2)}) collective-permute-start(bf16[1024,1536]{1,0:T(8,128)(2,1)} %collective-permute-done.15), channel_id=1, source_target_pairs={{0,2},{1,7},{2,4},{3,1},{4,6},{5,3},{6,0},{7,5},{8,10},{9,15},{10,... | collective-permute-start | bytes 9437192 | tf_op jit(solution)/shard_map/ppermute | solution.py:68
  113.0 38.9 %collective-permute-start.25 = (bf16[1024,1536]{1,0:T(8,128)(2,1)}, bf16[1024,1536]{1,0:T(8,128)(2,1)}, u32[]{:S(2)}, u32[]{:S(2)}) collective-permute-start(bf16[1024,1536]{1,0:T(8,128)(2,1)} %collective-permute-done.22), channel_id=1, source_target_pairs={{0,8},{1,25},{2,10},{3,27},{4,12},{5,29},{6,14},{7,31},{8,16},{9,1... | collective-permute-start | bytes 9437192 | tf_op jit(solution)/shard_map/ppermute | solution.py:68
  118.7 1.1 copy-start.3
  122.3 0.6 copy-start.8
  122.9 2.6 collective-permute-start.23
  131.0 23.2 %copy-start.6 = (bf16[3072,64]{0,1:T(8,128)(2,1)S(1)}, bf16[3072,64]{0,1:T(8,128)(2,1)}, u32[]{:S(2)}) copy-start(bf16[3072,64]{0,1:T(8,128)(2,1)} %param.19) | copy-start | bytes 1179652
  150.9 38.8 %collective-permute-start.26 = (bf16[1024,1536]{1,0:T(8,128)(2,1)}, bf16[1024,1536]{1,0:T(8,128)(2,1)}, u32[]{:S(2)}, u32[]{:S(2)}) collective-permute-start(bf16[1024,1536]{1,0:T(8,128)(2,1)} %collective-permute-done.24), channel_id=1, source_target_pairs={{0,2},{1,7},{2,4},{3,1},{4,6},{5,3},{6,0},{7,5},{8,10},{9,15},{10,... | collective-permute-start | bytes 9437192 | tf_op jit(solution)/shard_map/ppermute | solution.py:68
  151.8 38.8 %collective-permute-start.27 = (bf16[1024,1536]{1,0:T(8,128)(2,1)}, bf16[1024,1536]{1,0:T(8,128)(2,1)}, u32[]{:S(2)}, u32[]{:S(2)}) collective-permute-start(bf16[1024,1536]{1,0:T(8,128)(2,1)} %collective-permute-done.25), channel_id=1, source_target_pairs={{0,8},{1,25},{2,10},{3,27},{4,12},{5,29},{6,14},{7,31},{8,16},{9,1... | collective-permute-start | bytes 9437192 | tf_op jit(solution)/shard_map/ppermute | solution.py:68
  152.9 38.8 %collective-permute-start.28 = (bf16[1024,1536]{1,0:T(8,128)(2,1)}, bf16[1024,1536]{1,0:T(8,128)(2,1)}, u32[]{:S(2)}, u32[]{:S(2)}) collective-permute-start(bf16[1024,1536]{1,0:T(8,128)(2,1)} %collective-permute-done.8), channel_id=1, source_target_pairs={{0,32},{1,97},{2,34},{3,99},{4,36},{5,101},{6,38},{7,103},{8,40},{... | collective-permute-start | bytes 9437192 | tf_op jit(solution)/shard_map/ppermute | solution.py:68
  154.2 37.5 %copy-start = (bf16[3072,192]{1,0:T(8,128)(2,1)S(1)}, bf16[3072,192]{1,0:T(8,128)(2,1)}, u32[]{:S(2)}) copy-start(bf16[3072,192]{1,0:T(8,128)(2,1)} %maximum_bitcast_fusion.u_columns) | copy-start | bytes 3538948
  191.7 19.1 %copy-start.2 = (bf16[96,3072]{1,0:T(8,128)(2,1)S(1)}, bf16[96,3072]{1,0:T(8,128)(2,1)}, u32[]{:S(2)}) copy-start(bf16[96,3072]{1,0:T(8,128)(2,1)} %noise.3) | copy-start | bytes 1769476
  191.8 19.1 %copy-start.4 = (bf16[96,3072]{1,0:T(8,128)(2,1)S(1)}, bf16[96,3072]{1,0:T(8,128)(2,1)}, u32[]{:S(2)}) copy-start(bf16[96,3072]{1,0:T(8,128)(2,1)} %given.2) | copy-start | bytes 1769476
  191.8 19.1 %copy-start.7 = (f32[3072]{0:T(1024)S(1)}, f32[3072]{0:T(1024)}, u32[]{:S(2)}) copy-start(f32[3072]{0:T(1024)} %param.25) | copy-start | bytes 36868
  191.8 19.1 %copy-start.9 = (f32[4,3072]{1,0:T(4,128)S(1)}, f32[4,3072]{1,0:T(4,128)}, u32[]{:S(2)}) copy-start(f32[4,3072]{1,0:T(4,128)} %copy-done.8) | copy-start | bytes 147460
  208.8 6.3 %copy-start.12 = (bf16[3072,64]{0,1:T(8,128)(2,1)S(1)}, bf16[3072,64]{0,1:T(8,128)(2,1)}, u32[]{:S(2)}) copy-start(bf16[3072,64]{0,1:T(8,128)(2,1)} %param.21) | copy-start | bytes 1179652
  208.8 2.1 collective-permute-start.29
  212.7 2.3 collective-permute-start.30
  233.7 3.1 %collective-permute-start.31 = (bf16[192,3072]{1,0:T(8,128)(2,1)}, bf16[192,3072]{1,0:T(8,128)(2,1)S(1)}, u32[]{:S(2)}, u32[]{:S(2)}) collective-permute-start(bf16[192,3072]{1,0:T(8,128)(2,1)} %get-tuple-element.66), channel_id=1, source_target_pairs={{0,1},{1,0},{2,3},{3,2},{4,5},{5,4},{6,7},{7,6},{8,9},{9,8},{10,11... | collective-permute-start | bytes 3538952 | tf_op jit(solution)/shard_map/ppermute | solution.py:49
  236.9 1.3 copy-start.5
  238.1 4.5 %copy-start.1 = (f32[192,3072]{1,0:T(8,128)S(1)}, f32[192,3072]{1,0:T(8,128)}, u32[]{:S(2)}) copy-start(f32[192,3072]{1,0:T(8,128)} %get-tuple-element.72.slope_fake) | copy-start | bytes 7077892
  239.8 2.8 collective-permute-start.32
  254.7 1.9 collective-permute-start.33
